TPU v7x, 256 devices: a whole 4x4x8 slice. The times are simulated.
256 devices in a mesh: pb: 16 (over y, z_hi), ha: 8 (over x, z_lo), af: 2 (over core).
Axes of the slice: x: 4, y: 4, z: 8 (z_hi: 4, z_lo: 2; z = z_hi * 2 + z_lo), core: 2. Of those that a mesh axis runs over, the one named last changes fastest.
Arguments:
- queries: bfloat16 [2048, 8192], P('pb', ('ha', 'af')), may hold values from -16 to 16
- vis_keys: bfloat16 [8192, 1024], P(None, 'ha'), may hold values from -16 to 16
- vis_values: bfloat16 [8192, 1024], P(None, 'ha'), may hold values from -6 to 6
- out_grad: bfloat16 [2048, 8192], P('pb', ('ha', 'af')), may hold values from -96 to 96
- key_weight: bfloat16 [8192, 1024], P(None, 'ha'), may hold values from -0.0625 to 0.0625
- value_weight: bfloat16 [8192, 1024], P(None, 'ha'), may hold values from -0.0625 to 0.0625
- frame_ids: int32 [8192], replicated, may hold values from 0 to 7, as said below
- text_mask: int32 [64, 8], P('pb'), may hold values from 0 to 1
Outputs:
- query_grad: bfloat16 [2048, 8192], P('pb', ('ha', 'af'))
- visual_grad: bfloat16 [8192, 8192], P(('pb', 'af'), 'ha')
Inputs may be any that keep to these rules, and one draw needn't show every extreme that they name: `frame_ids`: never falls along the visual tokens; every frame holds one token or more, frame 0 two or more.
All inputs are finite; a program needn't handle non-finite values.
Results may differ from a plain program's by a relative error of at most 0.02.
Values may be sent and summed in bfloat16 or wider, within the bound.
No kernel may reach another device: no remote copies, remote signals or barrier semaphores. Data moves between devices by JAX's collectives and lax.ppermute only.
A program may use at most 128 MiB of HBM per device.

v0:
```python
import jax
import jax.numpy as jnp
from jax import lax
from jax.sharding import PartitionSpec as P

HQ = 64
KVH = 8
DH = 128
FRAMES = 8
QBLK = 32


def attend(query_cube, grad_cube, key_slab, value_slab, allowed, score_scale):
    tok_rows, head_count, head_size = query_cube.shape
    query_rows = query_cube.reshape(tok_rows * head_count, head_size)
    grad_rows = grad_cube.reshape(tok_rows * head_count, head_size)
    contract_last = (((1,), (1,)), ((), ()))
    scores = lax.dot_general(
        query_rows, key_slab, contract_last, preferred_element_type=jnp.float32
    )
    scores = scores.reshape(tok_rows, head_count, -1) * score_scale
    mask_cube = allowed[:, None, :]
    scores = jnp.where(mask_cube, scores, -1e30)
    row_max = jnp.max(scores, axis=2, keepdims=True)
    numer = jnp.where(mask_cube, jnp.exp(scores - row_max), 0.0)
    attn_prob = numer / jnp.sum(numer, axis=2, keepdims=True)
    prob_low = attn_prob.astype(jnp.bfloat16)
    prob_grad = lax.dot_general(
        grad_rows, value_slab, contract_last, preferred_element_type=jnp.float32
    )
    prob_grad = prob_grad.reshape(tok_rows, head_count, -1)
    row_delta = jnp.sum(prob_low.astype(jnp.float32) * prob_grad, axis=2, keepdims=True)
    score_grad = (attn_prob * (prob_grad - row_delta) * score_scale).astype(jnp.bfloat16)
    score_rows = score_grad.reshape(tok_rows * head_count, -1)
    prob_rows = prob_low.reshape(tok_rows * head_count, -1)
    contract_rows = (((0,), (0,)), ((), ()))
    key_part = lax.dot_general(
        score_rows, query_rows, contract_rows, preferred_element_type=jnp.float32
    )
    value_part = lax.dot_general(
        prob_rows, grad_rows, contract_rows, preferred_element_type=jnp.float32
    )
    return (score_rows, key_part, value_part)


def on_device(
    queries, vis_keys, vis_values, out_grad, key_weight, value_weight, frame_ids, text_mask
):
    score_scale = DH ** (-0.5)
    group_size = HQ // KVH
    tok_rows = queries.shape[0]
    local_heads = queries.shape[1] // DH
    per_kv = min(local_heads, group_size)
    onehot = (frame_ids[None, :] == jnp.arange(FRAMES, dtype=jnp.int32)[:, None]).astype(
        jnp.bfloat16
    )
    tok_mask = jnp.repeat(text_mask, QBLK, axis=0).astype(jnp.bfloat16)
    allowed = jnp.dot(tok_mask, onehot, preferred_element_type=jnp.float32) > 0.5
    query_cube = queries.reshape(tok_rows, local_heads, DH)
    grad_cube = out_grad.reshape(tok_rows, local_heads, DH)
    score_list, key_list, value_list = ([], [], [])
    score_rows, key_part, value_part = attend(
        query_cube, grad_cube, vis_keys, vis_values, allowed, score_scale
    )
    score_list.append(score_rows)
    key_list.append(key_part)
    value_list.append(value_part)
    key_part = key_list[0]
    value_part = value_list[0]
    key_sum, value_sum = (
        lax.psum_scatter(key_part, ("pb", "af"), scatter_dimension=0, tiled=True),
        lax.psum_scatter(value_part, ("pb", "af"), scatter_dimension=0, tiled=True),
    )
    query_out = jnp.dot(score_list[0], vis_keys, preferred_element_type=jnp.float32)
    query_list = query_out.reshape(tok_rows, per_kv * DH)
    query_grad = query_list.astype(jnp.bfloat16)
    key_low = key_sum.astype(jnp.bfloat16)
    value_low = value_sum.astype(jnp.bfloat16)
    contract_last = (((1,), (1,)), ((), ()))
    visual_term = lax.dot_general(
        key_low, key_weight, contract_last, preferred_element_type=jnp.float32
    )
    visual_term = visual_term + lax.dot_general(
        value_low, value_weight, contract_last, preferred_element_type=jnp.float32
    )
    visual_grad = lax.psum_scatter(visual_term, "ha", scatter_dimension=1, tiled=True).astype(
        jnp.bfloat16
    )
    return (query_grad, visual_grad)


def solution(mesh):
    in_specs = (
        P("pb", ("ha", "af")),
        P(None, "ha"),
        P(None, "ha"),
        P("pb", ("ha", "af")),
        P(None, "ha"),
        P(None, "ha"),
        P(),
        P("pb", None),
    )
    out_specs = (P("pb", ("ha", "af")), P(("pb", "af"), "ha"))
    return jax.shard_map(
        on_device, mesh=mesh, in_specs=in_specs, out_specs=out_specs, check_vma=False
    )
```

profile of v0, /device:TPU:32, one launch (start us, length us, event | category | flops | bytes accessed | tf_op | source)
XLA Modules:
  0.0 509.3 jit_solution(15890894219500314961)
XLA Ops:
  7.2 1.1 reshape_reshape.6
  8.4 0.5 copy-done
  8.8 9.0 %fusion.14 = f32[128,4,8192]{2,0,1:T(8,128)} fusion(bf16[8192,128]{1,0:T(8,128)(2,1)S(1)} %copy-done, bf16[128,512]{1,0:T(8,128)(2,1)} %param.8), kind=kOutput, calls=%fused_computation.19 | convolution fusion | flops 1073741824 | bytes 19005440 | tf_op jit(solution)/shard_map/dot_general | solution.py:18
  17.8 2.0 fusion.7
  19.8 3.0 copy.13
  22.8 25.3 %fusion.28 = (f32[128,4]{0,1:T(4,128)S(1)}, f32[128,4,8192]{2,0,1:T(8,128)}) fusion(f32[128,4,8192]{2,0,1:T(8,128)} %fusion.14, pred[128,8192]{1,0:T(8,128)(4,1)S(1)} %copy.13), kind=kOutput, calls=%fused_computation.34 | output fusion | flops 20979712 | bytes 34605056 | tf_op jit(solution)/shard_map/sub | solution.py:25
  48.1 8.1 %fusion.12 = f32[128,4,8192]{2,0,1:T(8,128)} fusion(bf16[8192,128]{1,0:T(8,128)(2,1)S(1)} %copy-done.1, bf16[128,512]{1,0:T(8,128)(2,1)S(1)} %copy-done.2), kind=kOutput, calls=%fused_computation.17 | convolution fusion | flops 1073741824 | bytes 19005440 | tf_op jit(solution)/shard_map/dot_general | solution.py:28
  56.2 25.0 %multiply_convert_fusion = bf16[128,4,8192]{2,0,1:T(8,128)(2,1)S(1)} fusion(f32[128,4,8192]{2,0,1:T(8,128)} %fusion.12, f32[128,4,8192]{2,0,1:T(8,128)} %get-tuple-element.3, f32[128,4]{0,1:T(4,128)S(1)} %get-tuple-element.2), kind=kOutput, calls=%fused_computation.2 | output fusion | flops 37757440 | bytes 41945088 | tf_op jit(solution)/shard_map/sub | solution.py:33
  81.2 17.7 %copy.16 = bf16[128,4,8192]{2,1,0:T(4,128)(2,1)} copy(bf16[128,4,8192]{2,0,1:T(8,128)(2,1)S(1)} %multiply_convert_fusion) | data formatting | bytes 16777216 | tf_op jit(solution)/shard_map/convert_element_type | solution.py:33
  98.9 12.5 %reshape.25 = bf16[512,8192]{1,0:T(8,128)(2,1)} reshape(bf16[128,4,8192]{2,1,0:T(4,128)(2,1)} %copy.16) | data formatting | bytes 16777216 | tf_op jit(solution)/shard_map/reshape | solution.py:34
  111.4 7.7 %fusion.30 = f32[8192,128]{1,0:T(8,128)} fusion(bf16[512,8192]{1,0:T(8,128)(2,1)} %reshape.25, bf16[512,128]{1,0:T(8,128)(2,1)S(1)} %reshape_reshape.6), kind=kOutput, calls=%fused_computation.35 | convolution fusion | flops 1073741824 | bytes 12713984 | tf_op jit(solution)/shard_map/dot_general | solution.py:37
  119.2 0.1 reshape_reshape.7
  119.3 6.9 %fusion.11 = bf16[128,4,8192]{2,0,1:T(8,128)(2,1)S(1)} fusion(f32[128,4,8192]{2,0,1:T(8,128)} %get-tuple-element.3, f32[128,4]{0,1:T(4,128)S(1)} %get-tuple-element.2), kind=kLoop, calls=%fused_computation.16 | loop fusion | flops 8388608 | bytes 25167872 | tf_op jit(solution)/shard_map/convert_element_type | solution.py:27
  126.2 17.7 %copy.17 = bf16[128,4,8192]{2,1,0:T(4,128)(2,1)} copy(bf16[128,4,8192]{2,0,1:T(8,128)(2,1)S(1)} %fusion.11) | data formatting | bytes 16777216 | tf_op jit(solution)/shard_map/convert_element_type | solution.py:27
  143.9 12.7 %reshape.26 = bf16[512,8192]{1,0:T(8,128)(2,1)} reshape(bf16[128,4,8192]{2,1,0:T(4,128)(2,1)} %copy.17) | data formatting | bytes 16777216 | tf_op jit(solution)/shard_map/reshape | solution.py:35
  156.7 7.9 %fusion.31 = f32[8192,128]{1,0:T(8,128)} fusion(bf16[512,8192]{1,0:T(8,128)(2,1)} %reshape.26, bf16[512,128]{1,0:T(8,128)(2,1)S(1)} %reshape_reshape.7), kind=kOutput, calls=%fused_computation.36 | convolution fusion | flops 1073741824 | bytes 12713984 | tf_op jit(solution)/shard_map/dot_general | solution.py:40
  164.7 55.8 %reduce-scatter.4.cloned.1.call-done = f32[256,128]{1,0:T(8,128)} async-done(((f32[8192,128]{1,0:T(8,128)}), f32[256,128]{1,0:T(8,128)}) %reduce-scatter.4.cloned.1.call-update) | async-done | bytes 131088 | tf_op jit(solution)/shard_map/reduce_scatter | solution.py:71
  220.4 6.1 %fusion.24 = f32[256,8192]{1,0:T(8,128)} fusion(bf16[8192,128]{1,0:T(8,128)(2,1)} %param.12, f32[256,128]{1,0:T(8,128)} %reduce-scatter.4.cloned.1.call-done), kind=kOutput, calls=%fused_computation.30 | convolution fusion | flops 536903680 | bytes 10616832 | tf_op jit(solution)/shard_map/dot_general | solution.py:80
  226.6 95.3 %reduce-scatter.6.cloned.1.call-done = f32[256,128]{1,0:T(8,128)} async-done(((f32[8192,128]{1,0:T(8,128)}), f32[256,128]{1,0:T(8,128)}) %reduce-scatter.6.cloned.1.call-update) | async-done | bytes 131088 | tf_op jit(solution)/shard_map/reduce_scatter | solution.py:72
  321.9 8.5 %convolution_add_fusion = f32[256,8192]{1,0:T(8,128)} fusion(f32[256,8192]{1,0:T(8,128)} %fusion.24, bf16[8192,128]{1,0:T(8,128)(2,1)} %param.13, f32[256,128]{1,0:T(8,128)} %reduce-scatter.6.cloned.1.call-done), kind=kOutput, calls=%fused_computation.9 | convolution fusion | flops 539000832 | bytes 19005440 | tf_op jit(solution)/shard_map/dot_general | solution.py:83
  330.4 5.7 %convolution_convert_fusion = bf16[512,128]{1,0:T(8,128)(2,1)S(1)} fusion(bf16[512,8192]{1,0:T(8,128)(2,1)} %reshape.25, bf16[8192,128]{1,0:T(8,128)(2,1)S(1)} %copy-done), kind=kOutput, calls=%fused_computation.21 | convolution fusion | flops 1073807360 | bytes 10616832 | tf_op jit(solution)/shard_map/dot_general | solution.py:74
  336.1 0.7 convert_element_type.38
  336.9 163.8 %reduce-scatter.8.cloned.1.call-done = f32[256,1024]{1,0:T(8,128)} async-done(((f32[256,8192]{1,0:T(8,128)}), f32[256,1024]{1,0:T(8,128)}) %reduce-scatter.8.cloned.1.call-update) | async-done | bytes 1048592 | tf_op jit(solution)/shard_map/reduce_scatter | solution.py:86
  500.7 2.1 convert_element_type.41
  (17 shorter events, 0.2 us)
Async XLA Ops:
  7.2 1.7 copy-start
  7.2 213.2 %reduce-scatter.4.cloned.1.call-start = ((), (), s32[]{:S(2)}) async-start(), calls=%async_computation.3 | async-start | bytes 4325376 | tf_op jit(solution)/shard_map/reduce_scatter | solution.py:71
  8.8 9.0 %copy-start.3 = (s32[4,8]{1,0:T(4,128)S(1)}, s32[4,8]{1,0:T(4,128)}, u32[]{:S(2)}) copy-start(s32[4,8]{1,0:T(4,128)} %param.15) | copy-start | bytes 388
  8.8 9.0 %copy-start.4 = (s32[8192]{0:T(1024)S(1)}, s32[8192]{0:T(1024)}, u32[]{:S(2)}) copy-start(s32[8192]{0:T(1024)} %param.14) | copy-start | bytes 98308
  22.8 25.3 %copy-start.1 = (bf16[8192,128]{1,0:T(8,128)(2,1)S(1)}, bf16[8192,128]{1,0:T(8,128)(2,1)}, u32[]{:S(2)}) copy-start(bf16[8192,128]{1,0:T(8,128)(2,1)} %param.10) | copy-start | bytes 6291460
  22.8 25.3 %copy-start.2 = (bf16[128,512]{1,0:T(8,128)(2,1)S(1)}, bf16[128,512]{1,0:T(8,128)(2,1)}, u32[]{:S(2)}) copy-start(bf16[128,512]{1,0:T(8,128)(2,1)} %param.11) | copy-start | bytes 393220
  119.2 202.7 %reduce-scatter.6.cloned.1.call-start = ((), (), s32[]{:S(2)}) async-start(), calls=%async_computation.4 | async-start | bytes 4325376 | tf_op jit(solution)/shard_map/reduce_scatter | solution.py:72
  164.6 336.1 %reduce-scatter.8.cloned.1.call-start = ((), (), s32[]{:S(2)}) async-start(), calls=%async_computation.5 | async-start | bytes 9437184 | tf_op jit(solution)/shard_map/reduce_scatter | solution.py:86
Sparse Core Ops, SparseCore 0:
  119.3 101.0 reduce-scatter.3
  224.9 96.9 reduce-scatter.5
  330.5 170.0 reduce-scatter.7
where the time goes:
time: 512 us; the launch traced here: 509 us
  waiting for transfers between devices  315 us (62%)
  local copies, waits for them, and re-layouts  66.1 us (13%)
  other arithmetic  59.3 us (12%)
  matrix products  55.1 us (11%)
  between operations  13.8 us (3%)
    reduce_scatter x1, waiting for transfers between devices, on_device(): lax.psum_scatter(visual_term, 'ha', scatter_dimension=1, tiled=True)  164 us
    reduce_scatter x1, waiting for transfers between devices, on_device(): lax.psum_scatter(value_part, ('pb', 'af'), scatter_dimension=0, tiled=True)  95.3 us
    reduce_scatter x1, waiting for transfers between devices, on_device(): lax.psum_scatter(key_part, ('pb', 'af'), scatter_dimension=0, tiled=True)  55.8 us
    sub x1, other arithmetic, attend(): numer = jnp.where(mask_cube, jnp.exp(scores - row_max), 0.0)  25.3 us
    sub x1, other arithmetic, attend(): prob_grad - row_delta  25 us
    convert_element_type x1, local copies, waits for them, and re-layouts, attend(): (attn_prob * (prob_grad - row_delta) * score_scale).astype(jnp.bfloat16)  17.7 us
    convert_element_type x1, local copies, waits for them, and re-layouts, attend(): prob_low = attn_prob.astype(jnp.bfloat16)  17.7 us
    reshape x1, local copies, waits for them, and re-layouts, attend(): prob_rows = prob_low.reshape(tok_rows * head_count, -1)  12.7 us
  transfers between devices with their start and end apart: 3, of which 3 were waited for; matrix products, arithmetic and copies ran while one was open for 11% of the time, Pallas kernels for 0%

commit v1 on v0

v1 whole, which is shorter than its diff:
```python
import functools

import jax
import jax.numpy as jnp
from jax import lax
from jax.experimental import pallas as pl
from jax.experimental.pallas import tpu as pltpu
from jax.sharding import PartitionSpec as P

DH = 128
FRAMES = 8
QBLK = 32
TOK = 128
ROWS = 512
VISUAL = 8192
CHUNKS = 2
PIECE = 256 // CHUNKS
SUB = 512
TILE = 2048
SCALE = DH**-0.5
C2 = SCALE * 1.4426950408889634
BIG = 2.0**100
F32 = jnp.float32
BF16 = jnp.bfloat16
NN = (((1,), (0,)), ((), ()))
NT = (((1,), (1,)), ((), ()))
TN = (((0,), (0,)), ((), ()))


def dot(a, b, dims):
    return lax.dot_general(a, b, dims, preferred_element_type=F32)


def marks(base, rows, first, last):
    at = base + lax.broadcasted_iota(jnp.int32, (rows, 128), 0)
    return jnp.where((at >= first) & (at < last), 1.0, 0.0).astype(BF16)


def pieces(x):
    hi = x.astype(BF16).astype(F32)
    rest = x - hi
    mid = rest.astype(BF16).astype(F32)
    return hi, mid, rest - mid


def stat_rows(top, x):
    hi, mid, low = pieces(x)
    row = lax.broadcasted_iota(jnp.int32, top.shape, 0)
    under = jnp.where(row == 0, hi, jnp.where(row == 1, mid, jnp.where(row == 2, low, 0.0)))
    return jnp.concatenate([top, under], axis=0).astype(BF16)


def stats_kernel(mask_ref, fid_ref, q_ref, d_ref, k_ref, v_ref, own_ref, edge_ref, qt, dt, top, m_ref, l_ref, o_ref):
    step = pl.program_id(0)

    @pl.when(step == 0)
    def _():
        fid = fid_ref[...]
        lane = lax.broadcasted_iota(jnp.int32, (8, 128), 1)
        first = jnp.zeros((8, 128), jnp.int32)
        last = jnp.where(lane < 8 + 3, VISUAL, 0)
        for f in range(1, FRAMES):
            below = jnp.sum((fid < f).astype(F32), axis=(0, 1), keepdims=True).astype(jnp.int32)
            first = jnp.where(lane == f, below, first)
            last = jnp.where(lane == f - 1, below, last)
        edge_ref[0] = first
        edge_ref[1] = last
        sub = lax.broadcasted_iota(jnp.int32, (8, 128), 0)
        bias = jnp.zeros((8, 128), F32)
        for b in range(TOK // QBLK):
            for f in range(FRAMES):
                here = (sub == f) & (lane // QBLK == b)
                bias = jnp.where(here, jnp.where(mask_ref[b, f] == 1, 0.0, -BIG), bias)
        top[...] = jnp.concatenate([bias] * 4, axis=1)
        for h in range(4):
            cols = slice(h * DH, (h + 1) * DH)
            qt[:DH, cols] = q_ref[:, cols].T
            dt[:, cols] = d_ref[:, cols].T
        qt[DH:DH + 16, :] = jnp.concatenate([top[...], jnp.zeros((8, ROWS), F32)], axis=0).astype(BF16)
        qt[DH + 16:, :] = jnp.zeros((DH - 16, ROWS), BF16)
        m_ref[...] = jnp.full((1, ROWS), -3e38, F32)
        l_ref[...] = jnp.zeros((1, ROWS), F32)
        o_ref[...] = jnp.zeros((DH, ROWS), F32)

    first, last = edge_ref[0, 0:1], edge_ref[1, 0:1]
    qa = qt[...]
    m, l, o = m_ref[...], l_ref[...], o_ref[...]
    for s in range(TILE // SUB):
        at = slice(s * SUB, (s + 1) * SUB)
        ka = jnp.concatenate([k_ref[at], marks(step * TILE + s * SUB, SUB, first, last)], axis=1)
        x = dot(ka, qa, NN) * C2
        m_new = jnp.maximum(m, jnp.max(x, axis=0, keepdims=True))
        shrink = jnp.exp2(m - m_new)
        p = jnp.exp2(x - m_new)
        l = l * shrink + jnp.sum(p, axis=0, keepdims=True)
        o = o * shrink + dot(v_ref[at], p.astype(BF16), TN)
        m = m_new
    m_ref[...], l_ref[...], o_ref[...] = m, l, o

    @pl.when(step == VISUAL // TILE - 1)
    def _():
        own_ref[0, :DH] = qt[:DH, :]
        own_ref[0, DH:] = stat_rows(top[...], (m + jnp.log2(l)) * (-1.0 / C2))
        delta = jnp.sum(dt[...].astype(F32) * o, axis=0, keepdims=True) / l
        own_ref[1, :DH] = dt[...]
        own_ref[1, DH:] = stat_rows(jnp.zeros((8, ROWS), F32), -delta)


def softmax_stats(queries, out_grad, keys, values, frame_ids, text_mask):
    whole = lambda *shape: pl.BlockSpec(shape, lambda i: (0,) * len(shape))
    tile = pl.BlockSpec((TILE, DH), lambda i: (i, 0))
    return pl.pallas_call(
        stats_kernel,
        grid=(VISUAL // TILE,),
        in_specs=[
            pl.BlockSpec(memory_space=pltpu.SMEM),
            whole(VISUAL // 128, 128),
            whole(TOK, ROWS),
            whole(TOK, ROWS),
            tile,
            tile,
        ],
        out_specs=[whole(2, DH + 16, ROWS), whole(2, 8, 128)],
        out_shape=[
            jax.ShapeDtypeStruct((2, DH + 16, ROWS), BF16),
            jax.ShapeDtypeStruct((2, 8, 128), jnp.int32),
        ],
        scratch_shapes=[
            pltpu.VMEM((2 * DH, ROWS), BF16),
            pltpu.VMEM((DH, ROWS), BF16),
            pltpu.VMEM((8, ROWS), F32),
            pltpu.VMEM((1, ROWS), F32),
            pltpu.VMEM((1, ROWS), F32),
            pltpu.VMEM((DH, ROWS), F32),
        ],
        compiler_params=pltpu.CompilerParams(vmem_limit_bytes=40 << 20),
        name="softmax_stats",
    )(text_mask, frame_ids.reshape(VISUAL // 128, 128), queries, out_grad, keys, values)


def grads_kernel(chunk, place, k_ref, v_ref, q_ref, d_ref, q2_ref, d2_ref, own_ref, other_ref, edge_ref, *rest):
    if chunk:
        sofar_ref, *rest = rest
    kk, ks, vk, vs, qsum, qt, dt, qr, dr = rest
    y, z, af = place[0], place[1], place[2]
    for side, (b, qq, dd) in enumerate(((own_ref, q_ref, d_ref), (other_ref, q2_ref, d2_ref))):
        cols = slice(side * ROWS, (side + 1) * ROWS)
        qt[:DH + 16, cols] = b[0]
        dt[:DH + 16, cols] = b[1]
        for h in range(4):
            at = slice(side * ROWS + h * TOK, side * ROWS + (h + 1) * TOK)
            qr[at] = qq[:, h * DH:(h + 1) * DH]
            dr[at] = dd[:, h * DH:(h + 1) * DH]
    qt[DH + 16:] = jnp.zeros((DH - 16, 2 * ROWS), BF16)
    dt[DH + 16:] = jnp.zeros((DH - 16, 2 * ROWS), BF16)
    first, last = edge_ref[0, 0:1], edge_ref[1, 0:1]
    total = sofar_ref[...] if chunk else jnp.zeros((DH, 2 * ROWS), F32)
    for r in range(4):
        kl, vl, ml = [], [], []
        for s in range(4):
            kl.append(k_ref[y ^ r, z ^ s, 0, 0])
            vl.append(v_ref[y ^ r, z ^ s, 0, 0])
            ml.append(marks((y ^ r) * 2048 + (z ^ s) * 512 + af * 256 + chunk * PIECE, PIECE, first, last))
        k = jnp.concatenate(kl, axis=0)
        mark = jnp.concatenate(ml, axis=0)
        p = jnp.exp2(dot(jnp.concatenate([k, mark], axis=1), qt[...], NN) * C2)
        dp = dot(jnp.concatenate([jnp.concatenate(vl, axis=0), mark], axis=1), dt[...], NN)
        ds = (p * dp).astype(BF16)
        kp = (dot(ds, qr[...], NN) * SCALE).astype(BF16)
        vp = dot(p.astype(BF16), dr[...], NN).astype(BF16)
        total = total + dot(k, ds, TN)
        kref, kat = ((kk, 0), (ks, 0), (ks, 1), (kk, 1))[r]
        vref, vat = ((vk, 0), (vk, 1), (vs, 1), (vs, 0))[r]
        kref[kat] = kp
        vref[vat] = vp
    qsum[...] = total


def chunk_grads(chunk, place, keys, values, q, d, q2, d2, own, other, edge, sofar):
    view = (4, 4, 2, CHUNKS, PIECE, DH)
    block = pl.BlockSpec((4, 4, 1, 1, PIECE, DH), lambda i, p: (0, 0, p[2], chunk, 0, 0))
    whole = lambda *shape: pl.BlockSpec(shape, lambda i, p: (0,) * len(shape))
    part = jax.ShapeDtypeStruct((2, 4 * PIECE, DH), BF16)
    more = [] if sofar is None else [sofar]
    return pl.pallas_call(
        functools.partial(grads_kernel, chunk),
        grid_spec=pltpu.PrefetchScalarGridSpec(
            num_scalar_prefetch=1,
            grid=(1,),
            in_specs=[block, block]
            + [whole(TOK, ROWS)] * 4
            + [whole(2, DH + 16, ROWS)] * 2
            + [whole(2, 8, 128)]
            + [whole(DH, 2 * ROWS)] * len(more),
            out_specs=[whole(2, 4 * PIECE, DH)] * 4 + [whole(DH, 2 * ROWS)],
            scratch_shapes=[
                pltpu.VMEM((2 * DH, 2 * ROWS), BF16),
                pltpu.VMEM((2 * DH, 2 * ROWS), BF16),
                pltpu.VMEM((2 * ROWS, DH), BF16),
                pltpu.VMEM((2 * ROWS, DH), BF16),
            ],
        ),
        out_shape=[part] * 4 + [jax.ShapeDtypeStruct((DH, 2 * ROWS), F32)],
        compiler_params=pltpu.CompilerParams(vmem_limit_bytes=48 << 20),
        name=f"chunk_grads_{chunk}",
    )(place, keys.reshape(view), values.reshape(view), q, d, q2, d2, own, other, edge, *more)


def query_kernel(mine_ref, got_ref, out_ref):
    total = (mine_ref[...] + got_ref[...].astype(F32)) * SCALE
    for h in range(4):
        out_ref[:, h * DH:(h + 1) * DH] = total[:, h * TOK:(h + 1) * TOK].T.astype(BF16)


def query_out(sums, got):
    return pl.pallas_call(
        query_kernel,
        grid=(1,),
        in_specs=[pl.BlockSpec((DH, ROWS), lambda i: (0, 0))] * 2,
        out_specs=pl.BlockSpec((TOK, ROWS), lambda i: (0, 0)),
        out_shape=jax.ShapeDtypeStruct((TOK, ROWS), BF16),
        name="query_out",
    )(sums, got)


def visual_kernel(place, mine_ref, other_ref, *rest):
    *parts, out_ref = rest
    af, x, zl = place[2], place[3], place[4]
    for ref, half in ((mine_ref, af), (other_ref, 1 - af)):
        total = jnp.zeros((256, 512), F32)
        for k in range(4):
            for e in range(2):
                source = ((x - k) & 3) * 2 + (zl ^ e)
                g = jnp.concatenate([parts[c * 4 + k][e] for c in range(CHUNKS)], axis=0)
                total = total + dot(g, ref[source], NT)
        out_ref[:, pl.ds(pl.multiple_of(half * 512, 512), 512)] = total.astype(BF16)


def visual_out(place, mine, other, parts):
    whole = lambda *shape: pl.BlockSpec(shape, lambda i, p: (0,) * len(shape))
    return pl.pallas_call(
        visual_kernel,
        grid_spec=pltpu.PrefetchScalarGridSpec(
            num_scalar_prefetch=1,
            grid=(1,),
            in_specs=[whole(8, 512, 256)] * 2 + [whole(2, PIECE, 256)] * len(parts),
            out_specs=whole(256, 1024),
        ),
        out_shape=jax.ShapeDtypeStruct((256, 1024), BF16),
        compiler_params=pltpu.CompilerParams(vmem_limit_bytes=32 << 20),
        name="visual_out",
    )(place, mine, other, *parts)


def swap_cores(a):
    return lax.ppermute(a, "af", [(0, 1), (1, 0)])


def along_y(a, bit):
    return lax.ppermute(a, "pb", [(i, i ^ (4 * bit)) for i in range(16)])


def along_z(a, bit):
    return lax.ppermute(a, "pb", [(i, i ^ bit) for i in range(16)])


def along_x(a, k):
    return lax.ppermute(a, "ha", [(i, (i + 2 * k) % 8) for i in range(8)])


def add(a, b):
    return (a.astype(F32) + b.astype(F32)).astype(BF16)


def reduce_chunk(kk, ks, vk, vs):
    rk, rv = along_y(ks, 1), along_y(vs, 3)
    rk2 = along_y(add(kk[1], rk[1]), 3)
    rv2 = along_y(add(vk[1], rv[1]), 1)
    k = (kk[0].astype(F32) + rk[0].astype(F32) + rk2.astype(F32)).astype(BF16).reshape(4, PIECE, DH)
    v = (vk[0].astype(F32) + rv[0].astype(F32) + rv2.astype(F32)).astype(BF16).reshape(4, PIECE, DH)
    rk, rv = along_z(k[1:3], 1), along_z(v[2:4], 3)
    rk2 = along_z(add(k[3], rk[1]), 3)
    rv2 = along_z(add(v[1], rv[0]), 1)
    k = (k[0].astype(F32) + rk[0].astype(F32) + rk2.astype(F32)).astype(BF16)
    v = (v[0].astype(F32) + rv[1].astype(F32) + rv2.astype(F32)).astype(BF16)
    g = jnp.concatenate([k, v], axis=1)
    pair = jnp.stack([g, lax.ppermute(g, "ha", [(i, i ^ 1) for i in range(8)])])
    return [pair] + [along_x(pair, i) for i in (1, 2, 3)]


def on_device(queries, vis_keys, vis_values, out_grad, key_weight, value_weight, frame_ids, text_mask):
    pb, ha, af = lax.axis_index("pb"), lax.axis_index("ha"), lax.axis_index("af")
    place = jnp.stack([pb // 4, pb % 4, af, ha // 2, ha % 2]).astype(jnp.int32)
    queries2, out_grad2 = swap_cores(queries), swap_cores(out_grad)
    half = lambda w: lax.dynamic_index_in_dim(w.reshape(8, 2, 512, DH), af, 1, keepdims=False)
    weights = jnp.concatenate([half(key_weight), half(value_weight)], axis=2)
    weights = lax.all_to_all(weights, "ha", 0, 0, tiled=True)
    weights2 = swap_cores(weights)
    own, edge = softmax_stats(queries, out_grad, vis_keys, vis_values, frame_ids, text_mask)
    other = swap_cores(own)
    qsum, parts = None, []
    for chunk in range(CHUNKS):
        kk, ks, vk, vs, qsum = chunk_grads(
            chunk, place, vis_keys, vis_values, queries, out_grad, queries2, out_grad2, own, other, edge, qsum
        )
        parts += reduce_chunk(kk, ks, vk, vs)
    query_grad = query_out(qsum[:, :ROWS], swap_cores(qsum[:, ROWS:].astype(BF16)))
    visual_grad = visual_out(place, weights, weights2, parts)
    return query_grad, visual_grad


def solution(mesh):
    in_specs = (
        P("pb", ("ha", "af")),
        P(None, "ha"),
        P(None, "ha"),
        P("pb", ("ha", "af")),
        P(None, "ha"),
        P(None, "ha"),
        P(),
        P("pb", None),
    )
    out_specs = (P("pb", ("ha", "af")), P(("pb", "af"), "ha"))
    return jax.shard_map(on_device, mesh=mesh, in_specs=in_specs, out_specs=out_specs, check_vma=False)
```

time: 512 us -> 103 us (0.20)
  waiting for transfers between devices: 315 us -> 18.1 us
  local copies, waits for them, and re-layouts: 66.1 us -> 5.13 us
  other arithmetic: 59.3 us -> 2.11 us
  matrix products: 55.1 us -> 0 us
  starting transfers between devices: 0.12 us -> 46 us
  Pallas kernels: 0 us -> 29.4 us
  between operations: 13.8 us -> 0.99 us
    reduce_scatter x3 -> x0, waiting for transfers between devices: 315 us -> none  [the longest x1 164 us: on_device(): lax.psum_scatter(visual_term, 'ha', scatter_dimension=1, tiled=True)]
    dot_general x8 -> x0, matrix products: 55.1 us -> none  [the longest x1 8.98 us: attend(): lax.dot_general(query_rows, key_slab, contract_last, preferred_element_ty...]
    sub x2 -> x0, other arithmetic: 50.3 us -> none  [the longest x1 25.3 us: attend(): numer = jnp.where(mask_cube, jnp.exp(scores - row_max), 0.0)]
    ppermute x0 -> x29, starting transfers between devices: none -> 39.8 us  [the longest x8 17.1 us: along_z(): return lax.ppermute(a, 'pb', [(i, i ^ bit) for i in range(16)])]
    convert_element_type x3 -> x0, local copies, waits for them, and re-layouts: 36.2 us -> none  [the longest x1 17.7 us: attend(): (attn_prob * (prob_grad - row_delta) * score_scale).astype(jnp.bfloat16)]
    pallas_call x0 -> x5, Pallas kernels: none -> 29.4 us  [the longest x2 13.6 us: chunk_grads(): pl.pallas_call(functools.partial(grads_kernel, chunk), grid_spec=pltpu.Pr...]
    reshape x2 -> x0, local copies, waits for them, and re-layouts: 25.2 us -> none  [the longest x1 12.7 us: attend(): prob_rows = prob_low.reshape(tok_rows * head_count, -1)]
    ppermute x0 -> x29, waiting for transfers between devices: none -> 18.1 us  [the longest x8 8.85 us: along_y(): return lax.ppermute(a, 'pb', [(i, i ^ 4 * bit) for i in range(16)])]
  transfers between devices with their start and end apart: 3 -> 30, of which waited for: 3 -> 12; matrix products, arithmetic and copies ran while one was open for 11% -> 2% of each run, Pallas kernels for 0% -> 25%
where the time goes in v1:
time: 103 us; the launch traced here: 102 us
  starting transfers between devices  46 us (45%)
  Pallas kernels  29.4 us (29%)
  waiting for transfers between devices  18.1 us (18%)
  local copies, waits for them, and re-layouts  5.13 us (5%)
  other arithmetic  2.11 us (2%)
    ppermute x8, starting transfers between devices, along_z(): return lax.ppermute(a, 'pb', [(i, i ^ bit) for i in range(16)])  17.1 us
    pallas_call x2, Pallas kernels, chunk_grads(): pl.pallas_call(functools.partial(grads_kernel, chunk), grid_spec=pltpu.Pr...  13.6 us
    ppermute x8, starting transfers between devices, along_y(): return lax.ppermute(a, 'pb', [(i, i ^ 4 * bit) for i in range(16)])  11.1 us
    ppermute x6, starting transfers between devices, along_x(): return lax.ppermute(a, 'ha', [(i, (i + 2 * k) % 8) for i in range(8)])  10.7 us
    pallas_call x1, Pallas kernels, softmax_stats(): pl.pallas_call(stats_kernel, grid=(VISUAL // TILE,), in_specs=[pl.BlockSp...  9.9 us
    ppermute x8, waiting for transfers between devices, along_y(): return lax.ppermute(a, 'pb', [(i, i ^ 4 * bit) for i in range(16)])  8.85 us
    all_to_all x1, starting transfers between devices, on_device(): weights = lax.all_to_all(weights, 'ha', 0, 0, tiled=True)  6.2 us
    ppermute x8, waiting for transfers between devices, along_z(): return lax.ppermute(a, 'pb', [(i, i ^ bit) for i in range(16)])  5.18 us
  transfers between devices with their start and end apart: 30, of which 12 were waited for; matrix products, arithmetic and copies ran while one was open for 2% of the time, Pallas kernels for 25%

profile of v1, /device:TPU:32, one launch (start us, length us, event | category | flops | bytes accessed | tf_op | source)
XLA Modules:
  0.0 101.8 jit_solution(7385114661732972113)
XLA Ops:
  0.6 1.7 %dynamic-slice_bitcast_fusion = (bf16[8,512,128]{2,1,0:T(8,128)(2,1)S(1)}, bf16[8,512,128]{2,1,0:T(8,128)(2,1)S(1)}) fusion(bf16[8,2,512,128]{3,2,1,0:T(8,128)(2,1)} %bitcast.97, s32[]{:T(128)S(6)} %select_n.27, bf16[8,2,512,128]{3,2,1,0:T(8,128)(2,1)} %bitcast.98), kind=kLoop, calls=%fused_computation.1 | loop fusion | bytes 4194308 | tf_op jit(solution)/shard_map/jit(dynamic_index_in_dim)/squeeze | solution.py:295
  3.9 6.2 %all-to-all-start = ((bf16[8,512,256]{2,1,0:T(8,128)(2,1)}), bf16[8,512,256]{2,1,0:T(8,128)(2,1)}, u32[]{:S(2)}, u32[]{:S(2)}) async-start(bf16[8,512,256]{2,1,0:T(8,128)(2,1)} %pad_maximum_fusion), calls=%async_computation | async-start | bytes 4194304 | tf_op jit(solution)/shard_map/all_to_all | solution.py:297
  10.2 1.6 %copy-done.1 = bf16[8192,128]{1,0:T(8,128)(2,1)S(1)} copy-done((bf16[8192,128]{1,0:T(8,128)(2,1)S(1)}, bf16[8192,128]{1,0:T(8,128)(2,1)}, u32[]{:S(2)}) %copy-start.1) | copy-done | bytes 2097176
  11.8 9.9 %softmax_stats.1 = (bf16[2,144,512]{2,1,0:T(8,128)(2,1)S(1)}, s32[2,8,128]{2,1,0:T(8,128)S(1)}) custom-call(s32[4,8]{1,0:T(4,128)S(1)} %copy-done.6, s32[64,128]{1,0:T(8,128)S(1)} %bitcast.96, bf16[128,512]{1,0:T(8,128)(2,1)S(1)} %copy-done.2, bf16[128,512]{1,0:T(8,128)(2,1)S(1)} %copy-done.3, bf16[8192,128]{1,0:T(8,128)(2,1)S(1)} %copy-done, ...), custom_call_target="tpu_custom_call" | custom-call | tf_op jit(solution)/shard_map/softmax_stats/pallas_call | solution.py:112
  23.7 6.8 %chunk_grads_0.1 = (bf16[2,512,128]{2,1,0:T(8,128)(2,1)S(1)}, bf16[2,512,128]{2,1,0:T(8,128)(2,1)S(1)}, bf16[2,512,128]{2,1,0:T(8,128)(2,1)S(1)}, bf16[2,512,128]{2,1,0:T(8,128)(2,1)S(1)}, f32[128,1024]{1,0:T(8,128)S(1)}) custom-call(s32[5]{0:T(128)S(1)} %stack.41.place, bf16[4,4,2,2,128,128]{5,4,3,2,1,0:T(8,128)(2,1)S(1)} %bitcast.92, ...), custom_call_target="tpu_custom_call" | custom-call | tf_op jit(solution)/shard_map/chunk_grads_0/pallas_call | solution.py:185
  30.5 6.8 %chunk_grads_1.1 = (bf16[2,512,128]{2,1,0:T(8,128)(2,1)S(1)}, bf16[2,512,128]{2,1,0:T(8,128)(2,1)S(1)}, bf16[2,512,128]{2,1,0:T(8,128)(2,1)S(1)}, bf16[2,512,128]{2,1,0:T(8,128)(2,1)S(1)}, f32[128,1024]{1,0:T(8,128)S(1)}) custom-call(s32[5]{0:T(128)S(1)} %stack.41.place, bf16[4,4,2,2,128,128]{5,4,3,2,1,0:T(8,128)(2,1)S(1)} %bitcast.93, ...), custom_call_target="tpu_custom_call" | custom-call | tf_op jit(solution)/shard_map/chunk_grads_1/pallas_call | solution.py:185
  38.7 2.2 %collective-permute-start.21 = (bf16[2,512,128]{2,1,0:T(8,128)(2,1)S(1)}, bf16[2,512,128]{2,1,0:T(8,128)(2,1)S(1)}, u32[]{:S(2)}, u32[]{:S(2)}) collective-permute-start(bf16[2,512,128]{2,1,0:T(8,128)(2,1)S(1)} %get-tuple-element.25), channel_id=1, source_target_pairs={{0,192},{16,208},{32,224},{48,240},{64,128},{80,144},{96,160},{112... | collective-permute-start | bytes 786440 | tf_op jit(solution)/shard_map/ppermute | solution.py:260
  42.4 4.1 %collective-permute-done.17 = bf16[2,512,128]{2,1,0:T(8,128)(2,1)S(1)} collective-permute-done((bf16[2,512,128]{2,1,0:T(8,128)(2,1)S(1)}, bf16[2,512,128]{2,1,0:T(8,128)(2,1)S(1)}, u32[]{:S(2)}, u32[]{:S(2)}) %collective-permute-start.17) | collective-permute-done | bytes 262176 | tf_op jit(solution)/shard_map/ppermute | solution.py:260
  46.6 2.8 %collective-permute-start.18 = (bf16[512,128]{1,0:T(8,128)(2,1)S(1)}, bf16[512,128]{1,0:T(8,128)(2,1)S(1)}, u32[]{:S(2)}, u32[]{:S(2)}) collective-permute-start(bf16[512,128]{1,0:T(8,128)(2,1)S(1)} %fusion.6), channel_id=1, source_target_pairs={{0,192},{16,208},{32,224},{48,240},{64,128},{80,144},{96,160},{112... | collective-permute-start | bytes 393224 | tf_op jit(solution)/shard_map/ppermute | solution.py:260
  49.7 2.5 %collective-permute-done.5 = bf16[2,512,128]{2,1,0:T(8,128)(2,1)S(1)} collective-permute-done((bf16[2,512,128]{2,1,0:T(8,128)(2,1)S(1)}, bf16[2,512,128]{2,1,0:T(8,128)(2,1)S(1)}, u32[]{:S(2)}, u32[]{:S(2)}) %collective-permute-start.5) | collective-permute-done | bytes 262176 | tf_op jit(solution)/shard_map/ppermute | solution.py:260
  52.2 2.8 %collective-permute-start.6 = (bf16[512,128]{1,0:T(8,128)(2,1)S(1)}, bf16[512,128]{1,0:T(8,128)(2,1)S(1)}, u32[]{:S(2)}, u32[]{:S(2)}) collective-permute-start(bf16[512,128]{1,0:T(8,128)(2,1)S(1)} %fusion.4), channel_id=1, source_target_pairs={{0,192},{16,208},{32,224},{48,240},{64,128},{80,144},{96,160},{112... | collective-permute-start | bytes 393224 | tf_op jit(solution)/shard_map/ppermute | solution.py:260
  55.3 2.2 %collective-permute-done.18 = bf16[512,128]{1,0:T(8,128)(2,1)S(1)} collective-permute-done((bf16[512,128]{1,0:T(8,128)(2,1)S(1)}, bf16[512,128]{1,0:T(8,128)(2,1)S(1)}, u32[]{:S(2)}, u32[]{:S(2)}) %collective-permute-start.18) | collective-permute-done | bytes 131104 | tf_op jit(solution)/shard_map/ppermute | solution.py:260
  57.6 3.3 %collective-permute-start.19 = (bf16[2,128,128]{2,1,0:T(8,128)(2,1)S(1)}, bf16[2,128,128]{2,1,0:T(8,128)(2,1)S(1)}, u32[]{:S(2)}, u32[]{:S(2)}) collective-permute-start(bf16[2,128,128]{2,1,0:T(8,128)(2,1)S(1)} %bitcast.99), channel_id=1, source_target_pairs={{0,16},{16,0},{32,48},{48,32},{64,80},{80,64},{96,112},{112,96},{1... | collective-permute-start | bytes 196616 | tf_op jit(solution)/shard_map/ppermute | solution.py:264
  61.0 3.7 %collective-permute-start.23 = (bf16[2,128,128]{2,1,0:T(8,128)(2,1)S(1)}, bf16[2,128,128]{2,1,0:T(8,128)(2,1)S(1)}, u32[]{:S(2)}, u32[]{:S(2)}) collective-permute-start(bf16[2,128,128]{2,1,0:T(8,128)(2,1)S(1)} %bitcast.101), channel_id=1, source_target_pairs={{0,48},{16,32},{32,16},{48,0},{64,112},{80,96},{96,80},{112,64},{1... | collective-permute-start | bytes 196616 | tf_op jit(solution)/shard_map/ppermute | solution.py:264
  64.7 1.6 %collective-permute-start.7 = (bf16[2,128,128]{2,1,0:T(8,128)(2,1)S(1)}, bf16[2,128,128]{2,1,0:T(8,128)(2,1)S(1)}, u32[]{:S(2)}, u32[]{:S(2)}) collective-permute-start(bf16[2,128,128]{2,1,0:T(8,128)(2,1)S(1)} %bitcast.100), channel_id=1, source_target_pairs={{0,16},{16,0},{32,48},{48,32},{64,80},{80,64},{96,112},{112,96},{1... | collective-permute-start | bytes 196616 | tf_op jit(solution)/shard_map/ppermute | solution.py:264
  66.6 4.2 %collective-permute-start.20 = (bf16[128,128]{1,0:T(8,128)(2,1)S(1)}, bf16[128,128]{1,0:T(8,128)(2,1)S(1)}, u32[]{:S(2)}, u32[]{:S(2)}) collective-permute-start(bf16[128,128]{1,0:T(8,128)(2,1)S(1)} %fusion.11), channel_id=1, source_target_pairs={{0,48},{16,32},{32,16},{48,0},{64,112},{80,96},{96,80},{112,64},{1... | collective-permute-start | bytes 98312 | tf_op jit(solution)/shard_map/ppermute | solution.py:264
  73.4 2.1 %collective-permute-start.8 = (bf16[128,128]{1,0:T(8,128)(2,1)S(1)}, bf16[128,128]{1,0:T(8,128)(2,1)S(1)}, u32[]{:S(2)}, u32[]{:S(2)}) collective-permute-start(bf16[128,128]{1,0:T(8,128)(2,1)S(1)} %fusion.17), channel_id=1, source_target_pairs={{0,48},{16,32},{32,16},{48,0},{64,112},{80,96},{96,80},{112,64},{1... | collective-permute-start | bytes 98312 | tf_op jit(solution)/shard_map/ppermute | solution.py:264
  76.3 3.1 %collective-permute-done.8 = bf16[128,128]{1,0:T(8,128)(2,1)S(1)} collective-permute-done((bf16[128,128]{1,0:T(8,128)(2,1)S(1)}, bf16[128,128]{1,0:T(8,128)(2,1)S(1)}, u32[]{:S(2)}, u32[]{:S(2)}) %collective-permute-start.8) | collective-permute-done | bytes 32800 | tf_op jit(solution)/shard_map/ppermute | solution.py:264
  80.6 2.9 %collective-permute-start.28 = (bf16[2,128,256]{2,1,0:T(8,128)(2,1)S(1)}, bf16[2,128,256]{2,1,0:T(8,128)(2,1)S(1)}, u32[]{:S(2)}, u32[]{:S(2)}) collective-permute-start(bf16[2,128,256]{2,1,0:T(8,128)(2,1)S(1)} %pad_maximum_fusion.2.rest_4_), channel_id=1, source_target_pairs={{0,12},{2,14},{4,0},{6,2},{8,4},{10,6},{12,8},{14,10},{1,13},{3,15... | collective-permute-start | bytes 393224 | tf_op jit(solution)/shard_map/ppermute | solution.py:268
  86.4 1.8 %collective-permute-start.16 = (bf16[2,128,256]{2,1,0:T(8,128)(2,1)S(1)}, bf16[2,128,256]{2,1,0:T(8,128)(2,1)S(1)}, u32[]{:S(2)}, u32[]{:S(2)}) collective-permute-start(bf16[2,128,256]{2,1,0:T(8,128)(2,1)S(1)} %pad_maximum_fusion.1.rest_0_), channel_id=1, source_target_pairs={{0,12},{2,14},{4,0},{6,2},{8,4},{10,6},{12,8},{14,10},{1,13},{3,15... | collective-permute-start | bytes 393224 | tf_op jit(solution)/shard_map/ppermute | solution.py:268
  91.4 2.3 %collective-permute-start.14 = (bf16[2,128,256]{2,1,0:T(8,128)(2,1)S(1)}, bf16[2,128,256]{2,1,0:T(8,128)(2,1)S(1)}, u32[]{:S(2)}, u32[]{:S(2)}) collective-permute-start(bf16[2,128,256]{2,1,0:T(8,128)(2,1)S(1)} %pad_maximum_fusion.1.rest_0_), channel_id=1, source_target_pairs={{0,4},{2,6},{4,8},{6,10},{8,12},{10,14},{12,0},{14,2},{1,5},{3,7},... | collective-permute-start | bytes 393224 | tf_op jit(solution)/shard_map/ppermute | solution.py:268
  93.7 1.7 %slice.135.mine_ref = f32[128,512]{1,0:T(8,128)} slice(f32[128,1024]{1,0:T(8,128)} %copy-done.4), slice={[0:128], [0:512]} | slice | bytes 524288 | tf_op jit(solution)/shard_map/slice | solution.py:307
  95.3 1.7 %query_out.1 = bf16[128,512]{1,0:T(8,128)(2,1)} custom-call(f32[128,512]{1,0:T(8,128)} %slice.135.mine_ref, bf16[128,512]{1,0:T(8,128)(2,1)} %copy-done.7), custom_call_target="tpu_custom_call" | custom-call | tf_op jit(solution)/shard_map/query_out/pallas_call | solution.py:216
  97.6 4.2 %visual_out.1 = bf16[256,1024]{1,0:T(8,128)(2,1)} custom-call(s32[5]{0:T(128)S(1)} %stack.41.place, bf16[8,512,256]{2,1,0:T(8,128)(2,1)} %all-to-all-done.mine_ref, bf16[8,512,256]{2,1,0:T(8,128)(2,1)S(1)} %collective-permute-done.4.other_ref, bf16[2,128,256]{2,1,0:T(8,128)(2,1)S(1)} %pad_maximum_fusion.1.rest_0_, ...), custom_call_target="tpu_custom_call" | custom-call | tf_op jit(solution)/shard_map/visual_out/pallas_call | solution.py:241
  (86 shorter events, 18.6 us)
Async XLA Ops:
  3.9 66.8 %all-to-all-start = ((bf16[8,512,256]{2,1,0:T(8,128)(2,1)}), bf16[8,512,256]{2,1,0:T(8,128)(2,1)}, u32[]{:S(2)}, u32[]{:S(2)}) async-start(bf16[8,512,256]{2,1,0:T(8,128)(2,1)} %pad_maximum_fusion), calls=%async_computation | async-start | bytes 4194304 | tf_op jit(solution)/shard_map/all_to_all | solution.py:297
  37.3 9.2 %collective-permute-start.17 = (bf16[2,512,128]{2,1,0:T(8,128)(2,1)S(1)}, bf16[2,512,128]{2,1,0:T(8,128)(2,1)S(1)}, u32[]{:S(2)}, u32[]{:S(2)}) collective-permute-start(bf16[2,512,128]{2,1,0:T(8,128)(2,1)S(1)} %get-tuple-element.23), channel_id=1, source_target_pairs={{0,64},{16,80},{32,96},{48,112},{64,0},{80,16},{96,32},{112,48},{1... | collective-permute-start | bytes 786440 | tf_op jit(solution)/shard_map/ppermute | solution.py:260
  38.7 10.7 %collective-permute-start.21 = (bf16[2,512,128]{2,1,0:T(8,128)(2,1)S(1)}, bf16[2,512,128]{2,1,0:T(8,128)(2,1)S(1)}, u32[]{:S(2)}, u32[]{:S(2)}) collective-permute-start(bf16[2,512,128]{2,1,0:T(8,128)(2,1)S(1)} %get-tuple-element.25), channel_id=1, source_target_pairs={{0,192},{16,208},{32,224},{48,240},{64,128},{80,144},{96,160},{112... | collective-permute-start | bytes 786440 | tf_op jit(solution)/shard_map/ppermute | solution.py:260
  40.9 45.5 %collective-permute-start.3 = (bf16[128,512]{1,0:T(8,128)(2,1)S(1)}, bf16[128,512]{1,0:T(8,128)(2,1)S(1)}, u32[]{:S(2)}, u32[]{:S(2)}) collective-permute-start(bf16[128,512]{1,0:T(8,128)(2,1)S(1)} %slice.255), channel_id=1, source_target_pairs={{0,1},{1,0},{2,3},{3,2},{4,5},{5,4},{6,7},{7,6},{8,9},{9,8},{10,11... | collective-permute-start | bytes 393224 | tf_op jit(solution)/shard_map/ppermute | solution.py:256
  41.0 11.2 %collective-permute-start.5 = (bf16[2,512,128]{2,1,0:T(8,128)(2,1)S(1)}, bf16[2,512,128]{2,1,0:T(8,128)(2,1)S(1)}, u32[]{:S(2)}, u32[]{:S(2)}) collective-permute-start(bf16[2,512,128]{2,1,0:T(8,128)(2,1)S(1)} %get-tuple-element.19), channel_id=1, source_target_pairs={{0,64},{16,80},{32,96},{48,112},{64,0},{80,16},{96,32},{112,48},{1... | collective-permute-start | bytes 786440 | tf_op jit(solution)/shard_map/ppermute | solution.py:260
  41.7 13.3 %collective-permute-start.9 = (bf16[2,512,128]{2,1,0:T(8,128)(2,1)S(1)}, bf16[2,512,128]{2,1,0:T(8,128)(2,1)S(1)}, u32[]{:S(2)}, u32[]{:S(2)}) collective-permute-start(bf16[2,512,128]{2,1,0:T(8,128)(2,1)S(1)} %get-tuple-element.21), channel_id=1, source_target_pairs={{0,192},{16,208},{32,224},{48,240},{64,128},{80,144},{96,160},{112... | collective-permute-start | bytes 786440 | tf_op jit(solution)/shard_map/ppermute | solution.py:260
  46.6 10.9 %collective-permute-start.18 = (bf16[512,128]{1,0:T(8,128)(2,1)S(1)}, bf16[512,128]{1,0:T(8,128)(2,1)S(1)}, u32[]{:S(2)}, u32[]{:S(2)}) collective-permute-start(bf16[512,128]{1,0:T(8,128)(2,1)S(1)} %fusion.6), channel_id=1, source_target_pairs={{0,192},{16,208},{32,224},{48,240},{64,128},{80,144},{96,160},{112... | collective-permute-start | bytes 393224 | tf_op jit(solution)/shard_map/ppermute | solution.py:260
  49.4 11.5 %collective-permute-start.22 = (bf16[512,128]{1,0:T(8,128)(2,1)S(1)}, bf16[512,128]{1,0:T(8,128)(2,1)S(1)}, u32[]{:S(2)}, u32[]{:S(2)}) collective-permute-start(bf16[512,128]{1,0:T(8,128)(2,1)S(1)} %fusion.7), channel_id=1, source_target_pairs={{0,64},{16,80},{32,96},{48,112},{64,0},{80,16},{96,32},{112,48},{1... | collective-permute-start | bytes 393224 | tf_op jit(solution)/shard_map/ppermute | solution.py:260
  52.2 12.5 %collective-permute-start.6 = (bf16[512,128]{1,0:T(8,128)(2,1)S(1)}, bf16[512,128]{1,0:T(8,128)(2,1)S(1)}, u32[]{:S(2)}, u32[]{:S(2)}) collective-permute-start(bf16[512,128]{1,0:T(8,128)(2,1)S(1)} %fusion.4), channel_id=1, source_target_pairs={{0,192},{16,208},{32,224},{48,240},{64,128},{80,144},{96,160},{112... | collective-permute-start | bytes 393224 | tf_op jit(solution)/shard_map/ppermute | solution.py:260
  55.1 11.3 %collective-permute-start.10 = (bf16[512,128]{1,0:T(8,128)(2,1)S(1)}, bf16[512,128]{1,0:T(8,128)(2,1)S(1)}, u32[]{:S(2)}, u32[]{:S(2)}) collective-permute-start(bf16[512,128]{1,0:T(8,128)(2,1)S(1)} %fusion.5), channel_id=1, source_target_pairs={{0,64},{16,80},{32,96},{48,112},{64,0},{80,16},{96,32},{112,48},{1... | collective-permute-start | bytes 393224 | tf_op jit(solution)/shard_map/ppermute | solution.py:260
  57.6 9.0 %collective-permute-start.19 = (bf16[2,128,128]{2,1,0:T(8,128)(2,1)S(1)}, bf16[2,128,128]{2,1,0:T(8,128)(2,1)S(1)}, u32[]{:S(2)}, u32[]{:S(2)}) collective-permute-start(bf16[2,128,128]{2,1,0:T(8,128)(2,1)S(1)} %bitcast.99), channel_id=1, source_target_pairs={{0,16},{16,0},{32,48},{48,32},{64,80},{80,64},{96,112},{112,96},{1... | collective-permute-start | bytes 196616 | tf_op jit(solution)/shard_map/ppermute | solution.py:264
  61.0 9.8 %collective-permute-start.23 = (bf16[2,128,128]{2,1,0:T(8,128)(2,1)S(1)}, bf16[2,128,128]{2,1,0:T(8,128)(2,1)S(1)}, u32[]{:S(2)}, u32[]{:S(2)}) collective-permute-start(bf16[2,128,128]{2,1,0:T(8,128)(2,1)S(1)} %bitcast.101), channel_id=1, source_target_pairs={{0,48},{16,32},{32,16},{48,0},{64,112},{80,96},{96,80},{112,64},{1... | collective-permute-start | bytes 196616 | tf_op jit(solution)/shard_map/ppermute | solution.py:264
  64.7 6.1 %collective-permute-start.7 = (bf16[2,128,128]{2,1,0:T(8,128)(2,1)S(1)}, bf16[2,128,128]{2,1,0:T(8,128)(2,1)S(1)}, u32[]{:S(2)}, u32[]{:S(2)}) collective-permute-start(bf16[2,128,128]{2,1,0:T(8,128)(2,1)S(1)} %bitcast.100), channel_id=1, source_target_pairs={{0,16},{16,0},{32,48},{48,32},{64,80},{80,64},{96,112},{112,96},{1... | collective-permute-start | bytes 196616 | tf_op jit(solution)/shard_map/ppermute | solution.py:264
  66.4 6.9 %collective-permute-start.11 = (bf16[2,128,128]{2,1,0:T(8,128)(2,1)S(1)}, bf16[2,128,128]{2,1,0:T(8,128)(2,1)S(1)}, u32[]{:S(2)}, u32[]{:S(2)}) collective-permute-start(bf16[2,128,128]{2,1,0:T(8,128)(2,1)S(1)} %bitcast.102), channel_id=1, source_target_pairs={{0,48},{16,32},{32,16},{48,0},{64,112},{80,96},{96,80},{112,64},{1... | collective-permute-start | bytes 196616 | tf_op jit(solution)/shard_map/ppermute | solution.py:264
  66.6 8.9 %collective-permute-start.20 = (bf16[128,128]{1,0:T(8,128)(2,1)S(1)}, bf16[128,128]{1,0:T(8,128)(2,1)S(1)}, u32[]{:S(2)}, u32[]{:S(2)}) collective-permute-start(bf16[128,128]{1,0:T(8,128)(2,1)S(1)} %fusion.11), channel_id=1, source_target_pairs={{0,48},{16,32},{32,16},{48,0},{64,112},{80,96},{96,80},{112,64},{1... | collective-permute-start | bytes 98312 | tf_op jit(solution)/shard_map/ppermute | solution.py:264
  70.8 26.8 %collective-permute-start.4 = (bf16[8,512,256]{2,1,0:T(8,128)(2,1)}, bf16[8,512,256]{2,1,0:T(8,128)(2,1)S(1)}, u32[]{:S(2)}, u32[]{:S(2)}) collective-permute-start(bf16[8,512,256]{2,1,0:T(8,128)(2,1)} %all-to-all-done.mine_ref), channel_id=1, source_target_pairs={{0,1},{1,0},{2,3},{3,2},{4,5},{5,4},{6,7},{7,6},{8,9},{9,8},{10,11... | collective-permute-start | bytes 6291464 | tf_op jit(solution)/shard_map/ppermute | solution.py:256
  70.8 5.3 %collective-permute-start.24 = (bf16[128,128]{1,0:T(8,128)(2,1)S(1)}, bf16[128,128]{1,0:T(8,128)(2,1)S(1)}, u32[]{:S(2)}, u32[]{:S(2)}) collective-permute-start(bf16[128,128]{1,0:T(8,128)(2,1)S(1)} %fusion.8), channel_id=1, source_target_pairs={{0,16},{16,0},{32,48},{48,32},{64,80},{80,64},{96,112},{112,96},{1... | collective-permute-start | bytes 98312 | tf_op jit(solution)/shard_map/ppermute | solution.py:264
  73.4 6.0 %collective-permute-start.8 = (bf16[128,128]{1,0:T(8,128)(2,1)S(1)}, bf16[128,128]{1,0:T(8,128)(2,1)S(1)}, u32[]{:S(2)}, u32[]{:S(2)}) collective-permute-start(bf16[128,128]{1,0:T(8,128)(2,1)S(1)} %fusion.17), channel_id=1, source_target_pairs={{0,48},{16,32},{32,16},{48,0},{64,112},{80,96},{96,80},{112,64},{1... | collective-permute-start | bytes 98312 | tf_op jit(solution)/shard_map/ppermute | solution.py:264
  80.6 8.1 %collective-permute-start.28 = (bf16[2,128,256]{2,1,0:T(8,128)(2,1)S(1)}, bf16[2,128,256]{2,1,0:T(8,128)(2,1)S(1)}, u32[]{:S(2)}, u32[]{:S(2)}) collective-permute-start(bf16[2,128,256]{2,1,0:T(8,128)(2,1)S(1)} %pad_maximum_fusion.2.rest_4_), channel_id=1, source_target_pairs={{0,12},{2,14},{4,0},{6,2},{8,4},{10,6},{12,8},{14,10},{1,13},{3,15... | collective-permute-start | bytes 393224 | tf_op jit(solution)/shard_map/ppermute | solution.py:268
  83.5 7.9 %collective-permute-start.27 = (bf16[2,128,256]{2,1,0:T(8,128)(2,1)S(1)}, bf16[2,128,256]{2,1,0:T(8,128)(2,1)S(1)}, u32[]{:S(2)}, u32[]{:S(2)}) collective-permute-start(bf16[2,128,256]{2,1,0:T(8,128)(2,1)S(1)} %pad_maximum_fusion.2.rest_4_), channel_id=1, source_target_pairs={{0,8},{2,10},{4,12},{6,14},{8,0},{10,2},{12,4},{14,6},{1,9},{3,11}... | collective-permute-start | bytes 393224 | tf_op jit(solution)/shard_map/ppermute | solution.py:268
  84.8 12.3 %collective-permute-start.26 = (bf16[2,128,256]{2,1,0:T(8,128)(2,1)S(1)}, bf16[2,128,256]{2,1,0:T(8,128)(2,1)S(1)}, u32[]{:S(2)}, u32[]{:S(2)}) collective-permute-start(bf16[2,128,256]{2,1,0:T(8,128)(2,1)S(1)} %pad_maximum_fusion.2.rest_4_), channel_id=1, source_target_pairs={{0,4},{2,6},{4,8},{6,10},{8,12},{10,14},{12,0},{14,2},{1,5},{3,7},... | collective-permute-start | bytes 393224 | tf_op jit(solution)/shard_map/ppermute | solution.py:268
  86.4 10.7 %collective-permute-start.16 = (bf16[2,128,256]{2,1,0:T(8,128)(2,1)S(1)}, bf16[2,128,256]{2,1,0:T(8,128)(2,1)S(1)}, u32[]{:S(2)}, u32[]{:S(2)}) collective-permute-start(bf16[2,128,256]{2,1,0:T(8,128)(2,1)S(1)} %pad_maximum_fusion.1.rest_0_), channel_id=1, source_target_pairs={{0,12},{2,14},{4,0},{6,2},{8,4},{10,6},{12,8},{14,10},{1,13},{3,15... | collective-permute-start | bytes 393224 | tf_op jit(solution)/shard_map/ppermute | solution.py:268
  88.6 8.5 %collective-permute-start.15 = (bf16[2,128,256]{2,1,0:T(8,128)(2,1)S(1)}, bf16[2,128,256]{2,1,0:T(8,128)(2,1)S(1)}, u32[]{:S(2)}, u32[]{:S(2)}) collective-permute-start(bf16[2,128,256]{2,1,0:T(8,128)(2,1)S(1)} %pad_maximum_fusion.1.rest_0_), channel_id=1, source_target_pairs={{0,8},{2,10},{4,12},{6,14},{8,0},{10,2},{12,4},{14,6},{1,9},{3,11}... | collective-permute-start | bytes 393224 | tf_op jit(solution)/shard_map/ppermute | solution.py:268
  91.4 6.2 %collective-permute-start.14 = (bf16[2,128,256]{2,1,0:T(8,128)(2,1)S(1)}, bf16[2,128,256]{2,1,0:T(8,128)(2,1)S(1)}, u32[]{:S(2)}, u32[]{:S(2)}) collective-permute-start(bf16[2,128,256]{2,1,0:T(8,128)(2,1)S(1)} %pad_maximum_fusion.1.rest_0_), channel_id=1, source_target_pairs={{0,4},{2,6},{4,8},{6,10},{8,12},{10,14},{12,0},{14,2},{1,5},{3,7},... | collective-permute-start | bytes 393224 | tf_op jit(solution)/shard_map/ppermute | solution.py:268
  (14 other events, 89.8 us)

commit v2 on v1

v2 whole, which is shorter than its diff:
```python
import functools

import jax
import jax.numpy as jnp
from jax import lax
from jax.experimental import pallas as pl
from jax.experimental.pallas import tpu as pltpu
from jax.sharding import PartitionSpec as P

DH = 128
FRAMES = 8
QBLK = 32
TOK = 128
ROWS = 512
VISUAL = 8192
CHUNKS = 2
PIECE = 256 // CHUNKS
SUB = 512
TILE = 2048
SCALE = DH**-0.5
C2 = SCALE * 1.4426950408889634
BIG = 2.0**100
VMEM_A = 60
VMEM_B = 58
F32 = jnp.float32
BF16 = jnp.bfloat16
NN = (((1,), (0,)), ((), ()))
NT = (((1,), (1,)), ((), ()))
TN = (((0,), (0,)), ((), ()))


def dot(a, b, dims):
    return lax.dot_general(a, b, dims, preferred_element_type=F32)


def cost(us):
    return pl.CostEstimate(flops=int(us * 1.1e9), transcendentals=0, bytes_accessed=1 << 20)


def marks(base, rows, first, last):
    at = base + lax.broadcasted_iota(jnp.int32, (rows, 128), 0)
    return jnp.where((at >= first) & (at < last), 1.0, 0.0).astype(BF16)


def pieces(x):
    hi = x.astype(BF16).astype(F32)
    rest = x - hi
    mid = rest.astype(BF16).astype(F32)
    return hi, mid, rest - mid


def stat_rows(top, x):
    hi, mid, low = pieces(x)
    row = lax.broadcasted_iota(jnp.int32, top.shape, 0)
    under = jnp.where(row == 0, hi, jnp.where(row == 1, mid, jnp.where(row == 2, low, 0.0)))
    return jnp.concatenate([top, under], axis=0).astype(BF16)


def stats_kernel(
    mask_ref, fid_ref, q_ref, d_ref, k_hbm, v_hbm, kw_hbm, vw_hbm, own_ref, edge_ref, w_hbm, k_ref, v_ref, qt, dt, sems, wsem
):
    af = lax.axis_index("af")
    loads = []
    for t in range(VISUAL // TILE):
        at = pl.ds(t * TILE, TILE)
        loads.append(
            [
                pltpu.make_async_copy(k_hbm.at[at], k_ref.at[at], sems.at[0, t]),
                pltpu.make_async_copy(v_hbm.at[at], v_ref.at[at], sems.at[1, t]),
            ]
        )
        for load in loads[t]:
            load.start()
    moves = [pltpu.make_async_copy(w.at[:, af], w_hbm.at[:, i], wsem.at[i]) for i, w in enumerate((kw_hbm, vw_hbm))]
    for move in moves:
        move.start()
    fid = fid_ref[...]
    lane = lax.broadcasted_iota(jnp.int32, (8, 128), 1)
    first = jnp.zeros((8, 128), jnp.int32)
    last = jnp.where(lane < 8 + 3, VISUAL, 0)
    for f in range(1, FRAMES):
        below = jnp.sum((fid < f).astype(F32), axis=(0, 1), keepdims=True).astype(jnp.int32)
        first = jnp.where(lane == f, below, first)
        last = jnp.where(lane == f - 1, below, last)
    edge_ref[0] = first
    edge_ref[1] = last
    first, last = first[0:1], last[0:1]
    sub = lax.broadcasted_iota(jnp.int32, (8, 128), 0)
    bias = jnp.zeros((8, 128), F32)
    for b in range(TOK // QBLK):
        for f in range(FRAMES):
            here = (sub == f) & (lane // QBLK == b)
            bias = jnp.where(here, jnp.where(mask_ref[b, f] == 1, 0.0, -BIG), bias)
    top = jnp.concatenate([bias] * 4, axis=1)
    for h in range(4):
        cols = slice(h * DH, (h + 1) * DH)
        qt[:DH, cols] = q_ref[:, cols].T
        dt[:, cols] = d_ref[:, cols].T
    qt[DH:DH + 16, :] = jnp.concatenate([top, jnp.zeros((8, ROWS), F32)], axis=0).astype(BF16)
    qt[DH + 16:, :] = jnp.zeros((DH - 16, ROWS), BF16)
    own_ref[0, :DH] = qt[:DH, :]
    own_ref[1, :DH] = dt[...]
    own_ref[0, DH + 16:] = q_ref[...]
    own_ref[1, DH + 16:] = d_ref[...]
    m = jnp.full((1, ROWS), -3e38, F32)
    l = jnp.zeros((1, ROWS), F32)
    o = jnp.zeros((DH, ROWS), F32)
    for s in range(VISUAL // SUB):
        if s % (TILE // SUB) == 0:
            for load in loads[s // (TILE // SUB)]:
                load.wait()
        at = slice(s * SUB, (s + 1) * SUB)
        ka = jnp.concatenate([k_ref[at], marks(s * SUB, SUB, first, last)], axis=1)
        x = dot(ka, qt[...], NN) * C2
        m_new = jnp.maximum(m, jnp.max(x, axis=0, keepdims=True))
        shrink = jnp.exp2(m - m_new)
        p = jnp.exp2(x - m_new)
        l = l * shrink + jnp.sum(p, axis=0, keepdims=True)
        o = o * shrink + dot(v_ref[at], p.astype(BF16), TN)
        m = m_new
    own_ref[0, DH:DH + 16] = stat_rows(top, (m + jnp.log2(l)) * (-1.0 / C2))
    delta = jnp.sum(dt[...].astype(F32) * o, axis=0, keepdims=True) / l
    own_ref[1, DH:DH + 16] = stat_rows(jnp.zeros((8, ROWS), F32), -delta)
    for move in moves:
        move.wait()


def softmax_stats(queries, out_grad, keys, values, frame_ids, text_mask, key_weight, value_weight):
    vmem, far = pl.BlockSpec(memory_space=pltpu.VMEM), pl.BlockSpec(memory_space=pltpu.HBM)
    return pl.pallas_call(
        stats_kernel,
        in_specs=[pl.BlockSpec(memory_space=pltpu.SMEM), vmem, vmem, vmem, far, far, far, far],
        out_specs=[vmem, vmem, far],
        out_shape=[
            jax.ShapeDtypeStruct((2, DH + 16 + TOK, ROWS), BF16),
            jax.ShapeDtypeStruct((2, 8, 128), jnp.int32),
            jax.ShapeDtypeStruct((8, 2, 512, DH), BF16),
        ],
        scratch_shapes=[
            pltpu.VMEM((VISUAL, DH), BF16),
            pltpu.VMEM((VISUAL, DH), BF16),
            pltpu.VMEM((2 * DH, ROWS), BF16),
            pltpu.VMEM((DH, ROWS), BF16),
            pltpu.SemaphoreType.DMA((2, VISUAL // TILE)),
            pltpu.SemaphoreType.DMA((2,)),
        ],
        compiler_params=pltpu.CompilerParams(vmem_limit_bytes=VMEM_A << 20),
        cost_estimate=cost(10),
        name="softmax_stats",
    )(
        text_mask,
        frame_ids.reshape(VISUAL // 128, 128),
        queries,
        out_grad,
        keys,
        values,
        key_weight.reshape(8, 2, 512, DH),
        value_weight.reshape(8, 2, 512, DH),
    )


def grads_kernel(chunk, place, k_hbm, v_hbm, own_ref, other_ref, edge_ref, *rest):
    if chunk:
        sofar_ref, *rest = rest
    if chunk == CHUNKS - 1:
        keep_ref, send_ref, qown_ref, qother_ref, *rest = rest
    else:
        keep_ref, send_ref, qsum_ref, *rest = rest
    qt, dt, qr, dr, k_ref, v_ref, sems = rest
    y, z, af = place[0], place[1], place[2]
    order = (0, 3 - 2 * af, 1 + 2 * af, 2)
    loads = []
    for r in range(4):
        loads.append(
            [
                pltpu.make_async_copy(hbm.at[y ^ order[r], :, af, chunk], ref.at[r], sems.at[i, r])
                for i, (hbm, ref) in enumerate(((k_hbm, k_ref), (v_hbm, v_ref)))
            ]
        )
        for load in loads[r]:
            load.start()
    for side, ref in enumerate((own_ref, other_ref)):
        cols = slice(side * ROWS, (side + 1) * ROWS)
        qt[:DH + 16, cols] = ref[0, :DH + 16]
        dt[:DH + 16, cols] = ref[1, :DH + 16]
        for h in range(4):
            at = slice(side * ROWS + h * TOK, side * ROWS + (h + 1) * TOK)
            qr[at] = ref[0, DH + 16:, h * DH:(h + 1) * DH]
            dr[at] = ref[1, DH + 16:, h * DH:(h + 1) * DH]
    qt[DH + 16:] = jnp.zeros((DH - 16, 2 * ROWS), BF16)
    dt[DH + 16:] = jnp.zeros((DH - 16, 2 * ROWS), BF16)
    first, last = edge_ref[0, 0:1], edge_ref[1, 0:1]
    total = sofar_ref[...] if chunk else jnp.zeros((DH, 2 * ROWS), F32)
    for r in range(4):
        for load in loads[r]:
            load.wait()
        kl, vl, ml = [], [], []
        for s in range(4):
            yy, zz = y ^ order[r], z ^ order[s]
            kl.append(k_ref[r, zz])
            vl.append(v_ref[r, zz])
            ml.append(marks(yy * 2048 + zz * 512 + af * 256 + chunk * PIECE, PIECE, first, last))
        k = jnp.concatenate(kl, axis=0)
        mark = jnp.concatenate(ml, axis=0)
        p = jnp.exp2(dot(jnp.concatenate([k, mark], axis=1), qt[...], NN) * C2)
        dp = dot(jnp.concatenate([jnp.concatenate(vl, axis=0), mark], axis=1), dt[...], NN)
        ds = (p * dp).astype(BF16)
        out = (keep_ref, send_ref)[r // 2]
        out[r % 2, :, :DH] = (dot(ds, qr[...], NN) * SCALE).astype(BF16)
        out[r % 2, :, DH:] = dot(p.astype(BF16), dr[...], NN).astype(BF16)
        total = total + dot(k, ds, TN)
    if chunk == CHUNKS - 1:
        qown_ref[...] = total[:, :ROWS]
        qother_ref[...] = total[:, ROWS:].astype(BF16)
    else:
        qsum_ref[...] = total


def chunk_grads(chunk, place, keys, values, own, other, edge, sofar):
    view = (4, 4, 2, CHUNKS, PIECE, DH)
    vmem, far = pl.BlockSpec(memory_space=pltpu.VMEM), pl.BlockSpec(memory_space=pltpu.HBM)
    part = jax.ShapeDtypeStruct((2, 4 * PIECE, 2 * DH), BF16)
    more = [] if sofar is None else [sofar]
    if chunk == CHUNKS - 1:
        sums = [jax.ShapeDtypeStruct((DH, ROWS), F32), jax.ShapeDtypeStruct((DH, ROWS), BF16)]
    else:
        sums = [jax.ShapeDtypeStruct((DH, 2 * ROWS), F32)]
    outs = [part, part] + sums
    return pl.pallas_call(
        functools.partial(grads_kernel, chunk),
        in_specs=[pl.BlockSpec(memory_space=pltpu.SMEM), far, far] + [vmem] * (3 + len(more)),
        out_specs=[vmem] * len(outs),
        scratch_shapes=[
            pltpu.VMEM((2 * DH, 2 * ROWS), BF16),
            pltpu.VMEM((2 * DH, 2 * ROWS), BF16),
            pltpu.VMEM((2 * ROWS, DH), BF16),
            pltpu.VMEM((2 * ROWS, DH), BF16),
            pltpu.VMEM((4, 4, PIECE, DH), BF16),
            pltpu.VMEM((4, 4, PIECE, DH), BF16),
            pltpu.SemaphoreType.DMA((2, 4)),
        ],
        out_shape=outs,
        compiler_params=pltpu.CompilerParams(vmem_limit_bytes=VMEM_B << 20),
        cost_estimate=cost(14 / CHUNKS),
        name=f"chunk_grads_{chunk}",
    )(place, keys.reshape(view), values.reshape(view), own, other, edge, *more)


def query_kernel(mine_ref, got_ref, out_ref):
    total = (mine_ref[...] + got_ref[...].astype(F32)) * SCALE
    for h in range(4):
        out_ref[:, h * DH:(h + 1) * DH] = total[:, h * TOK:(h + 1) * TOK].T.astype(BF16)


def query_out(sums, got):
    return pl.pallas_call(
        query_kernel,
        in_specs=[pl.BlockSpec(memory_space=pltpu.VMEM)] * 2,
        out_specs=pl.BlockSpec(memory_space=pltpu.VMEM),
        out_shape=jax.ShapeDtypeStruct((TOK, ROWS), BF16),
        cost_estimate=cost(1),
        name="query_out",
    )(sums, got)


def visual_kernel(place, mine_ref, other_ref, *rest):
    *parts, out_ref = rest
    af, ha = place[2], place[3]
    first = jnp.where(af == 0, 1, 6)
    second = jnp.where(af == 0, 2, 1)
    third = jnp.where(af == 0, 6, 2)
    for ref, half in ((mine_ref, af), (other_ref, 1 - af)):
        total = jnp.zeros((256, 512), F32)
        for k in range(8):
            source = ha
            for bit, mask in ((1, first), (2, second), (4, third)):
                if k & bit:
                    source = source ^ mask
            g = jnp.concatenate([parts[c * 2 + k // 4][k % 4] for c in range(CHUNKS)], axis=0)
            w = jnp.concatenate([ref[source, 0], ref[source, 1]], axis=1)
            total = total + dot(g, w, NT)
        out_ref[:, pl.ds(pl.multiple_of(half * 512, 512), 512)] = total.astype(BF16)


def visual_out(place, mine, other, parts):
    vmem = pl.BlockSpec(memory_space=pltpu.VMEM)
    return pl.pallas_call(
        visual_kernel,
        in_specs=[pl.BlockSpec(memory_space=pltpu.SMEM)] + [vmem] * (2 + len(parts)),
        out_specs=vmem,
        out_shape=jax.ShapeDtypeStruct((256, 1024), BF16),
        compiler_params=pltpu.CompilerParams(vmem_limit_bytes=24 << 20),
        cost_estimate=cost(3),
        name="visual_out",
    )(place, mine, other, *parts)


def swap_cores(a):
    return lax.ppermute(a, "af", [(0, 1), (1, 0)])


def pair(a, axis, masks):
    count = {"pb": 16, "ha": 8}[axis]
    return lax.ppermute(a, (axis, "af"), [(2 * i + c, 2 * (i ^ masks[c]) + c) for i in range(count) for c in range(2)])


def plus(*terms):
    return functools.reduce(jnp.add, [t.astype(F32) for t in terms]).astype(BF16)


def reduce_chunk(keep, got):
    got2 = pair(plus(keep[1], got[1]), "pb", (12, 4))
    part = plus(keep[0], got[0], got2).reshape(4, PIECE, 2 * DH)
    got = pair(part[2:], "pb", (1, 3))
    got2 = pair(plus(part[1], got[1]), "pb", (3, 1))
    return plus(part[0], got[0], got2)[None]


def gather_chunk(g):
    g = jnp.concatenate([g, pair(g, "ha", (1, 6))], axis=0)
    g = jnp.concatenate([g, pair(g, "ha", (2, 1))], axis=0)
    return [g, pair(g, "ha", (6, 2))]


def on_device(queries, vis_keys, vis_values, out_grad, key_weight, value_weight, frame_ids, text_mask):
    pb, ha, af = lax.axis_index("pb"), lax.axis_index("ha"), lax.axis_index("af")
    place = jnp.stack([pb // 4, pb % 4, af, ha]).astype(jnp.int32)
    own, edge, weights = softmax_stats(
        queries, out_grad, vis_keys, vis_values, frame_ids, text_mask, key_weight, value_weight
    )
    other = swap_cores(own)
    qsum, parts = None, []
    kept, sent = [], []
    for chunk in range(CHUNKS):
        keep, send, *qsum = chunk_grads(
            chunk, place, vis_keys, vis_values, own, other, edge, qsum[0] if chunk else None
        )
        if chunk == 0:
            weights, keep = lax.optimization_barrier((weights, keep))
            weights = lax.all_to_all(weights, "ha", 0, 0, tiled=True)
            weights2 = swap_cores(weights)
        else:
            send, sent[-1] = lax.optimization_barrier((send, sent[-1]))
        kept.append(keep)
        sent.append(pair(send, "pb", (4, 12)))
    for chunk in range(CHUNKS):
        g = reduce_chunk(kept[chunk], sent[chunk])
        if chunk == CHUNKS - 1:
            query_grad = query_out(qsum[0], swap_cores(qsum[1]))
            g, query_grad = lax.optimization_barrier((g, query_grad))
        parts += gather_chunk(g)
    visual_grad = visual_out(place, weights, weights2, parts)
    return query_grad, visual_grad


def solution(mesh):
    in_specs = (
        P("pb", ("ha", "af")),
        P(None, "ha"),
        P(None, "ha"),
        P("pb", ("ha", "af")),
        P(None, "ha"),
        P(None, "ha"),
        P(),
        P("pb", None),
    )
    out_specs = (P("pb", ("ha", "af")), P(("pb", "af"), "ha"))
    return jax.shard_map(on_device, mesh=mesh, in_specs=in_specs, out_specs=out_specs, check_vma=False)
```

time: 103 us -> 157 us (1.52)
  Pallas kernels: 29.4 us -> 88 us
  starting transfers between devices: 46 us -> 34.8 us
  waiting for transfers between devices: 18.1 us -> 28.8 us
  local copies, waits for them, and re-layouts: 5.13 us -> 1.53 us
    pallas_call x5, Pallas kernels: 29.4 us -> 88 us  [the longest x1 66.6 us: softmax_stats(): pl.pallas_call(stats_kernel, in_specs=[pl.BlockSpec(memory_space=pltpu.SM...]
    ppermute x24 -> x14, starting transfers between devices: 39 us -> 28.6 us  [pair(): lax.ppermute(a, (axis, 'af'), [(2 * i + c, 2 * (i ^ masks[c]) + c) for i...]
    ppermute x24 -> x14, waiting for transfers between devices: 16.9 us -> 27.2 us  [pair(): lax.ppermute(a, (axis, 'af'), [(2 * i + c, 2 * (i ^ masks[c]) + c) for i...]
    squeeze x1 -> x0, local copies, waits for them, and re-layouts: 1.71 us -> none  [on_device(): lax.dynamic_index_in_dim(w.reshape(8, 2, 512, DH), af, 1, keepdims=False)]
  transfers between devices with their start and end apart: 30 -> 18, of which waited for: 12 -> 8; matrix products, arithmetic and copies ran while one was open for 2% -> 2% of each run, Pallas kernels for 25% -> 7%
where the time goes in v2:
time: 157 us
  Pallas kernels  88 us (56%)
  starting transfers between devices  34.8 us (22%)
  waiting for transfers between devices  28.8 us (18%)
  other arithmetic  2.69 us (2%)
    pallas_call x1, Pallas kernels, softmax_stats(): pl.pallas_call(stats_kernel, in_specs=[pl.BlockSpec(memory_space=pltpu.SM...  66.6 us
    ppermute x14, starting transfers between devices, pair(): lax.ppermute(a, (axis, 'af'), [(2 * i + c, 2 * (i ^ masks[c]) + c) for i...  28.6 us
    ppermute x14, waiting for transfers between devices, pair(): lax.ppermute(a, (axis, 'af'), [(2 * i + c, 2 * (i ^ masks[c]) + c) for i...  27.2 us
    pallas_call x2, Pallas kernels, chunk_grads(): pl.pallas_call(functools.partial(grads_kernel, chunk), in_specs=[pl.Block...  17.1 us
    all_to_all x1, starting transfers between devices, on_device(): weights = lax.all_to_all(weights, 'ha', 0, 0, tiled=True)  5.89 us
  transfers between devices with their start and end apart: 18, of which 8 were waited for; matrix products, arithmetic and copies ran while one was open for 2% of the time, Pallas kernels for 7%

profile of v2, /device:TPU:32, one launch (start us, length us, event | category | flops | bytes accessed | tf_op | source)
XLA Modules:
  0.0 156.6 jit_solution(16906465985404348739)
XLA Ops:
  0.6 66.6 %softmax_stats.1 = (bf16[2,272,512]{2,1,0:T(8,128)(2,1)}, s32[2,8,128]{2,1,0:T(8,128)}, bf16[8,2,512,128]{3,2,1,0:T(8,128)(2,1)}) custom-call(s32[4,8]{1,0:T(4,128)} %mask_ref.1, s32[64,128]{1,0:T(8,128)} %bitcast.54, bf16[128,512]{1,0:T(8,128)(2,1)} %q_ref.1, bf16[128,512]{1,0:T(8,128)(2,1)} %d_ref.1, bf16[8192,128]{1,0:T(8,128)(2,1)} %k_hbm.1, ...), custom_call_target="tpu_custom_call" | custom-call | flops 11000000512 | bytes 1048576 | tf_op jit(solution)/shard_map/softmax_stats/pallas_call | solution.py:130
  68.1 1.6 %collective-permute-done.other_ref = bf16[2,272,512]{2,1,0:T(8,128)(2,1)S(1)} collective-permute-done((bf16[2,272,512]{2,1,0:T(8,128)(2,1)}, bf16[2,272,512]{2,1,0:T(8,128)(2,1)S(1)}, u32[]{:S(2)}, u32[]{:S(2)}) %collective-permute-start) | collective-permute-done | bytes 557088 | tf_op jit(solution)/shard_map/ppermute | solution.py:299
  70.4 8.5 %chunk_grads_0.1 = (bf16[2,512,256]{2,1,0:T(8,128)(2,1)}, bf16[2,512,256]{2,1,0:T(8,128)(2,1)}, f32[128,1024]{1,0:T(8,128)}) custom-call(s32[4]{0:T(128)} %pad_add_fusion.place, bf16[4,4,2,2,128,128]{5,4,3,2,1,0:T(8,128)(2,1)} %bitcast.50, bf16[4,4,2,2,128,128]{5,4,3,2,1,0:T(8,128)(2,1)} %bitcast.52, bf16[2,272,512]{2,1,0:T(8,128)(2,1)} %get-tuple-element.18.own_ref, ...), custom_call_target="tpu_custom_call" | custom-call | flops 7699999744 | bytes 1048576 | tf_op jit(solution)/shard_map/chunk_grads_0/pallas_call | solution.py:229
  79.0 5.9 %all-to-all-start = ((bf16[8,2,512,128]{3,2,1,0:T(8,128)(2,1)}), bf16[8,2,512,128]{3,2,1,0:T(8,128)(2,1)S(1)}, u32[]{:S(2)}, u32[]{:S(2)}) async-start(bf16[8,2,512,128]{3,2,1,0:T(8,128)(2,1)} %get-tuple-element.30), calls=%async_computation | async-start | bytes 4194304 | tf_op jit(solution)/shard_map/all_to_all | solution.py:340
  84.9 1.6 %collective-permute-start.1 = (bf16[2,512,256]{2,1,0:T(8,128)(2,1)S(1)}, bf16[2,512,256]{2,1,0:T(8,128)(2,1)S(1)}, u32[]{:S(2)}, u32[]{:S(2)}) collective-permute-start(bf16[2,512,256]{2,1,0:T(8,128)(2,1)S(1)} %copy-done.4), channel_id=1, source_target_pairs={{0,64},{1,193},{16,80},{17,209},{32,96},{33,225},{48,112},{49,241}... | collective-permute-start | bytes 1572872 | tf_op jit(solution)/shard_map/ppermute | solution.py:304
  86.5 8.5 %chunk_grads_1.1 = (bf16[2,512,256]{2,1,0:T(8,128)(2,1)}, bf16[2,512,256]{2,1,0:T(8,128)(2,1)}, f32[128,512]{1,0:T(8,128)}, bf16[128,512]{1,0:T(8,128)(2,1)}) custom-call(s32[4]{0:T(128)} %pad_add_fusion.place, bf16[4,4,2,2,128,128]{5,4,3,2,1,0:T(8,128)(2,1)} %bitcast.51, bf16[4,4,2,2,128,128]{5,4,3,2,1,0:T(8,128)(2,1)} %bitcast.53, ...), custom_call_target="tpu_custom_call" | custom-call | flops 7699999744 | bytes 1048576 | tf_op jit(solution)/shard_map/chunk_grads_1/pallas_call | solution.py:229
  95.7 3.0 %collective-permute-start.8 = (bf16[512,256]{1,0:T(8,128)(2,1)S(1)}, bf16[512,256]{1,0:T(8,128)(2,1)S(1)}, u32[]{:S(2)}, u32[]{:S(2)}) collective-permute-start(bf16[512,256]{1,0:T(8,128)(2,1)S(1)} %fusion.3), channel_id=1, source_target_pairs={{0,192},{1,65},{16,208},{17,81},{32,224},{33,97},{48,240},{49,113}... | collective-permute-start | bytes 786440 | tf_op jit(solution)/shard_map/ppermute | solution.py:304
  98.7 7.4 %collective-permute-done.8 = bf16[512,256]{1,0:T(8,128)(2,1)S(1)} collective-permute-done((bf16[512,256]{1,0:T(8,128)(2,1)S(1)}, bf16[512,256]{1,0:T(8,128)(2,1)S(1)}, u32[]{:S(2)}, u32[]{:S(2)}) %collective-permute-start.8) | collective-permute-done | bytes 262176 | tf_op jit(solution)/shard_map/ppermute | solution.py:304
  106.9 3.3 %collective-permute-start.9 = (bf16[2,128,256]{2,1,0:T(8,128)(2,1)}, bf16[2,128,256]{2,1,0:T(8,128)(2,1)S(1)}, u32[]{:S(2)}, u32[]{:S(2)}) collective-permute-start(bf16[2,128,256]{2,1,0:T(8,128)(2,1)} %bitcast.17), channel_id=1, source_target_pairs={{0,16},{1,49},{16,0},{17,33},{32,48},{33,17},{48,32},{49,1},{64,80... | collective-permute-start | bytes 393224 | tf_op jit(solution)/shard_map/ppermute | solution.py:304
  111.0 3.1 %collective-permute-start.3 = (bf16[512,256]{1,0:T(8,128)(2,1)}, bf16[512,256]{1,0:T(8,128)(2,1)}, u32[]{:S(2)}, u32[]{:S(2)}) collective-permute-start(bf16[512,256]{1,0:T(8,128)(2,1)} %fusion.2), channel_id=1, source_target_pairs={{0,192},{1,65},{16,208},{17,81},{32,224},{33,97},{48,240},{49,113}... | collective-permute-start | bytes 786440 | tf_op jit(solution)/shard_map/ppermute | solution.py:304
  114.0 1.7 %query_out.1 = bf16[128,512]{1,0:T(8,128)(2,1)} custom-call(f32[128,512]{1,0:T(8,128)} %get-tuple-element.25.mine_ref, bf16[128,512]{1,0:T(8,128)(2,1)} %collective-permute-done.6.got_ref), custom_call_target="tpu_custom_call" | custom-call | flops 1100000000 | bytes 1048576 | tf_op jit(solution)/shard_map/query_out/pallas_call | solution.py:256
  115.8 3.7 %collective-permute-start.10 = (bf16[128,256]{1,0:T(8,128)(2,1)S(1)}, bf16[128,256]{1,0:T(8,128)(2,1)S(1)}, u32[]{:S(2)}, u32[]{:S(2)}) collective-permute-start(bf16[128,256]{1,0:T(8,128)(2,1)S(1)} %fusion.4), channel_id=1, source_target_pairs={{0,48},{1,17},{16,32},{17,1},{32,16},{33,49},{48,0},{49,33},{64,11... | collective-permute-start | bytes 196616 | tf_op jit(solution)/shard_map/ppermute | solution.py:304
  119.5 1.1 fusion.1
  120.6 1.6 %collective-permute-start.4 = (bf16[2,128,256]{2,1,0:T(8,128)(2,1)S(1)}, bf16[2,128,256]{2,1,0:T(8,128)(2,1)S(1)}, u32[]{:S(2)}, u32[]{:S(2)}) collective-permute-start(bf16[2,128,256]{2,1,0:T(8,128)(2,1)S(1)} %bitcast.47), channel_id=1, source_target_pairs={{0,16},{1,49},{16,0},{17,33},{32,48},{33,17},{48,32},{49,1},{64,80... | collective-permute-start | bytes 393224 | tf_op jit(solution)/shard_map/ppermute | solution.py:304
  122.6 4.7 %collective-permute-done.4 = bf16[2,128,256]{2,1,0:T(8,128)(2,1)S(1)} collective-permute-done((bf16[2,128,256]{2,1,0:T(8,128)(2,1)S(1)}, bf16[2,128,256]{2,1,0:T(8,128)(2,1)S(1)}, u32[]{:S(2)}, u32[]{:S(2)}) %collective-permute-start.4) | collective-permute-done | bytes 131104 | tf_op jit(solution)/shard_map/ppermute | solution.py:304
  127.3 3.2 %collective-permute-start.5 = (bf16[128,256]{1,0:T(8,128)(2,1)S(1)}, bf16[128,256]{1,0:T(8,128)(2,1)S(1)}, u32[]{:S(2)}, u32[]{:S(2)}) collective-permute-start(bf16[128,256]{1,0:T(8,128)(2,1)S(1)} %fusion.7), channel_id=1, source_target_pairs={{0,48},{1,17},{16,32},{17,1},{32,16},{33,49},{48,0},{49,33},{64,11... | collective-permute-start | bytes 196616 | tf_op jit(solution)/shard_map/ppermute | solution.py:304
  130.6 1.9 %collective-permute-start.12 = (bf16[2,128,256]{2,1,0:T(8,128)(2,1)S(1)}, bf16[2,128,256]{2,1,0:T(8,128)(2,1)S(1)}, u32[]{:S(2)}, u32[]{:S(2)}) collective-permute-start(bf16[2,128,256]{2,1,0:T(8,128)(2,1)S(1)} %pad_maximum_fusion.1), channel_id=1, source_target_pairs={{0,4},{1,3},{2,6},{3,1},{4,0},{5,7},{6,2},{7,5},{8,12},{9,11},{10,... | collective-permute-start | bytes 393224 | tf_op jit(solution)/shard_map/ppermute | solution.py:304
  132.5 1.3 collective-permute-done.5
  133.9 2.4 %collective-permute-done.12 = bf16[2,128,256]{2,1,0:T(8,128)(2,1)S(1)} collective-permute-done((bf16[2,128,256]{2,1,0:T(8,128)(2,1)S(1)}, bf16[2,128,256]{2,1,0:T(8,128)(2,1)S(1)}, u32[]{:S(2)}, u32[]{:S(2)}) %collective-permute-start.12) | collective-permute-done | bytes 131104 | tf_op jit(solution)/shard_map/ppermute | solution.py:304
  136.3 3.9 %collective-permute-start.13 = (bf16[4,128,256]{2,1,0:T(8,128)(2,1)S(1)}, bf16[4,128,256]{2,1,0:T(8,128)(2,1)S(1)}, u32[]{:S(2)}, u32[]{:S(2)}) collective-permute-start(bf16[4,128,256]{2,1,0:T(8,128)(2,1)S(1)} %pad_maximum_fusion.rest_0_), channel_id=1, source_target_pairs={{0,12},{1,5},{2,14},{3,7},{4,8},{5,1},{6,10},{7,3},{8,4},{9,13},{1... | collective-permute-start | bytes 786440 | tf_op jit(solution)/shard_map/ppermute | solution.py:304
  140.6 5.7 %collective-permute-done.15 = bf16[2,128,256]{2,1,0:T(8,128)(2,1)S(1)} collective-permute-done((bf16[2,128,256]{2,1,0:T(8,128)(2,1)S(1)}, bf16[2,128,256]{2,1,0:T(8,128)(2,1)S(1)}, u32[]{:S(2)}, u32[]{:S(2)}) %collective-permute-start.15) | collective-permute-done | bytes 131104 | tf_op jit(solution)/shard_map/ppermute | solution.py:304
  146.3 2.3 %collective-permute-start.16 = (bf16[4,128,256]{2,1,0:T(8,128)(2,1)S(1)}, bf16[4,128,256]{2,1,0:T(8,128)(2,1)S(1)}, u32[]{:S(2)}, u32[]{:S(2)}) collective-permute-start(bf16[4,128,256]{2,1,0:T(8,128)(2,1)S(1)} %constant_dynamic-update-slice_fusion.rest_2_), channel_id=1, source_target_pairs={{0,12},{1,5},{2,14},{3,7},{4,8},{5,1},{6,10},{7,3},{8,4},{9,13},{1... | collective-permute-start | bytes 786440 | tf_op jit(solution)/shard_map/ppermute | solution.py:304
  148.7 5.3 %collective-permute-done.16.rest_3_ = bf16[4,128,256]{2,1,0:T(8,128)(2,1)S(1)} collective-permute-done((bf16[4,128,256]{2,1,0:T(8,128)(2,1)S(1)}, bf16[4,128,256]{2,1,0:T(8,128)(2,1)S(1)}, u32[]{:S(2)}, u32[]{:S(2)}) %collective-permute-start.16) | collective-permute-done | bytes 262176 | tf_op jit(solution)/shard_map/ppermute | solution.py:304
  154.0 2.6 %visual_out.1 = bf16[256,1024]{1,0:T(8,128)(2,1)} custom-call(s32[4]{0:T(128)S(1)} %copy-done, bf16[8,2,512,128]{3,2,1,0:T(8,128)(2,1)S(1)} %all-to-all-done.mine_ref, bf16[8,2,512,128]{3,2,1,0:T(8,128)(2,1)S(1)} %collective-permute-done.7.other_ref, bf16[4,128,256]{2,1,0:T(8,128)(2,1)S(1)} %pad_maximum_fusion.rest_0_, ...), custom_call_target="tpu_custom_call" | custom-call | flops 3300000000 | bytes 1048576 | tf_op jit(solution)/shard_map/visual_out/pallas_call | solution.py:287
  (44 shorter events, 5.0 us)
Async XLA Ops:
  67.2 2.4 %collective-permute-start = (bf16[2,272,512]{2,1,0:T(8,128)(2,1)}, bf16[2,272,512]{2,1,0:T(8,128)(2,1)S(1)}, u32[]{:S(2)}, u32[]{:S(2)}) collective-permute-start(bf16[2,272,512]{2,1,0:T(8,128)(2,1)} %get-tuple-element.18.own_ref), channel_id=1, source_target_pairs={{0,1},{1,0},{2,3},{3,2},{4,5},{5,4},{6,7},{7,6},{8,9},{9,8},{10,11... | collective-permute-start | bytes 1671176 | tf_op jit(solution)/shard_map/ppermute | solution.py:299
  69.6 0.8 copy-start.3
  79.0 5.9 %copy-start.4 = (bf16[2,512,256]{2,1,0:T(8,128)(2,1)S(1)}, bf16[2,512,256]{2,1,0:T(8,128)(2,1)}, u32[]{:S(2)}) copy-start(bf16[2,512,256]{2,1,0:T(8,128)(2,1)} %get-tuple-element.23) | copy-start | bytes 1572868
  79.0 36.8 %all-to-all-start = ((bf16[8,2,512,128]{3,2,1,0:T(8,128)(2,1)}), bf16[8,2,512,128]{3,2,1,0:T(8,128)(2,1)S(1)}, u32[]{:S(2)}, u32[]{:S(2)}) async-start(bf16[8,2,512,128]{3,2,1,0:T(8,128)(2,1)} %get-tuple-element.30), calls=%async_computation | async-start | bytes 4194304 | tf_op jit(solution)/shard_map/all_to_all | solution.py:340
  84.9 10.2 %collective-permute-start.1 = (bf16[2,512,256]{2,1,0:T(8,128)(2,1)S(1)}, bf16[2,512,256]{2,1,0:T(8,128)(2,1)S(1)}, u32[]{:S(2)}, u32[]{:S(2)}) collective-permute-start(bf16[2,512,256]{2,1,0:T(8,128)(2,1)S(1)} %copy-done.4), channel_id=1, source_target_pairs={{0,64},{1,193},{16,80},{17,209},{32,96},{33,225},{48,112},{49,241}... | collective-permute-start | bytes 1572872 | tf_op jit(solution)/shard_map/ppermute | solution.py:304
  86.5 9.2 %copy-start.2 = (bf16[2,512,256]{2,1,0:T(8,128)(2,1)S(1)}, bf16[2,512,256]{2,1,0:T(8,128)(2,1)}, u32[]{:S(2)}) copy-start(bf16[2,512,256]{2,1,0:T(8,128)(2,1)} %get-tuple-element.31) | copy-start | bytes 1572868
  95.0 15.2 %copy-start.1 = (bf16[2,512,256]{2,1,0:T(8,128)(2,1)S(1)}, bf16[2,512,256]{2,1,0:T(8,128)(2,1)}, u32[]{:S(2)}) copy-start(bf16[2,512,256]{2,1,0:T(8,128)(2,1)} %get-tuple-element.21) | copy-start | bytes 1572868
  95.1 15.1 %collective-permute-start.2 = (bf16[2,512,256]{2,1,0:T(8,128)(2,1)}, bf16[2,512,256]{2,1,0:T(8,128)(2,1)S(1)}, u32[]{:S(2)}, u32[]{:S(2)}) collective-permute-start(bf16[2,512,256]{2,1,0:T(8,128)(2,1)} %get-tuple-element.24), channel_id=1, source_target_pairs={{0,64},{1,193},{16,80},{17,209},{32,96},{33,225},{48,112},{49,241}... | collective-permute-start | bytes 1572872 | tf_op jit(solution)/shard_map/ppermute | solution.py:304
  95.7 10.4 %collective-permute-start.8 = (bf16[512,256]{1,0:T(8,128)(2,1)S(1)}, bf16[512,256]{1,0:T(8,128)(2,1)S(1)}, u32[]{:S(2)}, u32[]{:S(2)}) collective-permute-start(bf16[512,256]{1,0:T(8,128)(2,1)S(1)} %fusion.3), channel_id=1, source_target_pairs={{0,192},{1,65},{16,208},{17,81},{32,224},{33,97},{48,240},{49,113}... | collective-permute-start | bytes 786440 | tf_op jit(solution)/shard_map/ppermute | solution.py:304
  98.7 15.3 %collective-permute-start.6 = (bf16[128,512]{1,0:T(8,128)(2,1)}, bf16[128,512]{1,0:T(8,128)(2,1)}, u32[]{:S(2)}, u32[]{:S(2)}) collective-permute-start(bf16[128,512]{1,0:T(8,128)(2,1)} %get-tuple-element.26), channel_id=1, source_target_pairs={{0,1},{1,0},{2,3},{3,2},{4,5},{5,4},{6,7},{7,6},{8,9},{9,8},{10,11... | collective-permute-start | bytes 393224 | tf_op jit(solution)/shard_map/ppermute | solution.py:299
  106.9 8.9 %collective-permute-start.9 = (bf16[2,128,256]{2,1,0:T(8,128)(2,1)}, bf16[2,128,256]{2,1,0:T(8,128)(2,1)S(1)}, u32[]{:S(2)}, u32[]{:S(2)}) collective-permute-start(bf16[2,128,256]{2,1,0:T(8,128)(2,1)} %bitcast.17), channel_id=1, source_target_pairs={{0,16},{1,49},{16,0},{17,33},{32,48},{33,17},{48,32},{49,1},{64,80... | collective-permute-start | bytes 393224 | tf_op jit(solution)/shard_map/ppermute | solution.py:304
  111.0 8.5 %collective-permute-start.3 = (bf16[512,256]{1,0:T(8,128)(2,1)}, bf16[512,256]{1,0:T(8,128)(2,1)}, u32[]{:S(2)}, u32[]{:S(2)}) collective-permute-start(bf16[512,256]{1,0:T(8,128)(2,1)} %fusion.2), channel_id=1, source_target_pairs={{0,192},{1,65},{16,208},{17,81},{32,224},{33,97},{48,240},{49,113}... | collective-permute-start | bytes 786440 | tf_op jit(solution)/shard_map/ppermute | solution.py:304
  115.8 38.2 %copy-start = (s32[4]{0:T(128)S(1)}, s32[4]{0:T(128)}, u32[]{:S(2)}) copy-start(s32[4]{0:T(128)} %pad_add_fusion.place) | copy-start | bytes 52
  115.8 38.2 %collective-permute-start.7 = (bf16[8,2,512,128]{3,2,1,0:T(8,128)(2,1)S(1)}, bf16[8,2,512,128]{3,2,1,0:T(8,128)(2,1)S(1)}, u32[]{:S(2)}, u32[]{:S(2)}) collective-permute-start(bf16[8,2,512,128]{3,2,1,0:T(8,128)(2,1)S(1)} %all-to-all-done.mine_ref), channel_id=1, source_target_pairs={{0,1},{1,0},{2,3},{3,2},{4,5},{5,4},{6,7},{7,6},{8,9},{9,8},{10,11... | collective-permute-start | bytes 6291464 | tf_op jit(solution)/shard_map/ppermute | solution.py:299
  115.8 6.7 %collective-permute-start.10 = (bf16[128,256]{1,0:T(8,128)(2,1)S(1)}, bf16[128,256]{1,0:T(8,128)(2,1)S(1)}, u32[]{:S(2)}, u32[]{:S(2)}) collective-permute-start(bf16[128,256]{1,0:T(8,128)(2,1)S(1)} %fusion.4), channel_id=1, source_target_pairs={{0,48},{1,17},{16,32},{17,1},{32,16},{33,49},{48,0},{49,33},{64,11... | collective-permute-start | bytes 196616 | tf_op jit(solution)/shard_map/ppermute | solution.py:304
  120.6 6.8 %collective-permute-start.4 = (bf16[2,128,256]{2,1,0:T(8,128)(2,1)S(1)}, bf16[2,128,256]{2,1,0:T(8,128)(2,1)S(1)}, u32[]{:S(2)}, u32[]{:S(2)}) collective-permute-start(bf16[2,128,256]{2,1,0:T(8,128)(2,1)S(1)} %bitcast.47), channel_id=1, source_target_pairs={{0,16},{1,49},{16,0},{17,33},{32,48},{33,17},{48,32},{49,1},{64,80... | collective-permute-start | bytes 393224 | tf_op jit(solution)/shard_map/ppermute | solution.py:304
  122.5 8.0 %collective-permute-start.11 = (bf16[1,128,256]{2,1,0:T(8,128)(2,1)S(1)}, bf16[1,128,256]{2,1,0:T(8,128)(2,1)S(1)}, u32[]{:S(2)}, u32[]{:S(2)}) collective-permute-start(bf16[1,128,256]{2,1,0:T(8,128)(2,1)S(1)} %fusion.11), channel_id=1, source_target_pairs={{0,2},{1,13},{2,0},{3,15},{4,6},{5,9},{6,4},{7,11},{8,10},{9,5},{1... | collective-permute-start | bytes 196616 | tf_op jit(solution)/shard_map/ppermute | solution.py:304
  127.3 6.5 %collective-permute-start.5 = (bf16[128,256]{1,0:T(8,128)(2,1)S(1)}, bf16[128,256]{1,0:T(8,128)(2,1)S(1)}, u32[]{:S(2)}, u32[]{:S(2)}) collective-permute-start(bf16[128,256]{1,0:T(8,128)(2,1)S(1)} %fusion.7), channel_id=1, source_target_pairs={{0,48},{1,17},{16,32},{17,1},{32,16},{33,49},{48,0},{49,33},{64,11... | collective-permute-start | bytes 196616 | tf_op jit(solution)/shard_map/ppermute | solution.py:304
  130.6 5.7 %collective-permute-start.12 = (bf16[2,128,256]{2,1,0:T(8,128)(2,1)S(1)}, bf16[2,128,256]{2,1,0:T(8,128)(2,1)S(1)}, u32[]{:S(2)}, u32[]{:S(2)}) collective-permute-start(bf16[2,128,256]{2,1,0:T(8,128)(2,1)S(1)} %pad_maximum_fusion.1), channel_id=1, source_target_pairs={{0,4},{1,3},{2,6},{3,1},{4,0},{5,7},{6,2},{7,5},{8,12},{9,11},{10,... | collective-permute-start | bytes 393224 | tf_op jit(solution)/shard_map/ppermute | solution.py:304
  133.8 6.4 %collective-permute-start.14 = (bf16[1,128,256]{2,1,0:T(8,128)(2,1)S(1)}, bf16[1,128,256]{2,1,0:T(8,128)(2,1)S(1)}, u32[]{:S(2)}, u32[]{:S(2)}) collective-permute-start(bf16[1,128,256]{2,1,0:T(8,128)(2,1)S(1)} %fusion.10), channel_id=1, source_target_pairs={{0,2},{1,13},{2,0},{3,15},{4,6},{5,9},{6,4},{7,11},{8,10},{9,5},{1... | collective-permute-start | bytes 196616 | tf_op jit(solution)/shard_map/ppermute | solution.py:304
  136.3 12.3 %collective-permute-start.13 = (bf16[4,128,256]{2,1,0:T(8,128)(2,1)S(1)}, bf16[4,128,256]{2,1,0:T(8,128)(2,1)S(1)}, u32[]{:S(2)}, u32[]{:S(2)}) collective-permute-start(bf16[4,128,256]{2,1,0:T(8,128)(2,1)S(1)} %pad_maximum_fusion.rest_0_), channel_id=1, source_target_pairs={{0,12},{1,5},{2,14},{3,7},{4,8},{5,1},{6,10},{7,3},{8,4},{9,13},{1... | collective-permute-start | bytes 786440 | tf_op jit(solution)/shard_map/ppermute | solution.py:304
  140.2 6.1 %collective-permute-start.15 = (bf16[2,128,256]{2,1,0:T(8,128)(2,1)S(1)}, bf16[2,128,256]{2,1,0:T(8,128)(2,1)S(1)}, u32[]{:S(2)}, u32[]{:S(2)}) collective-permute-start(bf16[2,128,256]{2,1,0:T(8,128)(2,1)S(1)} %pad_maximum_fusion.2), channel_id=1, source_target_pairs={{0,4},{1,3},{2,6},{3,1},{4,0},{5,7},{6,2},{7,5},{8,12},{9,11},{10,... | collective-permute-start | bytes 393224 | tf_op jit(solution)/shard_map/ppermute | solution.py:304
  146.3 7.7 %collective-permute-start.16 = (bf16[4,128,256]{2,1,0:T(8,128)(2,1)S(1)}, bf16[4,128,256]{2,1,0:T(8,128)(2,1)S(1)}, u32[]{:S(2)}, u32[]{:S(2)}) collective-permute-start(bf16[4,128,256]{2,1,0:T(8,128)(2,1)S(1)} %constant_dynamic-update-slice_fusion.rest_2_), channel_id=1, source_target_pairs={{0,12},{1,5},{2,14},{3,7},{4,8},{5,1},{6,10},{7,3},{8,4},{9,13},{1... | collective-permute-start | bytes 786440 | tf_op jit(solution)/shard_map/ppermute | solution.py:304

commit v3 on v0

v3 whole, which is shorter than its diff:
```python
import functools

import jax
import jax.numpy as jnp
from jax import lax
from jax.experimental import pallas as pl
from jax.experimental.pallas import tpu as pltpu
from jax.sharding import PartitionSpec as P

DH = 128
FRAMES = 8
QBLK = 32
TOK = 128
ROWS = 512
VISUAL = 8192
PIECE = 256
SUB = 512
HALF = VISUAL // 2
TILE = 1024
SCALE = DH**-0.5
C2 = SCALE * 1.4426950408889634
BIG = 2.0**100
VMEM_A = 60
VMEM_B = 58
F32 = jnp.float32
BF16 = jnp.bfloat16
NN = (((1,), (0,)), ((), ()))
NT = (((1,), (1,)), ((), ()))
TN = (((0,), (0,)), ((), ()))


def dot(a, b, dims):
    return lax.dot_general(a, b, dims, preferred_element_type=F32)


def cost(us):
    return pl.CostEstimate(flops=int(us * 1.1e9), transcendentals=0, bytes_accessed=1 << 20)


def marks(base, rows, first, last):
    at = base + lax.broadcasted_iota(jnp.int32, (rows, 128), 0)
    return jnp.where((at >= first) & (at < last), 1.0, 0.0).astype(BF16)


def pieces(x):
    hi = x.astype(BF16).astype(F32)
    rest = x - hi
    mid = rest.astype(BF16).astype(F32)
    return hi, mid, rest - mid


def stat_rows(top, x):
    hi, mid, low = pieces(x)
    row = lax.broadcasted_iota(jnp.int32, top.shape, 0)
    under = jnp.where(row == 0, hi, jnp.where(row == 1, mid, jnp.where(row == 2, low, 0.0)))
    return jnp.concatenate([top, under], axis=0).astype(BF16)


def stats_kernel(half, *refs):
    refs = list(refs)
    take = lambda n: [refs.pop(0) for _ in range(n)]
    if half == 0:
        mask_ref, fid_ref, qd_ref, k_hbm, v_hbm, kw_hbm, vw_hbm = take(7)
        qt, dt, state, edge_ref, w_hbm = take(5)
        k_ref, v_ref, sems, w_ref, wsem = refs
    else:
        k_hbm, v_hbm, qt, dt, state, edge_ref, stat_ref, k_ref, v_ref, sems = refs
    loads = []
    for t in range(HALF // TILE):
        at, far = pl.ds(t * TILE, TILE), pl.ds(half * HALF + t * TILE, TILE)
        loads.append(
            [
                pltpu.make_async_copy(k_hbm.at[far], k_ref.at[at], sems.at[0, t]),
                pltpu.make_async_copy(v_hbm.at[far], v_ref.at[at], sems.at[1, t]),
            ]
        )
        for load in loads[t]:
            load.start()
    if half == 0:
        af = lax.axis_index("af")
        moves = [pltpu.make_async_copy(w.at[:, af], w_ref.at[i], wsem.at[i]) for i, w in enumerate((kw_hbm, vw_hbm))]
        backs = [pltpu.make_async_copy(w_ref.at[i], w_hbm.at[:, i], wsem.at[2 + i]) for i in range(2)]
        for move in moves:
            move.start()
        fid = fid_ref[...]
        lane = lax.broadcasted_iota(jnp.int32, (8, 128), 1)
        first = jnp.zeros((8, 128), jnp.int32)
        last = jnp.where(lane < 8 + 3, VISUAL, 0)
        for f in range(1, FRAMES):
            below = jnp.sum((fid < f).astype(F32), axis=(0, 1), keepdims=True).astype(jnp.int32)
            first = jnp.where(lane == f, below, first)
            last = jnp.where(lane == f - 1, below, last)
        edge_ref[0] = first
        edge_ref[1] = last
        sub = lax.broadcasted_iota(jnp.int32, (8, 128), 0)
        bias = jnp.zeros((8, 128), F32)
        for b in range(TOK // QBLK):
            for f in range(FRAMES):
                here = (sub == f) & (lane // QBLK == b)
                bias = jnp.where(here, jnp.where(mask_ref[b, f] == 1, 0.0, -BIG), bias)
        top = jnp.concatenate([bias] * 4, axis=1)
        for h in range(4):
            cols = slice(h * DH, (h + 1) * DH)
            qt[:DH, cols] = qd_ref[0, :, cols].T
            dt[:, cols] = qd_ref[1, :, cols].T
        qt[DH:DH + 16, :] = jnp.concatenate([top, jnp.zeros((8, ROWS), F32)], axis=0).astype(BF16)
        qt[DH + 16:, :] = jnp.zeros((DH - 16, ROWS), BF16)
        m = jnp.full((1, ROWS), -3e38, F32)
        l = jnp.zeros((1, ROWS), F32)
        o = jnp.zeros((DH, ROWS), F32)
    else:
        m, l, o = state[DH:DH + 1], state[DH + 8:DH + 9], state[:DH]
    first, last = edge_ref[0, 0:1], edge_ref[1, 0:1]
    for s in range(HALF // SUB):
        if s % (TILE // SUB) == 0:
            for load in loads[s // (TILE // SUB)]:
                load.wait()
        if half == 0 and s == HALF // SUB // 2:
            for move, back in zip(moves, backs):
                move.wait()
                back.start()
        at = slice(s * SUB, (s + 1) * SUB)
        ka = jnp.concatenate([k_ref[at], marks(half * HALF + s * SUB, SUB, first, last)], axis=1)
        x = dot(ka, qt[...], NN) * C2
        m_new = jnp.maximum(m, jnp.max(x, axis=0, keepdims=True))
        shrink = jnp.exp2(m - m_new)
        p = jnp.exp2(x - m_new)
        l = l * shrink + jnp.sum(p, axis=0, keepdims=True)
        o = o * shrink + dot(v_ref[at], p.astype(BF16), TN)
        m = m_new
    if half == 0:
        state[:DH] = o
        state[DH:DH + 8] = jnp.broadcast_to(m, (8, ROWS))
        state[DH + 8:] = jnp.broadcast_to(l, (8, ROWS))
        for back in backs:
            back.wait()
    else:
        delta = jnp.sum(dt[...].astype(F32) * o, axis=0, keepdims=True) / l
        stat_ref[0] = stat_rows(qt[DH:DH + 8].astype(F32), (m + jnp.log2(l)) * (-1.0 / C2))
        stat_ref[1] = stat_rows(jnp.zeros((8, ROWS), F32), -delta)


def softmax_stats(half, *args):
    vmem, far = pl.BlockSpec(memory_space=pltpu.VMEM), pl.BlockSpec(memory_space=pltpu.HBM)
    scratch = [
        pltpu.VMEM((HALF, DH), BF16),
        pltpu.VMEM((HALF, DH), BF16),
        pltpu.SemaphoreType.DMA((2, HALF // TILE)),
    ]
    if half == 0:
        in_specs = [pl.BlockSpec(memory_space=pltpu.SMEM), vmem, vmem, far, far, far, far]
        out_specs = [vmem] * 4 + [far]
        outs = [
            jax.ShapeDtypeStruct((2 * DH, ROWS), BF16),
            jax.ShapeDtypeStruct((DH, ROWS), BF16),
            jax.ShapeDtypeStruct((DH + 16, ROWS), F32),
            jax.ShapeDtypeStruct((2, 8, 128), jnp.int32),
            jax.ShapeDtypeStruct((8, 2, 512, DH), BF16),
        ]
        scratch += [pltpu.VMEM((2, 8, 512, DH), BF16), pltpu.SemaphoreType.DMA((4,))]
    else:
        in_specs = [far, far] + [vmem] * 4
        out_specs = vmem
        outs = jax.ShapeDtypeStruct((2, 16, ROWS), BF16)
    return pl.pallas_call(
        functools.partial(stats_kernel, half),
        in_specs=in_specs,
        out_specs=out_specs,
        out_shape=outs,
        scratch_shapes=scratch,
        compiler_params=pltpu.CompilerParams(vmem_limit_bytes=VMEM_A << 20),
        cost_estimate=cost(6),
        name=f"softmax_stats_{half}",
    )(*args)


def grads_kernel(place, k_hbm, v_hbm, edge_ref, own_ref, other_ref, ostat_ref, pstat_ref, part_ref, qsum_ref, *scratch):
    ka, va, kt, ksum, vsum, k_ref, v_ref, sems = scratch
    y, z, af = place[0], place[1], place[2]
    order = (0, 3 - 2 * af, 1 + 2 * af, 2)
    loads = []
    for i, (hbm, ref) in enumerate(((k_hbm, k_ref), (v_hbm, v_ref))):
        loads.append(pltpu.make_async_copy(hbm.at[y, :, af], ref, sems.at[i]))
        loads[i].start()
    first, last = edge_ref[0, 0:1], edge_ref[1, 0:1]
    for s in range(4):
        at = slice(s * PIECE, (s + 1) * PIECE)
        mark = marks(y * 2048 + (z ^ order[s]) * 512 + af * 256, PIECE, first, last)
        ka[at, DH:] = mark
        va[at, DH:] = mark
    for load in loads:
        load.wait()
    for s in range(4):
        at = slice(s * PIECE, (s + 1) * PIECE)
        k = k_ref[z ^ order[s]]
        ka[at, :DH] = k
        va[at, :DH] = v_ref[z ^ order[s]]
        kt[:, at] = k.T
    for block in range(8):
        side, slot = block // 4, block % 4
        raw, stat = ((own_ref, ostat_ref), (other_ref, pstat_ref))[side]
        heads = [slice(h * DH, (h + 1) * DH) for h in range(4)]
        empty = jnp.zeros((DH - 16, ROWS), BF16)
        qt = jnp.concatenate(
            [jnp.concatenate([raw[slot, 0, :, h].T for h in heads], axis=1), stat[slot, 0], empty], axis=0
        )
        dt = jnp.concatenate(
            [jnp.concatenate([raw[slot, 1, :, h].T for h in heads], axis=1), stat[slot, 1], empty], axis=0
        )
        qr = jnp.concatenate([raw[slot, 0, :, h] for h in heads], axis=0)
        dr = jnp.concatenate([raw[slot, 1, :, h] for h in heads], axis=0)
        total = jnp.zeros((DH, ROWS), F32)
        for t in range(2):
            at = slice(t * 512, (t + 1) * 512)
            p = jnp.exp2(dot(ka[at], qt, NN) * C2)
            ds = (p * dot(va[at], dt, NN)).astype(BF16)
            kp = dot(ds, qr, NN)
            vp = dot(p.astype(BF16), dr, NN)
            if block:
                kp = kp + ksum[at]
                vp = vp + vsum[at]
            if block < 7:
                ksum[at] = kp
                vsum[at] = vp
            else:
                for s in range(2):
                    rows = slice(s * PIECE, (s + 1) * PIECE)
                    part_ref[2 * t + s, :, :DH] = (kp[rows] * SCALE).astype(BF16)
                    part_ref[2 * t + s, :, DH:] = vp[rows].astype(BF16)
            total = total + dot(kt[:, at], ds, NN)
        qsum_ref[side, slot] = total.astype(BF16)


def visual_token_grads(place, keys, values, edge, *rest):
    view = (4, 4, 2, PIECE, DH)
    vmem, far = pl.BlockSpec(memory_space=pltpu.VMEM), pl.BlockSpec(memory_space=pltpu.HBM)
    return pl.pallas_call(
        grads_kernel,
        in_specs=[pl.BlockSpec(memory_space=pltpu.SMEM), far, far] + [vmem] * 5,
        out_specs=[vmem, vmem],
        out_shape=[
            jax.ShapeDtypeStruct((4, PIECE, 2 * DH), BF16),
            jax.ShapeDtypeStruct((2, 4, DH, ROWS), BF16),
        ],
        scratch_shapes=[
            pltpu.VMEM((4 * PIECE, 2 * DH), BF16),
            pltpu.VMEM((4 * PIECE, 2 * DH), BF16),
            pltpu.VMEM((DH, 4 * PIECE), BF16),
            pltpu.VMEM((4 * PIECE, DH), F32),
            pltpu.VMEM((4 * PIECE, DH), F32),
            pltpu.VMEM((4, PIECE, DH), BF16),
            pltpu.VMEM((4, PIECE, DH), BF16),
            pltpu.SemaphoreType.DMA((2,)),
        ],
        compiler_params=pltpu.CompilerParams(vmem_limit_bytes=VMEM_B << 20),
        cost_estimate=cost(14),
        name="visual_token_grads",
    )(place, keys.reshape(view), values.reshape(view), edge, *rest)


def query_kernel(mine_ref, got_ref, out_ref):
    total = (mine_ref[...].astype(F32) + got_ref[...].astype(F32)) * SCALE
    for h in range(4):
        out_ref[:, h * DH:(h + 1) * DH] = total[:, h * TOK:(h + 1) * TOK].T.astype(BF16)


def query_out(mine, got):
    return pl.pallas_call(
        query_kernel,
        in_specs=[pl.BlockSpec(memory_space=pltpu.VMEM)] * 2,
        out_specs=pl.BlockSpec(memory_space=pltpu.VMEM),
        out_shape=jax.ShapeDtypeStruct((TOK, ROWS), BF16),
        cost_estimate=cost(1),
        name="query_out",
    )(mine, got)


def visual_kernel(place, mine_ref, other_ref, near_ref, far_ref, out_ref):
    af, ha = place[2], place[3]
    first = jnp.where(af == 0, 1, 6)
    second = jnp.where(af == 0, 2, 1)
    third = jnp.where(af == 0, 6, 2)
    for ref, half in ((mine_ref, af), (other_ref, 1 - af)):
        total = jnp.zeros((256, 512), F32)
        for k in range(8):
            source = ha
            for bit, mask in ((1, first), (2, second), (4, third)):
                if k & bit:
                    source = source ^ mask
            w = jnp.concatenate([ref[source, 0], ref[source, 1]], axis=1)
            total = total + dot((near_ref, far_ref)[k // 4][k % 4], w, NT)
        out_ref[:, pl.ds(pl.multiple_of(half * 512, 512), 512)] = total.astype(BF16)


def visual_out(place, mine, other, near, far):
    vmem = pl.BlockSpec(memory_space=pltpu.VMEM)
    return pl.pallas_call(
        visual_kernel,
        in_specs=[pl.BlockSpec(memory_space=pltpu.SMEM)] + [vmem] * 4,
        out_specs=vmem,
        out_shape=jax.ShapeDtypeStruct((256, 1024), BF16),
        compiler_params=pltpu.CompilerParams(vmem_limit_bytes=24 << 20),
        cost_estimate=cost(3),
        name="visual_out",
    )(place, mine, other, near, far)


def swap_cores(a):
    return lax.ppermute(a, "af", [(0, 1), (1, 0)])


def pair(a, axis, masks):
    count = {"pb": 16, "ha": 8}[axis]
    return lax.ppermute(a, (axis, "af"), [(2 * i + c, 2 * (i ^ masks[c]) + c) for i in range(count) for c in range(2)])


def plus(*terms):
    return functools.reduce(jnp.add, [t.astype(F32) for t in terms]).astype(BF16)


def gather_y(a):
    return [a, pair(a, "pb", (4, 12)), pair(a, "pb", (12, 4)), pair(a, "pb", (8, 8))]


def on_device(queries, vis_keys, vis_values, out_grad, key_weight, value_weight, frame_ids, text_mask):
    pb, ha, af = lax.axis_index("pb"), lax.axis_index("ha"), lax.axis_index("af")
    place = jnp.stack([pb // 4, pb % 4, af, ha]).astype(jnp.int32)
    tie = lax.optimization_barrier
    split = lambda w: w.reshape(8, 2, 512, DH)
    qd = jnp.stack([queries, out_grad])
    near, back = pair(qd, "pb", (4, 12)), pair(qd, "pb", (12, 4))
    qt, dt, state, edge, weights = softmax_stats(
        0, text_mask, frame_ids.reshape(VISUAL // 128, 128), qd, vis_keys, vis_values, split(key_weight), split(value_weight)
    )
    state, near, back = tie((state, near, back))
    across = pair(near, "pb", (12, 4))
    stat = softmax_stats(1, vis_keys, vis_values, qt, dt, state, edge)
    stat, across, weights = tie((stat, across, weights))
    stats = jnp.stack(gather_y(stat))
    own = jnp.stack([qd, near, back, across])
    other, stats2 = swap_cores(own), swap_cores(stats)
    weights = lax.all_to_all(weights, "ha", 0, 0, tiled=True)
    part, qsum = visual_token_grads(place, vis_keys, vis_values, edge, own, other, stats, stats2)

    got = pair(part[2:], "pb", (1, 3))
    qpart = plus(qsum[0], swap_cores(qsum[1]))
    got2 = pair(plus(part[1], got[1]), "pb", (3, 1))
    qgot = pair(qpart[2:], "pb", (12, 4))
    g = plus(part[0], got[0], got2)[None]
    qgot2 = pair(plus(qpart[1], qgot[1]), "pb", (4, 12))
    weights2 = swap_cores(weights)
    g = jnp.concatenate([g, pair(g, "ha", (1, 6))], axis=0)
    g = jnp.concatenate([g, pair(g, "ha", (2, 1))], axis=0)
    far = pair(g, "ha", (6, 2))
    query_grad = query_out(plus(qpart[0], qgot[0]), qgot2)
    far, query_grad = tie((far, query_grad))
    visual_grad = visual_out(place, weights, weights2, g, far)
    return query_grad, visual_grad


def solution(mesh):
    in_specs = (
        P("pb", ("ha", "af")),
        P(None, "ha"),
        P(None, "ha"),
        P("pb", ("ha", "af")),
        P(None, "ha"),
        P(None, "ha"),
        P(),
        P("pb", None),
    )
    out_specs = (P("pb", ("ha", "af")), P(("pb", "af"), "ha"))
    return jax.shard_map(on_device, mesh=mesh, in_specs=in_specs, out_specs=out_specs, check_vma=False)
```

time: 512 us -> 105 us (0.21)
  the two profiles are of different devices: /device:TPU:32 before, /device:TPU:96 now
where the time goes in v3:
time: 105 us; the launch traced here: 104 us
  Pallas kernels  34.6 us (33%)
  starting transfers between devices  29.9 us (28%)
  waiting for transfers between devices  28.3 us (27%)
  other arithmetic  5.7 us (5%)
  local copies, waits for them, and re-layouts  4.87 us (5%)
    ppermute x13, waiting for transfers between devices, pair(): lax.ppermute(a, (axis, 'af'), [(2 * i + c, 2 * (i ^ masks[c]) + c) for i...  27.9 us
    ppermute x13, starting transfers between devices, pair(): lax.ppermute(a, (axis, 'af'), [(2 * i + c, 2 * (i ^ masks[c]) + c) for i...  19.7 us
    pallas_call x2, Pallas kernels, softmax_stats(): pl.pallas_call(functools.partial(stats_kernel, half), in_specs=in_specs,...  15.4 us
    pallas_call x1, Pallas kernels, visual_token_grads(): pl.pallas_call(grads_kernel, in_specs=[pl.BlockSpec(memory_space=pltpu.SM...  13.8 us
    all_to_all x1, starting transfers between devices, on_device(): weights = lax.all_to_all(weights, 'ha', 0, 0, tiled=True)  5.77 us
    ppermute x4, starting transfers between devices, swap_cores(): return lax.ppermute(a, 'af', [(0, 1), (1, 0)])  4.49 us
    pallas_call x1, Pallas kernels, visual_out(): pl.pallas_call(visual_kernel, in_specs=[pl.BlockSpec(memory_space=pltpu.S...  3.68 us
    another operation x2, other arithmetic, on_device(): own = jnp.stack([qd, near, back, across])  2.25 us
  transfers between devices with their start and end apart: 18, of which 9 were waited for; matrix products, arithmetic and copies ran while one was open for 7% of the time, Pallas kernels for 30%

profile of v3, /device:TPU:96, one launch (start us, length us, event | category | flops | bytes accessed | tf_op | source)
XLA Modules:
  0.0 104.2 jit_solution(566908567934575509)
XLA Ops:
  1.6 1.7 %collective-permute-start = (bf16[2,128,512]{2,1,0:T(8,128)(2,1)S(1)}, bf16[2,128,512]{2,1,0:T(8,128)(2,1)S(1)}, u32[]{:S(2)}, u32[]{:S(2)}) collective-permute-start(bf16[2,128,512]{2,1,0:T(8,128)(2,1)S(1)} %get-tuple-element.35.refs_2_), channel_id=1, source_target_pairs={{0,64},{1,193},{16,80},{17,209},{32,96},{33,225},{48,112},{49,241}... | collective-permute-start | bytes 786440 | tf_op jit(solution)/shard_map/ppermute | solution.py:314
  3.3 2.2 %collective-permute-start.1 = (bf16[2,128,512]{2,1,0:T(8,128)(2,1)S(1)}, bf16[2,128,512]{2,1,0:T(8,128)(2,1)S(1)}, u32[]{:S(2)}, u32[]{:S(2)}) collective-permute-start(bf16[2,128,512]{2,1,0:T(8,128)(2,1)S(1)} %get-tuple-element.35.refs_2_), channel_id=1, source_target_pairs={{0,192},{1,65},{16,208},{17,81},{32,224},{33,97},{48,240},{49,113}... | collective-permute-start | bytes 786440 | tf_op jit(solution)/shard_map/ppermute | solution.py:314
  5.5 7.7 %softmax_stats_0.1 = (bf16[256,512]{1,0:T(8,128)(2,1)}, bf16[128,512]{1,0:T(8,128)(2,1)}, f32[144,512]{1,0:T(8,128)}, s32[2,8,128]{2,1,0:T(8,128)}, bf16[8,2,512,128]{3,2,1,0:T(8,128)(2,1)}) custom-call(s32[4,8]{1,0:T(4,128)} %refs_0_.2, s32[64,128]{1,0:T(8,128)} %bitcast.52, bf16[2,128,512]{2,1,0:T(8,128)(2,1)} %copy-done.3, bf16[8192,128]{1,0:T(8,128)(2,1)} %refs_0_.3, ...), custom_call_target="tpu_custom_call" | custom-call | flops 6600000000 | bytes 1048576 | tf_op jit(solution)/shard_map/softmax_stats_0/pallas_call | solution.py:165
  13.2 1.1 %collective-permute-start.2 = (bf16[2,128,512]{2,1,0:T(8,128)(2,1)S(1)}, bf16[2,128,512]{2,1,0:T(8,128)(2,1)S(1)}, u32[]{:S(2)}, u32[]{:S(2)}) collective-permute-start(bf16[2,128,512]{2,1,0:T(8,128)(2,1)S(1)} %collective-permute-done), channel_id=1, source_target_pairs={{0,192},{1,65},{16,208},{17,81},{32,224},{33,97},{48,240},{49,113}... | collective-permute-start | bytes 786440 | tf_op jit(solution)/shard_map/ppermute | solution.py:314
  14.4 7.7 %softmax_stats_1.1 = bf16[2,16,512]{2,1,0:T(8,128)(2,1)} custom-call(bf16[8192,128]{1,0:T(8,128)(2,1)} %refs_0_.3, bf16[8192,128]{1,0:T(8,128)(2,1)} %refs_1_.1, bf16[256,512]{1,0:T(8,128)(2,1)} %get-tuple-element.21.refs_2_, bf16[128,512]{1,0:T(8,128)(2,1)} %get-tuple-element.22.refs_3_, f32[144,512]{1,0:T(8,128)} %get-tuple-element.23.refs_4_, ...), custom_call_target="tpu_custom_call" | custom-call | flops 6600000000 | bytes 1048576 | tf_op jit(solution)/shard_map/softmax_stats_1/pallas_call | solution.py:165
  22.8 5.8 %all-to-all-start = ((bf16[8,2,512,128]{3,2,1,0:T(8,128)(2,1)}), bf16[8,2,512,128]{3,2,1,0:T(8,128)(2,1)S(1)}, u32[]{:S(2)}, u32[]{:S(2)}) async-start(bf16[8,2,512,128]{3,2,1,0:T(8,128)(2,1)} %get-tuple-element.30), calls=%async_computation | async-start | bytes 4194304 | tf_op jit(solution)/shard_map/all_to_all | solution.py:342
  28.6 1.2 %pad_maximum_fusion.own_ref = bf16[4,2,128,512]{3,2,1,0:T(8,128)(2,1)S(1)} fusion(bf16[1,2,128,512]{3,2,1,0:T(8,128)(2,1)} %bitcast.41, bf16[1,2,128,512]{3,2,1,0:T(8,128)(2,1)} %bitcast.40, bf16[1,2,128,512]{3,2,1,0:T(8,128)(2,1)} %bitcast.39, bf16[1,2,128,512]{3,2,1,0:T(8,128)(2,1)S(1)} %get-tuple-element.34), kind=kLoop, calls=%fused_computation | loop fusion | flops 1572864 | bytes 2097152 | tf_op jit(solution)/shard_map/stack | solution.py:340
  30.0 1.8 %collective-permute-start.6 = (bf16[2,16,512]{2,1,0:T(8,128)(2,1)S(1)}, bf16[2,16,512]{2,1,0:T(8,128)(2,1)S(1)}, u32[]{:S(2)}, u32[]{:S(2)}) collective-permute-start(bf16[2,16,512]{2,1,0:T(8,128)(2,1)S(1)} %copy-done.8), channel_id=1, source_target_pairs={{0,128},{1,129},{16,144},{17,145},{32,160},{33,161},{48,176},{49,1... | collective-permute-start | bytes 98312 | tf_op jit(solution)/shard_map/ppermute | solution.py:314
  33.6 2.1 %collective-permute-done.6 = bf16[2,16,512]{2,1,0:T(8,128)(2,1)S(1)} collective-permute-done((bf16[2,16,512]{2,1,0:T(8,128)(2,1)S(1)}, bf16[2,16,512]{2,1,0:T(8,128)(2,1)S(1)}, u32[]{:S(2)}, u32[]{:S(2)}) %collective-permute-start.6) | collective-permute-done | bytes 32800 | tf_op jit(solution)/shard_map/ppermute | solution.py:314
  35.7 1.3 %collective-permute-done.5 = bf16[2,16,512]{2,1,0:T(8,128)(2,1)S(1)} collective-permute-done((bf16[2,16,512]{2,1,0:T(8,128)(2,1)S(1)}, bf16[2,16,512]{2,1,0:T(8,128)(2,1)S(1)}, u32[]{:S(2)}, u32[]{:S(2)}) %collective-permute-start.5) | collective-permute-done | bytes 32800 | tf_op jit(solution)/shard_map/ppermute | solution.py:314
  39.1 13.8 %visual_token_grads.1 = (bf16[4,256,256]{2,1,0:T(8,128)(2,1)}, bf16[2,4,128,512]{3,2,1,0:T(8,128)(2,1)}) custom-call(s32[4]{0:T(128)} %pad_add_fusion.place, bf16[4,4,2,256,128]{4,3,2,1,0:T(8,128)(2,1)} %bitcast.50, bf16[4,4,2,256,128]{4,3,2,1,0:T(8,128)(2,1)} %bitcast.51, s32[2,8,128]{2,1,0:T(8,128)} %get-tuple-element.17.refs_5_.edge_ref, ...), custom_call_target="tpu_custom_call" | custom-call | flops 15399999488 | bytes 1048576 | tf_op jit(solution)/shard_map/visual_token_grads/pallas_call | solution.py:237
  52.9 1.8 %slice.37 = bf16[2,256,256]{2,1,0:T(8,128)(2,1)} slice(bf16[4,256,256]{2,1,0:T(8,128)(2,1)} %get-tuple-element.27), slice={[2:4], [0:256], [0:256]} | slice | bytes 524288 | tf_op jit(solution)/shard_map/slice | solution.py:345
  54.7 3.6 %collective-permute-start.16 = (bf16[8,2,512,128]{3,2,1,0:T(8,128)(2,1)S(1)}, bf16[8,2,512,128]{3,2,1,0:T(8,128)(2,1)}, u32[]{:S(2)}, u32[]{:S(2)}) collective-permute-start(bf16[8,2,512,128]{3,2,1,0:T(8,128)(2,1)S(1)} %all-to-all-done.mine_ref), channel_id=1, source_target_pairs={{0,1},{1,0},{2,3},{3,2},{4,5},{5,4},{6,7},{7,6},{8,9},{9,8},{10,11... | collective-permute-start | bytes 6291464 | tf_op jit(solution)/shard_map/ppermute | solution.py:309
  58.3 6.2 %collective-permute-done.8 = bf16[2,256,256]{2,1,0:T(8,128)(2,1)S(1)} collective-permute-done((bf16[2,256,256]{2,1,0:T(8,128)(2,1)}, bf16[2,256,256]{2,1,0:T(8,128)(2,1)S(1)}, u32[]{:S(2)}, u32[]{:S(2)}) %collective-permute-start.8) | collective-permute-done | bytes 262176 | tf_op jit(solution)/shard_map/ppermute | solution.py:314
  65.4 3.7 %collective-permute-start.9 = (bf16[256,256]{1,0:T(8,128)(2,1)S(1)}, bf16[256,256]{1,0:T(8,128)(2,1)S(1)}, u32[]{:S(2)}, u32[]{:S(2)}) collective-permute-start(bf16[256,256]{1,0:T(8,128)(2,1)S(1)} %fusion.2), channel_id=1, source_target_pairs={{0,48},{1,17},{16,32},{17,1},{32,16},{33,49},{48,0},{49,33},{64,11... | collective-permute-start | bytes 393224 | tf_op jit(solution)/shard_map/ppermute | solution.py:314
  70.6 3.5 %collective-permute-done.9 = bf16[256,256]{1,0:T(8,128)(2,1)S(1)} collective-permute-done((bf16[256,256]{1,0:T(8,128)(2,1)S(1)}, bf16[256,256]{1,0:T(8,128)(2,1)S(1)}, u32[]{:S(2)}, u32[]{:S(2)}) %collective-permute-start.9) | collective-permute-done | bytes 131104 | tf_op jit(solution)/shard_map/ppermute | solution.py:314
  75.1 5.0 %collective-permute-done.10 = bf16[1,256,256]{2,1,0:T(8,128)(2,1)S(1)} collective-permute-done((bf16[1,256,256]{2,1,0:T(8,128)(2,1)S(1)}, bf16[1,256,256]{2,1,0:T(8,128)(2,1)S(1)}, u32[]{:S(2)}, u32[]{:S(2)}) %collective-permute-start.10) | collective-permute-done | bytes 131104 | tf_op jit(solution)/shard_map/ppermute | solution.py:314
  80.1 3.1 %collective-permute-start.11 = (bf16[2,256,256]{2,1,0:T(8,128)(2,1)S(1)}, bf16[2,256,256]{2,1,0:T(8,128)(2,1)S(1)}, u32[]{:S(2)}, u32[]{:S(2)}) collective-permute-start(bf16[2,256,256]{2,1,0:T(8,128)(2,1)S(1)} %pad_maximum_fusion.3), channel_id=1, source_target_pairs={{0,4},{1,3},{2,6},{3,1},{4,0},{5,7},{6,2},{7,5},{8,12},{9,11},{10,... | collective-permute-start | bytes 786440 | tf_op jit(solution)/shard_map/ppermute | solution.py:314
  83.4 2.0 %collective-permute-start.14 = (bf16[2,128,512]{2,1,0:T(8,128)(2,1)S(1)}, bf16[2,128,512]{2,1,0:T(8,128)(2,1)S(1)}, u32[]{:S(2)}, u32[]{:S(2)}) collective-permute-start(bf16[2,128,512]{2,1,0:T(8,128)(2,1)S(1)} %slice.51), channel_id=1, source_target_pairs={{0,192},{1,65},{16,208},{17,81},{32,224},{33,97},{48,240},{49,113}... | collective-permute-start | bytes 786440 | tf_op jit(solution)/shard_map/ppermute | solution.py:314
  85.4 3.9 %collective-permute-done.11 = bf16[2,256,256]{2,1,0:T(8,128)(2,1)S(1)} collective-permute-done((bf16[2,256,256]{2,1,0:T(8,128)(2,1)S(1)}, bf16[2,256,256]{2,1,0:T(8,128)(2,1)S(1)}, u32[]{:S(2)}, u32[]{:S(2)}) %collective-permute-start.11) | collective-permute-done | bytes 262176 | tf_op jit(solution)/shard_map/ppermute | solution.py:314
  89.4 2.2 %collective-permute-start.12 = (bf16[4,256,256]{2,1,0:T(8,128)(2,1)S(1)}, bf16[4,256,256]{2,1,0:T(8,128)(2,1)S(1)}, u32[]{:S(2)}, u32[]{:S(2)}) collective-permute-start(bf16[4,256,256]{2,1,0:T(8,128)(2,1)S(1)} %pad_maximum_fusion.1.near_ref), channel_id=1, source_target_pairs={{0,12},{1,5},{2,14},{3,7},{4,8},{5,1},{6,10},{7,3},{8,4},{9,13},{1... | collective-permute-start | bytes 1572872 | tf_op jit(solution)/shard_map/ppermute | solution.py:314
  93.2 5.0 %collective-permute-done.15.got_ref = bf16[128,512]{1,0:T(8,128)(2,1)S(1)} collective-permute-done((bf16[128,512]{1,0:T(8,128)(2,1)S(1)}, bf16[128,512]{1,0:T(8,128)(2,1)S(1)}, u32[]{:S(2)}, u32[]{:S(2)}) %collective-permute-start.15) | collective-permute-done | bytes 131104 | tf_op jit(solution)/shard_map/ppermute | solution.py:314
  98.8 1.7 %query_out.1 = bf16[128,512]{1,0:T(8,128)(2,1)} custom-call(bf16[128,512]{1,0:T(8,128)(2,1)} %get-tuple-element.33.mine_ref, bf16[128,512]{1,0:T(8,128)(2,1)} %copy-done.10), custom_call_target="tpu_custom_call" | custom-call | flops 1100000000 | bytes 1048576 | tf_op jit(solution)/shard_map/query_out/pallas_call | solution.py:268
  100.5 3.7 %visual_out.1 = bf16[256,1024]{1,0:T(8,128)(2,1)} custom-call(s32[4]{0:T(128)S(1)} %copy-done, bf16[8,2,512,128]{3,2,1,0:T(8,128)(2,1)S(1)} %all-to-all-done.mine_ref, bf16[8,2,512,128]{3,2,1,0:T(8,128)(2,1)} %collective-permute-done.16.other_ref, bf16[4,256,256]{2,1,0:T(8,128)(2,1)S(1)} %pad_maximum_fusion.1.near_ref, ...), custom_call_target="tpu_custom_call" | custom-call | flops 3300000000 | bytes 1048576 | tf_op jit(solution)/shard_map/visual_out/pallas_call | solution.py:297
  (52 shorter events, 11.7 us)
Async XLA Ops:
  1.6 3.9 %copy-start.3 = (bf16[2,128,512]{2,1,0:T(8,128)(2,1)}, bf16[2,128,512]{2,1,0:T(8,128)(2,1)S(1)}, u32[]{:S(2)}) copy-start(bf16[2,128,512]{2,1,0:T(8,128)(2,1)S(1)} %get-tuple-element.35.refs_2_) | copy-start | bytes 786436
  1.6 11.5 %collective-permute-start = (bf16[2,128,512]{2,1,0:T(8,128)(2,1)S(1)}, bf16[2,128,512]{2,1,0:T(8,128)(2,1)S(1)}, u32[]{:S(2)}, u32[]{:S(2)}) collective-permute-start(bf16[2,128,512]{2,1,0:T(8,128)(2,1)S(1)} %get-tuple-element.35.refs_2_), channel_id=1, source_target_pairs={{0,64},{1,193},{16,80},{17,209},{32,96},{33,225},{48,112},{49,241}... | collective-permute-start | bytes 786440 | tf_op jit(solution)/shard_map/ppermute | solution.py:314
  3.3 9.9 %collective-permute-start.1 = (bf16[2,128,512]{2,1,0:T(8,128)(2,1)S(1)}, bf16[2,128,512]{2,1,0:T(8,128)(2,1)S(1)}, u32[]{:S(2)}, u32[]{:S(2)}) collective-permute-start(bf16[2,128,512]{2,1,0:T(8,128)(2,1)S(1)} %get-tuple-element.35.refs_2_), channel_id=1, source_target_pairs={{0,192},{1,65},{16,208},{17,81},{32,224},{33,97},{48,240},{49,113}... | collective-permute-start | bytes 786440 | tf_op jit(solution)/shard_map/ppermute | solution.py:314
  13.2 8.9 %copy-start.4 = (bf16[2,128,512]{2,1,0:T(8,128)(2,1)}, bf16[2,128,512]{2,1,0:T(8,128)(2,1)S(1)}, u32[]{:S(2)}) copy-start(bf16[2,128,512]{2,1,0:T(8,128)(2,1)S(1)} %collective-permute-done) | copy-start | bytes 786436
  13.2 8.9 %copy-start.5 = (bf16[2,128,512]{2,1,0:T(8,128)(2,1)}, bf16[2,128,512]{2,1,0:T(8,128)(2,1)S(1)}, u32[]{:S(2)}) copy-start(bf16[2,128,512]{2,1,0:T(8,128)(2,1)S(1)} %collective-permute-done.1) | copy-start | bytes 786436
  13.2 8.9 %collective-permute-start.2 = (bf16[2,128,512]{2,1,0:T(8,128)(2,1)S(1)}, bf16[2,128,512]{2,1,0:T(8,128)(2,1)S(1)}, u32[]{:S(2)}, u32[]{:S(2)}) collective-permute-start(bf16[2,128,512]{2,1,0:T(8,128)(2,1)S(1)} %collective-permute-done), channel_id=1, source_target_pairs={{0,192},{1,65},{16,208},{17,81},{32,224},{33,97},{48,240},{49,113}... | collective-permute-start | bytes 786440 | tf_op jit(solution)/shard_map/ppermute | solution.py:314
  22.8 31.8 %all-to-all-start = ((bf16[8,2,512,128]{3,2,1,0:T(8,128)(2,1)}), bf16[8,2,512,128]{3,2,1,0:T(8,128)(2,1)S(1)}, u32[]{:S(2)}, u32[]{:S(2)}) async-start(bf16[8,2,512,128]{3,2,1,0:T(8,128)(2,1)} %get-tuple-element.30), calls=%async_computation | async-start | bytes 4194304 | tf_op jit(solution)/shard_map/all_to_all | solution.py:342
  29.9 8.6 %copy-start.2 = (bf16[4,2,128,512]{3,2,1,0:T(8,128)(2,1)}, bf16[4,2,128,512]{3,2,1,0:T(8,128)(2,1)S(1)}, u32[]{:S(2)}) copy-start(bf16[4,2,128,512]{3,2,1,0:T(8,128)(2,1)S(1)} %pad_maximum_fusion.own_ref) | copy-start | bytes 3145732
  29.9 8.6 %collective-permute-start.3 = (bf16[4,2,128,512]{3,2,1,0:T(8,128)(2,1)S(1)}, bf16[4,2,128,512]{3,2,1,0:T(8,128)(2,1)}, u32[]{:S(2)}, u32[]{:S(2)}) collective-permute-start(bf16[4,2,128,512]{3,2,1,0:T(8,128)(2,1)S(1)} %pad_maximum_fusion.own_ref), channel_id=1, source_target_pairs={{0,1},{1,0},{2,3},{3,2},{4,5},{5,4},{6,7},{7,6},{8,9},{9,8},{10,11... | collective-permute-start | bytes 3145736 | tf_op jit(solution)/shard_map/ppermute | solution.py:309
  30.0 5.7 %collective-permute-start.6 = (bf16[2,16,512]{2,1,0:T(8,128)(2,1)S(1)}, bf16[2,16,512]{2,1,0:T(8,128)(2,1)S(1)}, u32[]{:S(2)}, u32[]{:S(2)}) collective-permute-start(bf16[2,16,512]{2,1,0:T(8,128)(2,1)S(1)} %copy-done.8), channel_id=1, source_target_pairs={{0,128},{1,129},{16,144},{17,145},{32,160},{33,161},{48,176},{49,1... | collective-permute-start | bytes 98312 | tf_op jit(solution)/shard_map/ppermute | solution.py:314
  31.8 5.2 %collective-permute-start.5 = (bf16[2,16,512]{2,1,0:T(8,128)(2,1)S(1)}, bf16[2,16,512]{2,1,0:T(8,128)(2,1)S(1)}, u32[]{:S(2)}, u32[]{:S(2)}) collective-permute-start(bf16[2,16,512]{2,1,0:T(8,128)(2,1)S(1)} %copy-done.8), channel_id=1, source_target_pairs={{0,192},{1,65},{16,208},{17,81},{32,224},{33,97},{48,240},{49,113}... | collective-permute-start | bytes 98312 | tf_op jit(solution)/shard_map/ppermute | solution.py:314
  32.5 4.5 %collective-permute-start.4 = (bf16[2,16,512]{2,1,0:T(8,128)(2,1)S(1)}, bf16[2,16,512]{2,1,0:T(8,128)(2,1)S(1)}, u32[]{:S(2)}, u32[]{:S(2)}) collective-permute-start(bf16[2,16,512]{2,1,0:T(8,128)(2,1)S(1)} %copy-done.8), channel_id=1, source_target_pairs={{0,64},{1,193},{16,80},{17,209},{32,96},{33,225},{48,112},{49,241}... | collective-permute-start | bytes 98312 | tf_op jit(solution)/shard_map/ppermute | solution.py:314
  37.0 1.4 %collective-permute-start.7 = (bf16[4,2,16,512]{3,2,1,0:T(8,128)(2,1)S(1)}, bf16[4,2,16,512]{3,2,1,0:T(8,128)(2,1)S(1)}, u32[]{:S(2)}, u32[]{:S(2)}) collective-permute-start(bf16[4,2,16,512]{3,2,1,0:T(8,128)(2,1)S(1)} %pad_maximum_fusion.4.ostat_ref), channel_id=1, source_target_pairs={{0,1},{1,0},{2,3},{3,2},{4,5},{5,4},{6,7},{7,6},{8,9},{9,8},{10,11... | collective-permute-start | bytes 393224 | tf_op jit(solution)/shard_map/ppermute | solution.py:309
  52.9 30.3 %copy-start.1 = (bf16[2,4,128,512]{3,2,1,0:T(8,128)(2,1)S(1)}, bf16[2,4,128,512]{3,2,1,0:T(8,128)(2,1)}, u32[]{:S(2)}) copy-start(bf16[2,4,128,512]{3,2,1,0:T(8,128)(2,1)} %get-tuple-element.28) | copy-start | bytes 3145732
  54.7 9.8 %collective-permute-start.8 = (bf16[2,256,256]{2,1,0:T(8,128)(2,1)}, bf16[2,256,256]{2,1,0:T(8,128)(2,1)S(1)}, u32[]{:S(2)}, u32[]{:S(2)}) collective-permute-start(bf16[2,256,256]{2,1,0:T(8,128)(2,1)} %slice.37), channel_id=1, source_target_pairs={{0,16},{1,49},{16,0},{17,33},{32,48},{33,17},{48,32},{49,1},{64,80... | collective-permute-start | bytes 786440 | tf_op jit(solution)/shard_map/ppermute | solution.py:314
  54.7 45.8 %collective-permute-start.16 = (bf16[8,2,512,128]{3,2,1,0:T(8,128)(2,1)S(1)}, bf16[8,2,512,128]{3,2,1,0:T(8,128)(2,1)}, u32[]{:S(2)}, u32[]{:S(2)}) collective-permute-start(bf16[8,2,512,128]{3,2,1,0:T(8,128)(2,1)S(1)} %all-to-all-done.mine_ref), channel_id=1, source_target_pairs={{0,1},{1,0},{2,3},{3,2},{4,5},{5,4},{6,7},{7,6},{8,9},{9,8},{10,11... | collective-permute-start | bytes 6291464 | tf_op jit(solution)/shard_map/ppermute | solution.py:309
  65.4 8.6 %collective-permute-start.9 = (bf16[256,256]{1,0:T(8,128)(2,1)S(1)}, bf16[256,256]{1,0:T(8,128)(2,1)S(1)}, u32[]{:S(2)}, u32[]{:S(2)}) collective-permute-start(bf16[256,256]{1,0:T(8,128)(2,1)S(1)} %fusion.2), channel_id=1, source_target_pairs={{0,48},{1,17},{16,32},{17,1},{32,16},{33,49},{48,0},{49,33},{64,11... | collective-permute-start | bytes 393224 | tf_op jit(solution)/shard_map/ppermute | solution.py:314
  70.2 13.0 %collective-permute-start.13 = (bf16[4,128,512]{2,1,0:T(8,128)(2,1)S(1)}, bf16[4,128,512]{2,1,0:T(8,128)(2,1)S(1)}, u32[]{:S(2)}, u32[]{:S(2)}) collective-permute-start(bf16[4,128,512]{2,1,0:T(8,128)(2,1)S(1)} %slice_bitcast_fusion), channel_id=1, source_target_pairs={{0,1},{1,0},{2,3},{3,2},{4,5},{5,4},{6,7},{7,6},{8,9},{9,8},{10,11... | collective-permute-start | bytes 1572872 | tf_op jit(solution)/shard_map/ppermute | solution.py:309
  75.0 5.1 %collective-permute-start.10 = (bf16[1,256,256]{2,1,0:T(8,128)(2,1)S(1)}, bf16[1,256,256]{2,1,0:T(8,128)(2,1)S(1)}, u32[]{:S(2)}, u32[]{:S(2)}) collective-permute-start(bf16[1,256,256]{2,1,0:T(8,128)(2,1)S(1)} %fusion.5), channel_id=1, source_target_pairs={{0,2},{1,13},{2,0},{3,15},{4,6},{5,9},{6,4},{7,11},{8,10},{9,5},{1... | collective-permute-start | bytes 393224 | tf_op jit(solution)/shard_map/ppermute | solution.py:314
  80.1 9.2 %collective-permute-start.11 = (bf16[2,256,256]{2,1,0:T(8,128)(2,1)S(1)}, bf16[2,256,256]{2,1,0:T(8,128)(2,1)S(1)}, u32[]{:S(2)}, u32[]{:S(2)}) collective-permute-start(bf16[2,256,256]{2,1,0:T(8,128)(2,1)S(1)} %pad_maximum_fusion.3), channel_id=1, source_target_pairs={{0,4},{1,3},{2,6},{3,1},{4,0},{5,7},{6,2},{7,5},{8,12},{9,11},{10,... | collective-permute-start | bytes 786440 | tf_op jit(solution)/shard_map/ppermute | solution.py:314
  83.4 9.1 %collective-permute-start.14 = (bf16[2,128,512]{2,1,0:T(8,128)(2,1)S(1)}, bf16[2,128,512]{2,1,0:T(8,128)(2,1)S(1)}, u32[]{:S(2)}, u32[]{:S(2)}) collective-permute-start(bf16[2,128,512]{2,1,0:T(8,128)(2,1)S(1)} %slice.51), channel_id=1, source_target_pairs={{0,192},{1,65},{16,208},{17,81},{32,224},{33,97},{48,240},{49,113}... | collective-permute-start | bytes 786440 | tf_op jit(solution)/shard_map/ppermute | solution.py:314
  89.4 11.2 %collective-permute-start.12 = (bf16[4,256,256]{2,1,0:T(8,128)(2,1)S(1)}, bf16[4,256,256]{2,1,0:T(8,128)(2,1)S(1)}, u32[]{:S(2)}, u32[]{:S(2)}) collective-permute-start(bf16[4,256,256]{2,1,0:T(8,128)(2,1)S(1)} %pad_maximum_fusion.1.near_ref), channel_id=1, source_target_pairs={{0,12},{1,5},{2,14},{3,7},{4,8},{5,1},{6,10},{7,3},{8,4},{9,13},{1... | collective-permute-start | bytes 1572872 | tf_op jit(solution)/shard_map/ppermute | solution.py:314
  93.2 7.4 %copy-start = (s32[4]{0:T(128)S(1)}, s32[4]{0:T(128)}, u32[]{:S(2)}) copy-start(s32[4]{0:T(128)} %pad_add_fusion.place) | copy-start | bytes 52
  93.2 5.0 %collective-permute-start.15 = (bf16[128,512]{1,0:T(8,128)(2,1)S(1)}, bf16[128,512]{1,0:T(8,128)(2,1)S(1)}, u32[]{:S(2)}, u32[]{:S(2)}) collective-permute-start(bf16[128,512]{1,0:T(8,128)(2,1)S(1)} %get-tuple-element.32), channel_id=1, source_target_pairs={{0,64},{1,193},{16,80},{17,209},{32,96},{33,225},{48,112},{49,241}... | collective-permute-start | bytes 393224 | tf_op jit(solution)/shard_map/ppermute | solution.py:314
  (5 other events, 4.8 us)

commit v4 on v2

v4 whole, which is shorter than its diff:
```python
import functools

import jax
import jax.numpy as jnp
from jax import lax
from jax.experimental import pallas as pl
from jax.experimental.pallas import tpu as pltpu
from jax.sharding import PartitionSpec as P

DH = 128
FRAMES = 8
QBLK = 32
TOK = 128
ROWS = 512
VISUAL = 8192
PIECE = 256
SUB = 512
TILE = 1024
SCALE = DH**-0.5
C2 = SCALE * 1.4426950408889634
BIG = 2.0**100
VMEM_A = 55
VMEM_B = 24
F32 = jnp.float32
BF16 = jnp.bfloat16
NN = (((1,), (0,)), ((), ()))
NT = (((1,), (1,)), ((), ()))
TN = (((0,), (0,)), ((), ()))


def dot(a, b, dims):
    return lax.dot_general(a, b, dims, preferred_element_type=F32)


def cost(us):
    return pl.CostEstimate(flops=int(us * 1.1e9), transcendentals=0, bytes_accessed=1 << 20)


def marks(base, rows, first, last):
    at = base + lax.broadcasted_iota(jnp.int32, (rows, 128), 0)
    return jnp.where((at >= first) & (at < last), 1.0, 0.0).astype(BF16)


def pieces(x):
    hi = x.astype(BF16).astype(F32)
    rest = x - hi
    mid = rest.astype(BF16).astype(F32)
    return hi, mid, rest - mid


def stat_rows(top, x):
    hi, mid, low = pieces(x)
    row = lax.broadcasted_iota(jnp.int32, top.shape, 0)
    under = jnp.where(row == 0, hi, jnp.where(row == 1, mid, jnp.where(row == 2, low, 0.0)))
    return jnp.concatenate([top, under], axis=0).astype(BF16)


def stats_kernel(
    mask_hbm, fid_hbm, q_hbm, d_hbm, k_hbm, v_hbm, kw_hbm, vw_hbm, own_ref, ka_ref, va_ref, kt_ref, w_hbm,
    mask_ref, fid_ref, k_ref, v_ref, w_ref, qt, dt, sems, wsem, small,
):
    af = lax.axis_index("af")
    smalls = [
        pltpu.make_async_copy(src, dst, small.at[i])
        for i, (src, dst) in enumerate(
            (
                (q_hbm, own_ref.at[0, pl.ds(0, TOK)]),
                (d_hbm, own_ref.at[1, pl.ds(0, TOK)]),
                (fid_hbm, fid_ref),
                (mask_hbm, mask_ref),
            )
        )
    ]
    for copy in smalls:
        copy.start()
    loads = []
    for t in range(VISUAL // TILE):
        at = pl.ds(t * TILE, TILE)
        loads.append(
            [
                pltpu.make_async_copy(k_hbm.at[at], k_ref.at[at], sems.at[0, t]),
                pltpu.make_async_copy(v_hbm.at[at], v_ref.at[at], sems.at[1, t]),
            ]
        )
        for load in loads[t]:
            load.start()
    moves = [pltpu.make_async_copy(w.at[:, af], w_ref.at[i], wsem.at[i]) for i, w in enumerate((kw_hbm, vw_hbm))]
    backs = [pltpu.make_async_copy(w_ref.at[i], w_hbm.at[:, i], wsem.at[2 + i]) for i in range(2)]
    for move in moves:
        move.start()
    for copy in smalls:
        copy.wait()
    fid = fid_ref[...]
    lane = lax.broadcasted_iota(jnp.int32, (8, 128), 1)
    first = jnp.zeros((8, 128), jnp.int32)
    last = jnp.where(lane < 8 + 3, VISUAL, 0)
    for f in range(1, FRAMES):
        below = jnp.sum((fid < f).astype(F32), axis=(0, 1), keepdims=True).astype(jnp.int32)
        first = jnp.where(lane == f, below, first)
        last = jnp.where(lane == f - 1, below, last)
    first, last = first[0:1], last[0:1]
    sub = lax.broadcasted_iota(jnp.int32, (8, 128), 0)
    bias = jnp.zeros((8, 128), F32)
    for b in range(TOK // QBLK):
        for f in range(FRAMES):
            here = (sub == f) & (lane // QBLK == b)
            bias = jnp.where(here, jnp.where(mask_ref[b, f] == 1, 0.0, -BIG), bias)
    top = jnp.concatenate([bias] * 4, axis=1)
    for h in range(4):
        cols = slice(h * DH, (h + 1) * DH)
        qt[:DH, cols] = own_ref[0, :TOK, cols].T
        dt[:, cols] = own_ref[1, :TOK, cols].T
    qt[DH:DH + 16, :] = jnp.concatenate([top, jnp.zeros((8, ROWS), F32)], axis=0).astype(BF16)
    qt[DH + 16:, :] = jnp.zeros((DH - 16, ROWS), BF16)
    m = jnp.full((1, ROWS), -3e38, F32)
    l = jnp.zeros((1, ROWS), F32)
    o = jnp.zeros((DH, ROWS), F32)

    def scores(s):
        if s % (TILE // SUB) == 0:
            for load in loads[s // (TILE // SUB)]:
                load.wait()
        ka = jnp.concatenate([k_ref[s * SUB:(s + 1) * SUB], marks(s * SUB, SUB, first, last)], axis=1)
        return dot(ka, qt[...], NN) * C2

    later = scores(0)
    for s in range(VISUAL // SUB):
        x = later
        m_new = jnp.maximum(m, jnp.max(x, axis=0, keepdims=True))
        if s + 1 < VISUAL // SUB:
            later = scores(s + 1)
        if s == VISUAL // SUB // 2:
            for move, back in zip(moves, backs):
                move.wait()
                back.start()
        shrink = jnp.exp2(m - m_new)
        p = jnp.exp2(x - m_new)
        l = l * shrink + jnp.sum(p, axis=0, keepdims=True)
        o = o * shrink + dot(v_ref[s * SUB:(s + 1) * SUB], p.astype(BF16), TN)
        m = m_new
    y, z = lax.axis_index("pb") // 4, lax.axis_index("pb") % 4
    order = (0, 3 - 2 * af, 1 + 2 * af, 2)
    for s in range(4):
        at = slice(s * PIECE, (s + 1) * PIECE)
        base = y * 2048 + (z ^ order[s]) * 512 + af * 256
        far = pl.ds(pl.multiple_of(base, 256), PIECE)
        mark = marks(base, PIECE, first, last)
        ka_ref[at] = jnp.concatenate([k_ref[far], mark], axis=1)
        va_ref[at] = jnp.concatenate([v_ref[far], mark], axis=1)
        kt_ref[:, at] = k_ref[far].T
    delta = jnp.sum(dt[...].astype(F32) * o, axis=0, keepdims=True) / l
    own_ref[0, TOK:] = stat_rows(top, (m + jnp.log2(l)) * (-1.0 / C2))
    own_ref[1, TOK:] = stat_rows(jnp.zeros((8, ROWS), F32), -delta)
    for back in backs:
        back.wait()


def softmax_stats(*args):
    vmem, far = pl.BlockSpec(memory_space=pltpu.VMEM), pl.BlockSpec(memory_space=pltpu.HBM)
    return pl.pallas_call(
        stats_kernel,
        in_specs=[far] * 8,
        out_specs=[vmem] * 4 + [far],
        out_shape=[
            jax.ShapeDtypeStruct((2, TOK + 16, ROWS), BF16),
            jax.ShapeDtypeStruct((4 * PIECE, 2 * DH), BF16),
            jax.ShapeDtypeStruct((4 * PIECE, 2 * DH), BF16),
            jax.ShapeDtypeStruct((DH, 4 * PIECE), BF16),
            jax.ShapeDtypeStruct((8, 2, 512, DH), BF16),
        ],
        scratch_shapes=[
            pltpu.SMEM((TOK // QBLK, FRAMES), jnp.int32),
            pltpu.VMEM((VISUAL // 128, 128), jnp.int32),
            pltpu.VMEM((VISUAL, DH), BF16),
            pltpu.VMEM((VISUAL, DH), BF16),
            pltpu.VMEM((2, 8, 512, DH), BF16),
            pltpu.VMEM((2 * DH, ROWS), BF16),
            pltpu.VMEM((DH, ROWS), BF16),
            pltpu.SemaphoreType.DMA((2, VISUAL // TILE)),
            pltpu.SemaphoreType.DMA((4,)),
            pltpu.SemaphoreType.DMA((4,)),
        ],
        compiler_params=pltpu.CompilerParams(vmem_limit_bytes=VMEM_A << 20),
        cost_estimate=cost(10),
        name="softmax_stats",
    )(*args)


def grads_kernel(pairs, first_call, last_call, *refs):
    refs = list(refs)
    take = lambda n: [refs.pop(0) for _ in range(n)]
    ka, va, kt = take(3)
    if not first_call:
        ksum_in, vsum_in, *q_in = take(4)
    bundles = take(2 * pairs)
    q_refs = take(2)
    if last_call:
        keep_ref, send_ref = take(2)
    else:
        ksum_out, vsum_out = take(2)
    ksum, vsum = refs
    if not first_call:
        for q_ref, q_old in zip(q_refs, q_in):
            q_ref[0] = q_old[0]
    for block, ref in enumerate(bundles):
        heads = [slice(h * DH, (h + 1) * DH) for h in range(4)]
        empty = jnp.zeros((DH - 16, ROWS), BF16)
        qt, dt = [
            jnp.concatenate(
                [jnp.concatenate([ref[i, :TOK, h].T for h in heads], axis=1), ref[i, TOK:], empty], axis=0
            )
            for i in range(2)
        ]
        qr, dr = [jnp.concatenate([ref[i, :TOK, h] for h in heads], axis=0) for i in range(2)]
        total = jnp.zeros((DH, ROWS), F32)
        final = block == len(bundles) - 1
        for t in range(2):
            at = slice(t * 512, (t + 1) * 512)
            p = jnp.exp2(dot(ka[at], qt, NN) * C2)
            ds = (p * dot(va[at], dt, NN)).astype(BF16)
            kp = dot(ds, qr, NN)
            vp = dot(p.astype(BF16), dr, NN)
            if block or not first_call:
                kp = kp + (ksum if block else ksum_in)[at]
                vp = vp + (vsum if block else vsum_in)[at]
            if not final:
                ksum[at] = kp
                vsum[at] = vp
            elif not last_call:
                ksum_out[at] = kp
                vsum_out[at] = vp
            else:
                for s in range(2):
                    rows = slice(s * PIECE, (s + 1) * PIECE)
                    out = (keep_ref, send_ref)[t]
                    out[s, :, :DH] = (kp[rows] * SCALE).astype(BF16)
                    out[s, :, DH:] = vp[rows].astype(BF16)
            total = total + dot(kt[:, at], ds, NN)
        q_refs[block % 2][block // 2 + (not first_call)] = total.astype(BF16)


def visual_token_grads(name, before, bundles, first_call=False, last_call=False):
    vmem = pl.BlockSpec(memory_space=pltpu.VMEM)
    shape = jax.ShapeDtypeStruct
    outs = [shape((len(bundles) // 2 + (not first_call), DH, ROWS), BF16)] * 2
    outs += [shape((2, PIECE, 2 * DH), BF16)] * 2 if last_call else [shape((4 * PIECE, DH), F32)] * 2
    scratch = [pltpu.VMEM((4 * PIECE, DH), F32)] * 2
    return pl.pallas_call(
        functools.partial(grads_kernel, len(bundles) // 2, first_call, last_call),
        in_specs=[vmem] * (len(before) + len(bundles)),
        out_specs=[vmem] * len(outs),
        out_shape=outs,
        scratch_shapes=scratch,
        compiler_params=pltpu.CompilerParams(vmem_limit_bytes=VMEM_B << 20),
        cost_estimate=cost(1.6 * len(bundles)),
        name=f"visual_token_grads_{name}",
    )(*before, *bundles)


def query_kernel(mine_ref, got_ref, out_ref):
    total = (mine_ref[...].astype(F32) + got_ref[...].astype(F32)) * SCALE
    for h in range(4):
        out_ref[:, h * DH:(h + 1) * DH] = total[:, h * TOK:(h + 1) * TOK].T.astype(BF16)


def query_out(mine, got):
    return pl.pallas_call(
        query_kernel,
        in_specs=[pl.BlockSpec(memory_space=pltpu.VMEM)] * 2,
        out_specs=pl.BlockSpec(memory_space=pltpu.VMEM),
        out_shape=jax.ShapeDtypeStruct((TOK, ROWS), BF16),
        compiler_params=pltpu.CompilerParams(vmem_limit_bytes=4 << 20),
        cost_estimate=cost(1),
        name="query_out",
    )(mine, got)


def visual_kernel(late, place, mine_ref, other_ref, g_ref, *rest):
    sofar_ref, out_ref = rest if late else (None, rest[0])
    af, ha = place[2], place[3]
    first = jnp.where(af == 0, 1, 6)
    second = jnp.where(af == 0, 2, 1)
    third = jnp.where(af == 0, 6, 2)
    totals = []
    for side, ref in enumerate((mine_ref, other_ref)):
        total = sofar_ref[side] if late else jnp.zeros((256, 512), F32)
        for k in range(4):
            source = ha ^ third if late else ha
            for bit, mask in ((1, first), (2, second)):
                if k & bit:
                    source = source ^ mask
            w = jnp.concatenate([ref[source, 0], ref[source, 1]], axis=1)
            total = total + dot(g_ref[k], w, NT)
        if late:
            totals.append(total)
        else:
            out_ref[side] = total
    for core in range(2) if late else ():

        @pl.when(af == core)
        def _():
            for side in range(2):
                at = (side ^ core) * 512
                out_ref[:, at:at + 512] = totals[side].astype(BF16)


def visual_out(place, mine, other, g, *sofar):
    vmem = pl.BlockSpec(memory_space=pltpu.VMEM)
    early = jax.ShapeDtypeStruct((2, 256, 512), F32)
    return pl.pallas_call(
        functools.partial(visual_kernel, bool(sofar)),
        in_specs=[pl.BlockSpec(memory_space=pltpu.SMEM)] + [vmem] * (3 + len(sofar)),
        out_specs=vmem,
        out_shape=jax.ShapeDtypeStruct((256, 1024), BF16) if sofar else early,
        compiler_params=pltpu.CompilerParams(vmem_limit_bytes=24 << 20),
        cost_estimate=cost(2),
        name="visual_late" if sofar else "visual_early",
    )(place, mine, other, g, *sofar)


def swap_cores(a):
    return lax.ppermute(a, "af", [(0, 1), (1, 0)])


def pair(a, axis, masks):
    count = {"pb": 16, "ha": 8}[axis]
    return lax.ppermute(a, (axis, "af"), [(2 * i + c, 2 * (i ^ masks[c]) + c) for i in range(count) for c in range(2)])


def plus(*terms):
    return functools.reduce(jnp.add, [t.astype(F32) for t in terms]).astype(BF16)


def on_device(queries, vis_keys, vis_values, out_grad, key_weight, value_weight, frame_ids, text_mask):
    pb, ha, af = lax.axis_index("pb"), lax.axis_index("ha"), lax.axis_index("af")
    place = jnp.stack([pb // 4, pb % 4, af, ha]).astype(jnp.int32)
    tie = lax.optimization_barrier
    split = lambda w: w.reshape(8, 2, 512, DH)
    own, ka, va, kt, weights = softmax_stats(
        text_mask, frame_ids.reshape(VISUAL // 128, 128), queries, out_grad, vis_keys, vis_values, split(key_weight), split(value_weight)
    )
    weights = lax.all_to_all(weights, "ha", 0, 0, tiled=True)
    near, back = pair(own, "pb", (4, 12)), pair(own, "pb", (12, 4))
    own2 = swap_cores(own)
    early = visual_token_grads("early", [ka, va, kt], [own, own2], first_call=True)
    near, back, early = tie((near, back, early))
    across = pair(near, "pb", (12, 4))
    near2, back2 = swap_cores(near), swap_cores(back)
    qown, qother, keep, send = visual_token_grads(
        "late",
        [ka, va, kt, *early[2:], *early[:2]],
        [near, near2, back, back2, across, swap_cores(across)],
        last_call=True,
    )

    got = pair(send, "pb", (1, 3))
    qpart = plus(qown, swap_cores(qother))
    qgot = pair(qpart[2:], "pb", (12, 4))
    got, qpart = tie((got, qpart))
    got2 = pair(plus(keep[1], got[1]), "pb", (3, 1))
    g = plus(keep[0], got[0], got2)[None]
    weights2 = swap_cores(weights)
    g = jnp.concatenate([g, pair(g, "ha", (1, 6))], axis=0)
    g, qgot = tie((g, qgot))
    qgot2 = pair(plus(qpart[1], qgot[1]), "pb", (4, 12))
    g = jnp.concatenate([g, pair(g, "ha", (2, 1))], axis=0)
    g, qgot2 = tie((g, qgot2))
    far = pair(g, "ha", (6, 2))
    early = visual_out(place, weights, weights2, g)
    query_grad = query_out(plus(qpart[0], qgot[0]), qgot2)
    far, query_grad, early = tie((far, query_grad, early))
    visual_grad = visual_out(place, weights, weights2, far, early)
    return query_grad, visual_grad


def solution(mesh):
    in_specs = (
        P("pb", ("ha", "af")),
        P(None, "ha"),
        P(None, "ha"),
        P("pb", ("ha", "af")),
        P(None, "ha"),
        P(None, "ha"),
        P(),
        P("pb", None),
    )
    out_specs = (P("pb", ("ha", "af")), P(("pb", "af"), "ha"))
    return jax.shard_map(on_device, mesh=mesh, in_specs=in_specs, out_specs=out_specs, check_vma=False)
```

time: 157 us -> 92.4 us (0.59)
  Pallas kernels: 88 us -> 27.2 us
  starting transfers between devices: 34.8 us -> 29.9 us
    pallas_call x4 -> x5, Pallas kernels: 86.3 us -> 26.4 us  [the longest x1 10.7 us: softmax_stats(): pl.pallas_call(stats_kernel, in_specs=[far] * 8, out_specs=[vmem] * 4 + [...]
    ppermute x14 -> x10, starting transfers between devices: 28.6 us -> 23 us  [pair(): lax.ppermute(a, (axis, 'af'), [(2 * i + c, 2 * (i ^ masks[c]) + c) for i...]
    ppermute x14 -> x10, waiting for transfers between devices: 27.2 us -> 28.3 us  [pair(): lax.ppermute(a, (axis, 'af'), [(2 * i + c, 2 * (i ^ masks[c]) + c) for i...]
  transfers between devices with their start and end apart: 18 -> 17, of which waited for: 8 -> 9; matrix products, arithmetic and copies ran while one was open for 2% -> 2% of each run, Pallas kernels for 7% -> 15%
where the time goes in v4:
time: 92.4 us; the launch traced here: 91 us
  starting transfers between devices  29.9 us (32%)
  waiting for transfers between devices  29.9 us (32%)
  Pallas kernels  27.2 us (29%)
  local copies, waits for them, and re-layouts  1.68 us (2%)
  other arithmetic  1.48 us (2%)
    ppermute x10, waiting for transfers between devices, pair(): lax.ppermute(a, (axis, 'af'), [(2 * i + c, 2 * (i ^ masks[c]) + c) for i...  28.3 us
    ppermute x10, starting transfers between devices, pair(): lax.ppermute(a, (axis, 'af'), [(2 * i + c, 2 * (i ^ masks[c]) + c) for i...  23 us
    pallas_call x1, Pallas kernels, softmax_stats(): pl.pallas_call(stats_kernel, in_specs=[far] * 8, out_specs=[vmem] * 4 + [...  10.7 us
    pallas_call x2, Pallas kernels, visual_token_grads(): pl.pallas_call(functools.partial(grads_kernel, len(bundles) // 2, first_c...  10.2 us
    all_to_all x1, starting transfers between devices, on_device(): weights = lax.all_to_all(weights, 'ha', 0, 0, tiled=True)  5.91 us
    pallas_call x2, Pallas kernels, visual_out(): pl.pallas_call(functools.partial(visual_kernel, bool(sofar)), in_specs=[p...  5.53 us
  transfers between devices with their start and end apart: 17, of which 9 were waited for; matrix products, arithmetic and copies ran while one was open for 2% of the time, Pallas kernels for 15%

profile of v4, /device:TPU:32, one launch (start us, length us, event | category | flops | bytes accessed | tf_op | source)
XLA Modules:
  0.0 91.0 jit_solution(3583308115824671815)
XLA Ops:
  0.6 10.7 %softmax_stats.1 = (bf16[2,144,512]{2,1,0:T(8,128)(2,1)}, bf16[1024,256]{1,0:T(8,128)(2,1)}, bf16[1024,256]{1,0:T(8,128)(2,1)}, bf16[128,1024]{1,0:T(8,128)(2,1)}, bf16[8,2,512,128]{3,2,1,0:T(8,128)(2,1)}) custom-call(s32[4,8]{1,0:T(4,128)} %mask_hbm.1, s32[64,128]{1,0:T(8,128)} %bitcast.23, bf16[128,512]{1,0:T(8,128)(2,1)} %q_hbm.1, ...), custom_call_target="tpu_custom_call" | custom-call | flops 11000000512 | bytes 1048576 | tf_op jit(solution)/shard_map/softmax_stats/pallas_call | solution.py:160
  11.4 5.9 %all-to-all-start = ((bf16[8,2,512,128]{3,2,1,0:T(8,128)(2,1)}), bf16[8,2,512,128]{3,2,1,0:T(8,128)(2,1)S(1)}, u32[]{:S(2)}, u32[]{:S(2)}) async-start(bf16[8,2,512,128]{3,2,1,0:T(8,128)(2,1)} %get-tuple-element.54), calls=%async_computation | async-start | bytes 4194304 | tf_op jit(solution)/shard_map/all_to_all | solution.py:342
  17.3 1.7 %collective-permute-start = (bf16[2,144,512]{2,1,0:T(8,128)(2,1)S(1)}, bf16[2,144,512]{2,1,0:T(8,128)(2,1)S(1)}, u32[]{:S(2)}, u32[]{:S(2)}) collective-permute-start(bf16[2,144,512]{2,1,0:T(8,128)(2,1)S(1)} %copy-done), channel_id=1, source_target_pairs={{0,64},{1,193},{16,80},{17,209},{32,96},{33,225},{48,112},{49,241}... | collective-permute-start | bytes 884744 | tf_op jit(solution)/shard_map/ppermute | solution.py:327
  18.9 2.2 %collective-permute-start.1 = (bf16[2,144,512]{2,1,0:T(8,128)(2,1)S(1)}, bf16[2,144,512]{2,1,0:T(8,128)(2,1)S(1)}, u32[]{:S(2)}, u32[]{:S(2)}) collective-permute-start(bf16[2,144,512]{2,1,0:T(8,128)(2,1)S(1)} %copy-done), channel_id=1, source_target_pairs={{0,192},{1,65},{16,208},{17,81},{32,224},{33,97},{48,240},{49,113}... | collective-permute-start | bytes 884744 | tf_op jit(solution)/shard_map/ppermute | solution.py:327
  21.1 0.9 %copy-done.6 = bf16[128,1024]{1,0:T(8,128)(2,1)S(1)} copy-done((bf16[128,1024]{1,0:T(8,128)(2,1)S(1)}, bf16[128,1024]{1,0:T(8,128)(2,1)}, u32[]{:S(2)}) %copy-start.6) | copy-done | bytes 262168
  22.1 2.7 %visual_token_grads_early.1 = (bf16[1,128,512]{2,1,0:T(8,128)(2,1)S(1)}, bf16[1,128,512]{2,1,0:T(8,128)(2,1)S(1)}, f32[1024,128]{1,0:T(8,128)S(1)}, f32[1024,128]{1,0:T(8,128)S(1)}) custom-call(bf16[1024,256]{1,0:T(8,128)(2,1)S(1)} %copy-done.2, bf16[1024,256]{1,0:T(8,128)(2,1)S(1)} %copy-done.4, bf16[128,1024]{1,0:T(8,128)(2,1)S(1)} %copy-done.6, ...), custom_call_target="tpu_custom_call" | custom-call | flops 3520000000 | bytes 1048576 | tf_op jit(solution)/shard_map/visual_token_grads_early/pallas_call | solution.py:248
  25.5 2.5 %collective-permute-done.1.refs_9_ = bf16[2,144,512]{2,1,0:T(8,128)(2,1)S(1)} collective-permute-done((bf16[2,144,512]{2,1,0:T(8,128)(2,1)S(1)}, bf16[2,144,512]{2,1,0:T(8,128)(2,1)S(1)}, u32[]{:S(2)}, u32[]{:S(2)}) %collective-permute-start.1) | collective-permute-done | bytes 294944 | tf_op jit(solution)/shard_map/ppermute | solution.py:327
  28.0 3.0 %collective-permute-start.5 = (bf16[2,144,512]{2,1,0:T(8,128)(2,1)S(1)}, bf16[2,144,512]{2,1,0:T(8,128)(2,1)S(1)}, u32[]{:S(2)}, u32[]{:S(2)}) collective-permute-start(bf16[2,144,512]{2,1,0:T(8,128)(2,1)S(1)} %collective-permute-done.refs_7_), channel_id=1, source_target_pairs={{0,192},{1,65},{16,208},{17,81},{32,224},{33,97},{48,240},{49,113}... | collective-permute-start | bytes 884744 | tf_op jit(solution)/shard_map/ppermute | solution.py:327
  31.4 4.5 %collective-permute-done.5.refs_11_ = bf16[2,144,512]{2,1,0:T(8,128)(2,1)S(1)} collective-permute-done((bf16[2,144,512]{2,1,0:T(8,128)(2,1)S(1)}, bf16[2,144,512]{2,1,0:T(8,128)(2,1)S(1)}, u32[]{:S(2)}, u32[]{:S(2)}) %collective-permute-start.5) | collective-permute-done | bytes 294944 | tf_op jit(solution)/shard_map/ppermute | solution.py:327
  35.9 1.6 %collective-permute-done.6.refs_12_ = bf16[2,144,512]{2,1,0:T(8,128)(2,1)S(1)} collective-permute-done((bf16[2,144,512]{2,1,0:T(8,128)(2,1)S(1)}, bf16[2,144,512]{2,1,0:T(8,128)(2,1)S(1)}, u32[]{:S(2)}, u32[]{:S(2)}) %collective-permute-start.6) | collective-permute-done | bytes 294944 | tf_op jit(solution)/shard_map/ppermute | solution.py:322
  37.5 7.6 %visual_token_grads_late.1 = (bf16[4,128,512]{2,1,0:T(8,128)(2,1)S(1)}, bf16[4,128,512]{2,1,0:T(8,128)(2,1)S(1)}, bf16[2,256,256]{2,1,0:T(8,128)(2,1)S(1)}, bf16[2,256,256]{2,1,0:T(8,128)(2,1)S(1)}) custom-call(bf16[1024,256]{1,0:T(8,128)(2,1)S(1)} %copy-done.3, bf16[1024,256]{1,0:T(8,128)(2,1)S(1)} %copy-done.5, bf16[128,1024]{1,0:T(8,128)(2,1)S(1)} %copy-done.6, ...), custom_call_target="tpu_custom_call" | custom-call | flops 10560000000 | bytes 1048576 | tf_op jit(solution)/shard_map/visual_token_grads_late/pallas_call | solution.py:248
  46.3 3.3 %collective-permute-start.7 = (bf16[2,256,256]{2,1,0:T(8,128)(2,1)}, bf16[2,256,256]{2,1,0:T(8,128)(2,1)S(1)}, u32[]{:S(2)}, u32[]{:S(2)}) collective-permute-start(bf16[2,256,256]{2,1,0:T(8,128)(2,1)} %copy-done.1), channel_id=1, source_target_pairs={{0,16},{1,49},{16,0},{17,33},{32,48},{33,17},{48,32},{49,1},{64,80... | collective-permute-start | bytes 786440 | tf_op jit(solution)/shard_map/ppermute | solution.py:327
  49.5 1.2 %add_convert_fusion = bf16[4,128,512]{2,1,0:T(8,128)(2,1)S(1)} fusion(bf16[4,128,512]{2,1,0:T(8,128)(2,1)} %collective-permute-done.8, bf16[4,128,512]{2,1,0:T(8,128)(2,1)S(1)} %get-tuple-element.46), kind=kLoop, calls=%fused_computation | loop fusion | flops 1048576 | bytes 1572864 | tf_op jit(solution)/shard_map/convert_element_type | solution.py:331
  50.7 6.2 %collective-permute-done.7 = bf16[2,256,256]{2,1,0:T(8,128)(2,1)S(1)} collective-permute-done((bf16[2,256,256]{2,1,0:T(8,128)(2,1)}, bf16[2,256,256]{2,1,0:T(8,128)(2,1)S(1)}, u32[]{:S(2)}, u32[]{:S(2)}) %collective-permute-start.7) | collective-permute-done | bytes 262176 | tf_op jit(solution)/shard_map/ppermute | solution.py:327
  57.0 4.6 %collective-permute-start.9 = (bf16[256,256]{1,0:T(8,128)(2,1)S(1)}, bf16[256,256]{1,0:T(8,128)(2,1)S(1)}, u32[]{:S(2)}, u32[]{:S(2)}) collective-permute-start(bf16[256,256]{1,0:T(8,128)(2,1)S(1)} %fusion.1), channel_id=1, source_target_pairs={{0,48},{1,17},{16,32},{17,1},{32,16},{33,49},{48,0},{49,33},{64,11... | collective-permute-start | bytes 393224 | tf_op jit(solution)/shard_map/ppermute | solution.py:327
  61.6 3.0 %collective-permute-start.11 = (bf16[2,128,512]{2,1,0:T(8,128)(2,1)S(1)}, bf16[2,128,512]{2,1,0:T(8,128)(2,1)S(1)}, u32[]{:S(2)}, u32[]{:S(2)}) collective-permute-start(bf16[2,128,512]{2,1,0:T(8,128)(2,1)S(1)} %slice.36), channel_id=1, source_target_pairs={{0,192},{1,65},{16,208},{17,81},{32,224},{33,97},{48,240},{49,113}... | collective-permute-start | bytes 786440 | tf_op jit(solution)/shard_map/ppermute | solution.py:327
  64.9 5.0 %collective-permute-done.10 = bf16[1,256,256]{2,1,0:T(8,128)(2,1)S(1)} collective-permute-done((bf16[1,256,256]{2,1,0:T(8,128)(2,1)S(1)}, bf16[1,256,256]{2,1,0:T(8,128)(2,1)S(1)}, u32[]{:S(2)}, u32[]{:S(2)}) %collective-permute-start.10) | collective-permute-done | bytes 131104 | tf_op jit(solution)/shard_map/ppermute | solution.py:327
  69.8 2.5 %collective-permute-start.12 = (bf16[2,256,256]{2,1,0:T(8,128)(2,1)S(1)}, bf16[2,256,256]{2,1,0:T(8,128)(2,1)S(1)}, u32[]{:S(2)}, u32[]{:S(2)}) collective-permute-start(bf16[2,256,256]{2,1,0:T(8,128)(2,1)S(1)} %pad_maximum_fusion.1), channel_id=1, source_target_pairs={{0,4},{1,3},{2,6},{3,1},{4,0},{5,7},{6,2},{7,5},{8,12},{9,11},{10,... | collective-permute-start | bytes 786440 | tf_op jit(solution)/shard_map/ppermute | solution.py:327
  72.5 4.2 %collective-permute-done.12 = bf16[2,256,256]{2,1,0:T(8,128)(2,1)S(1)} collective-permute-done((bf16[2,256,256]{2,1,0:T(8,128)(2,1)S(1)}, bf16[2,256,256]{2,1,0:T(8,128)(2,1)S(1)}, u32[]{:S(2)}, u32[]{:S(2)}) %collective-permute-start.12) | collective-permute-done | bytes 262176 | tf_op jit(solution)/shard_map/ppermute | solution.py:327
  77.5 2.6 %collective-permute-start.14 = (bf16[4,256,256]{2,1,0:T(8,128)(2,1)S(1)}, bf16[4,256,256]{2,1,0:T(8,128)(2,1)S(1)}, u32[]{:S(2)}, u32[]{:S(2)}) collective-permute-start(bf16[4,256,256]{2,1,0:T(8,128)(2,1)S(1)} %pad_maximum_fusion.g_ref), channel_id=1, source_target_pairs={{0,12},{1,5},{2,14},{3,7},{4,8},{5,1},{6,10},{7,3},{8,4},{9,13},{1... | collective-permute-start | bytes 1572872 | tf_op jit(solution)/shard_map/ppermute | solution.py:327
  80.1 0.8 query_out.1
  80.9 2.3 %visual_early.1.rest_0_ = f32[2,256,512]{2,1,0:T(8,128)S(1)} custom-call(s32[4]{0:T(128)S(1)} %pad_add_fusion.place, bf16[8,2,512,128]{3,2,1,0:T(8,128)(2,1)S(1)} %all-to-all-done.mine_ref, bf16[8,2,512,128]{3,2,1,0:T(8,128)(2,1)} %collective-permute-done.15.other_ref, bf16[4,256,256]{2,1,0:T(8,128)(2,1)S(1)} %pad_maximum_fusion.g_ref), custom_call_target="tpu_custom_call" | custom-call | flops 2200000000 | bytes 1048576 | tf_op jit(solution)/shard_map/visual_early/pallas_call | solution.py:310
  83.3 4.6 %collective-permute-done.14.g_ref = bf16[4,256,256]{2,1,0:T(8,128)(2,1)S(1)} collective-permute-done((bf16[4,256,256]{2,1,0:T(8,128)(2,1)S(1)}, bf16[4,256,256]{2,1,0:T(8,128)(2,1)S(1)}, u32[]{:S(2)}, u32[]{:S(2)}) %collective-permute-start.14) | collective-permute-done | bytes 524320 | tf_op jit(solution)/shard_map/ppermute | solution.py:327
  87.8 3.2 %visual_late.1 = bf16[256,1024]{1,0:T(8,128)(2,1)} custom-call(s32[4]{0:T(128)S(1)} %pad_add_fusion.place, bf16[8,2,512,128]{3,2,1,0:T(8,128)(2,1)S(1)} %all-to-all-done.mine_ref, bf16[8,2,512,128]{3,2,1,0:T(8,128)(2,1)} %collective-permute-done.15.other_ref, bf16[4,256,256]{2,1,0:T(8,128)(2,1)S(1)} %collective-permute-done.14.g_ref, ...), custom_call_target="tpu_custom_call" | custom-call | flops 2200000000 | bytes 1048576 | tf_op jit(solution)/shard_map/visual_late/pallas_call | solution.py:310
  (38 shorter events, 3.7 us)
Async XLA Ops:
  11.3 5.9 %copy-start = (bf16[2,144,512]{2,1,0:T(8,128)(2,1)S(1)}, bf16[2,144,512]{2,1,0:T(8,128)(2,1)}, u32[]{:S(2)}) copy-start(bf16[2,144,512]{2,1,0:T(8,128)(2,1)} %get-tuple-element.33.refs_3_) | copy-start | bytes 884740
  11.3 9.8 %copy-start.2 = (bf16[1024,256]{1,0:T(8,128)(2,1)S(1)}, bf16[1024,256]{1,0:T(8,128)(2,1)}, u32[]{:S(2)}) copy-start(bf16[1024,256]{1,0:T(8,128)(2,1)} %get-tuple-element.30.refs_0_) | copy-start | bytes 1572868
  11.3 9.8 %copy-start.4 = (bf16[1024,256]{1,0:T(8,128)(2,1)S(1)}, bf16[1024,256]{1,0:T(8,128)(2,1)}, u32[]{:S(2)}) copy-start(bf16[1024,256]{1,0:T(8,128)(2,1)} %get-tuple-element.31.refs_1_) | copy-start | bytes 1572868
  11.4 34.6 %all-to-all-start = ((bf16[8,2,512,128]{3,2,1,0:T(8,128)(2,1)}), bf16[8,2,512,128]{3,2,1,0:T(8,128)(2,1)S(1)}, u32[]{:S(2)}, u32[]{:S(2)}) async-start(bf16[8,2,512,128]{3,2,1,0:T(8,128)(2,1)} %get-tuple-element.54), calls=%async_computation | async-start | bytes 4194304 | tf_op jit(solution)/shard_map/all_to_all | solution.py:342
  17.3 3.9 %collective-permute-start.2 = (bf16[2,144,512]{2,1,0:T(8,128)(2,1)S(1)}, bf16[2,144,512]{2,1,0:T(8,128)(2,1)S(1)}, u32[]{:S(2)}, u32[]{:S(2)}) collective-permute-start(bf16[2,144,512]{2,1,0:T(8,128)(2,1)S(1)} %copy-done), channel_id=1, source_target_pairs={{0,1},{1,0},{2,3},{3,2},{4,5},{5,4},{6,7},{7,6},{8,9},{9,8},{10,11... | collective-permute-start | bytes 884744 | tf_op jit(solution)/shard_map/ppermute | solution.py:322
  17.3 8.2 %collective-permute-start = (bf16[2,144,512]{2,1,0:T(8,128)(2,1)S(1)}, bf16[2,144,512]{2,1,0:T(8,128)(2,1)S(1)}, u32[]{:S(2)}, u32[]{:S(2)}) collective-permute-start(bf16[2,144,512]{2,1,0:T(8,128)(2,1)S(1)} %copy-done), channel_id=1, source_target_pairs={{0,64},{1,193},{16,80},{17,209},{32,96},{33,225},{48,112},{49,241}... | collective-permute-start | bytes 884744 | tf_op jit(solution)/shard_map/ppermute | solution.py:327
  18.9 9.0 %collective-permute-start.1 = (bf16[2,144,512]{2,1,0:T(8,128)(2,1)S(1)}, bf16[2,144,512]{2,1,0:T(8,128)(2,1)S(1)}, u32[]{:S(2)}, u32[]{:S(2)}) collective-permute-start(bf16[2,144,512]{2,1,0:T(8,128)(2,1)S(1)} %copy-done), channel_id=1, source_target_pairs={{0,192},{1,65},{16,208},{17,81},{32,224},{33,97},{48,240},{49,113}... | collective-permute-start | bytes 884744 | tf_op jit(solution)/shard_map/ppermute | solution.py:327
  21.1 1.0 %copy-start.6 = (bf16[128,1024]{1,0:T(8,128)(2,1)S(1)}, bf16[128,1024]{1,0:T(8,128)(2,1)}, u32[]{:S(2)}) copy-start(bf16[128,1024]{1,0:T(8,128)(2,1)} %get-tuple-element.32.refs_2_) | copy-start | bytes 786436
  22.1 15.4 %copy-start.3 = (bf16[1024,256]{1,0:T(8,128)(2,1)S(1)}, bf16[1024,256]{1,0:T(8,128)(2,1)}, u32[]{:S(2)}) copy-start(bf16[1024,256]{1,0:T(8,128)(2,1)} %get-tuple-element.30.refs_0_) | copy-start | bytes 1572868
  22.1 15.4 %copy-start.5 = (bf16[1024,256]{1,0:T(8,128)(2,1)S(1)}, bf16[1024,256]{1,0:T(8,128)(2,1)}, u32[]{:S(2)}) copy-start(bf16[1024,256]{1,0:T(8,128)(2,1)} %get-tuple-element.31.refs_1_) | copy-start | bytes 1572868
  28.0 7.9 %collective-permute-start.5 = (bf16[2,144,512]{2,1,0:T(8,128)(2,1)S(1)}, bf16[2,144,512]{2,1,0:T(8,128)(2,1)S(1)}, u32[]{:S(2)}, u32[]{:S(2)}) collective-permute-start(bf16[2,144,512]{2,1,0:T(8,128)(2,1)S(1)} %collective-permute-done.refs_7_), channel_id=1, source_target_pairs={{0,192},{1,65},{16,208},{17,81},{32,224},{33,97},{48,240},{49,113}... | collective-permute-start | bytes 884744 | tf_op jit(solution)/shard_map/ppermute | solution.py:327
  30.9 5.0 %collective-permute-start.3 = (bf16[2,144,512]{2,1,0:T(8,128)(2,1)S(1)}, bf16[2,144,512]{2,1,0:T(8,128)(2,1)S(1)}, u32[]{:S(2)}, u32[]{:S(2)}) collective-permute-start(bf16[2,144,512]{2,1,0:T(8,128)(2,1)S(1)} %collective-permute-done.refs_7_), channel_id=1, source_target_pairs={{0,1},{1,0},{2,3},{3,2},{4,5},{5,4},{6,7},{7,6},{8,9},{9,8},{10,11... | collective-permute-start | bytes 884744 | tf_op jit(solution)/shard_map/ppermute | solution.py:322
  30.9 5.0 %collective-permute-start.4 = (bf16[2,144,512]{2,1,0:T(8,128)(2,1)S(1)}, bf16[2,144,512]{2,1,0:T(8,128)(2,1)S(1)}, u32[]{:S(2)}, u32[]{:S(2)}) collective-permute-start(bf16[2,144,512]{2,1,0:T(8,128)(2,1)S(1)} %collective-permute-done.1.refs_9_), channel_id=1, source_target_pairs={{0,1},{1,0},{2,3},{3,2},{4,5},{5,4},{6,7},{7,6},{8,9},{9,8},{10,11... | collective-permute-start | bytes 884744 | tf_op jit(solution)/shard_map/ppermute | solution.py:322
  35.9 1.6 %collective-permute-start.6 = (bf16[2,144,512]{2,1,0:T(8,128)(2,1)S(1)}, bf16[2,144,512]{2,1,0:T(8,128)(2,1)S(1)}, u32[]{:S(2)}, u32[]{:S(2)}) collective-permute-start(bf16[2,144,512]{2,1,0:T(8,128)(2,1)S(1)} %collective-permute-done.5.refs_11_), channel_id=1, source_target_pairs={{0,1},{1,0},{2,3},{3,2},{4,5},{5,4},{6,7},{7,6},{8,9},{9,8},{10,11... | collective-permute-start | bytes 884744 | tf_op jit(solution)/shard_map/ppermute | solution.py:322
  45.1 0.7 copy-start.1
  45.8 3.8 %collective-permute-start.8 = (bf16[4,128,512]{2,1,0:T(8,128)(2,1)S(1)}, bf16[4,128,512]{2,1,0:T(8,128)(2,1)}, u32[]{:S(2)}, u32[]{:S(2)}) collective-permute-start(bf16[4,128,512]{2,1,0:T(8,128)(2,1)S(1)} %get-tuple-element.47), channel_id=1, source_target_pairs={{0,1},{1,0},{2,3},{3,2},{4,5},{5,4},{6,7},{7,6},{8,9},{9,8},{10,11... | collective-permute-start | bytes 1572872 | tf_op jit(solution)/shard_map/ppermute | solution.py:322
  45.9 35.0 %collective-permute-start.15 = (bf16[8,2,512,128]{3,2,1,0:T(8,128)(2,1)S(1)}, bf16[8,2,512,128]{3,2,1,0:T(8,128)(2,1)}, u32[]{:S(2)}, u32[]{:S(2)}) collective-permute-start(bf16[8,2,512,128]{3,2,1,0:T(8,128)(2,1)S(1)} %all-to-all-done.mine_ref), channel_id=1, source_target_pairs={{0,1},{1,0},{2,3},{3,2},{4,5},{5,4},{6,7},{7,6},{8,9},{9,8},{10,11... | collective-permute-start | bytes 6291464 | tf_op jit(solution)/shard_map/ppermute | solution.py:322
  46.3 10.7 %collective-permute-start.7 = (bf16[2,256,256]{2,1,0:T(8,128)(2,1)}, bf16[2,256,256]{2,1,0:T(8,128)(2,1)S(1)}, u32[]{:S(2)}, u32[]{:S(2)}) collective-permute-start(bf16[2,256,256]{2,1,0:T(8,128)(2,1)} %copy-done.1), channel_id=1, source_target_pairs={{0,16},{1,49},{16,0},{17,33},{32,48},{33,17},{48,32},{49,1},{64,80... | collective-permute-start | bytes 786440 | tf_op jit(solution)/shard_map/ppermute | solution.py:327
  57.0 7.7 %collective-permute-start.9 = (bf16[256,256]{1,0:T(8,128)(2,1)S(1)}, bf16[256,256]{1,0:T(8,128)(2,1)S(1)}, u32[]{:S(2)}, u32[]{:S(2)}) collective-permute-start(bf16[256,256]{1,0:T(8,128)(2,1)S(1)} %fusion.1), channel_id=1, source_target_pairs={{0,48},{1,17},{16,32},{17,1},{32,16},{33,49},{48,0},{49,33},{64,11... | collective-permute-start | bytes 393224 | tf_op jit(solution)/shard_map/ppermute | solution.py:327
  61.6 8.2 %collective-permute-start.11 = (bf16[2,128,512]{2,1,0:T(8,128)(2,1)S(1)}, bf16[2,128,512]{2,1,0:T(8,128)(2,1)S(1)}, u32[]{:S(2)}, u32[]{:S(2)}) collective-permute-start(bf16[2,128,512]{2,1,0:T(8,128)(2,1)S(1)} %slice.36), channel_id=1, source_target_pairs={{0,192},{1,65},{16,208},{17,81},{32,224},{33,97},{48,240},{49,113}... | collective-permute-start | bytes 786440 | tf_op jit(solution)/shard_map/ppermute | solution.py:327
  64.8 5.1 %collective-permute-start.10 = (bf16[1,256,256]{2,1,0:T(8,128)(2,1)S(1)}, bf16[1,256,256]{2,1,0:T(8,128)(2,1)S(1)}, u32[]{:S(2)}, u32[]{:S(2)}) collective-permute-start(bf16[1,256,256]{2,1,0:T(8,128)(2,1)S(1)} %fusion.4), channel_id=1, source_target_pairs={{0,2},{1,13},{2,0},{3,15},{4,6},{5,9},{6,4},{7,11},{8,10},{9,5},{1... | collective-permute-start | bytes 393224 | tf_op jit(solution)/shard_map/ppermute | solution.py:327
  69.8 6.8 %collective-permute-start.12 = (bf16[2,256,256]{2,1,0:T(8,128)(2,1)S(1)}, bf16[2,256,256]{2,1,0:T(8,128)(2,1)S(1)}, u32[]{:S(2)}, u32[]{:S(2)}) collective-permute-start(bf16[2,256,256]{2,1,0:T(8,128)(2,1)S(1)} %pad_maximum_fusion.1), channel_id=1, source_target_pairs={{0,4},{1,3},{2,6},{3,1},{4,0},{5,7},{6,2},{7,5},{8,12},{9,11},{10,... | collective-permute-start | bytes 786440 | tf_op jit(solution)/shard_map/ppermute | solution.py:327
  72.4 5.1 %collective-permute-start.13 = (bf16[128,512]{1,0:T(8,128)(2,1)S(1)}, bf16[128,512]{1,0:T(8,128)(2,1)S(1)}, u32[]{:S(2)}, u32[]{:S(2)}) collective-permute-start(bf16[128,512]{1,0:T(8,128)(2,1)S(1)} %get-tuple-element.59), channel_id=1, source_target_pairs={{0,64},{1,193},{16,80},{17,209},{32,96},{33,225},{48,112},{49,241}... | collective-permute-start | bytes 393224 | tf_op jit(solution)/shard_map/ppermute | solution.py:327
  77.5 10.4 %collective-permute-start.14 = (bf16[4,256,256]{2,1,0:T(8,128)(2,1)S(1)}, bf16[4,256,256]{2,1,0:T(8,128)(2,1)S(1)}, u32[]{:S(2)}, u32[]{:S(2)}) collective-permute-start(bf16[4,256,256]{2,1,0:T(8,128)(2,1)S(1)} %pad_maximum_fusion.g_ref), channel_id=1, source_target_pairs={{0,12},{1,5},{2,14},{3,7},{4,8},{5,1},{6,10},{7,3},{8,4},{9,13},{1... | collective-permute-start | bytes 1572872 | tf_op jit(solution)/shard_map/ppermute | solution.py:327

commit v5 on v4

--- a/solution.py
+++ b/solution.py
@@ -56,8 +56,8 @@
 
 
 def stats_kernel(
-    mask_hbm, fid_hbm, q_hbm, d_hbm, k_hbm, v_hbm, kw_hbm, vw_hbm, own_ref, ka_ref, va_ref, kt_ref, w_hbm,
-    mask_ref, fid_ref, k_ref, v_ref, w_ref, qt, dt, sems, wsem, small,
+    mask_hbm, fid_hbm, q_hbm, d_hbm, k_hbm, v_hbm, kw_hbm, vw_hbm, own_ref, ka_hbm, va_hbm, kt_hbm, w_hbm,
+    mask_ref, fid_ref, k_ref, v_ref, w_ref, qt, dt, ka_ref, va_ref, kt_ref, sems, wsem, small, osem,
 ):
     af = lax.axis_index("af")
     smalls = [
@@ -123,6 +123,25 @@
         ka = jnp.concatenate([k_ref[s * SUB:(s + 1) * SUB], marks(s * SUB, SUB, first, last)], axis=1)
         return dot(ka, qt[...], NN) * C2
 
+    outs = [
+        pltpu.make_async_copy(src, dst, osem.at[i])
+        for i, (src, dst) in enumerate(((ka_ref, ka_hbm), (va_ref, va_hbm), (kt_ref, kt_hbm)))
+    ]
+
+    def own_tokens():
+        y, z = lax.axis_index("pb") // 4, lax.axis_index("pb") % 4
+        order = (0, 3 - 2 * af, 1 + 2 * af, 2)
+        for s in range(4):
+            at = slice(s * PIECE, (s + 1) * PIECE)
+            base = y * 2048 + (z ^ order[s]) * 512 + af * 256
+            far = pl.ds(pl.multiple_of(base, 256), PIECE)
+            mark = marks(base, PIECE, first, last)
+            ka_ref[at] = jnp.concatenate([k_ref[far], mark], axis=1)
+            va_ref[at] = jnp.concatenate([v_ref[far], mark], axis=1)
+            kt_ref[:, at] = k_ref[far].T
+        for out in outs:
+            out.start()
+
     later = scores(0)
     for s in range(VISUAL // SUB):
         x = later
@@ -133,25 +152,17 @@
             for move, back in zip(moves, backs):
                 move.wait()
                 back.start()
+        if s == VISUAL // SUB - 3:
+            own_tokens()
         shrink = jnp.exp2(m - m_new)
         p = jnp.exp2(x - m_new)
         l = l * shrink + jnp.sum(p, axis=0, keepdims=True)
         o = o * shrink + dot(v_ref[s * SUB:(s + 1) * SUB], p.astype(BF16), TN)
         m = m_new
-    y, z = lax.axis_index("pb") // 4, lax.axis_index("pb") % 4
-    order = (0, 3 - 2 * af, 1 + 2 * af, 2)
-    for s in range(4):
-        at = slice(s * PIECE, (s + 1) * PIECE)
-        base = y * 2048 + (z ^ order[s]) * 512 + af * 256
-        far = pl.ds(pl.multiple_of(base, 256), PIECE)
-        mark = marks(base, PIECE, first, last)
-        ka_ref[at] = jnp.concatenate([k_ref[far], mark], axis=1)
-        va_ref[at] = jnp.concatenate([v_ref[far], mark], axis=1)
-        kt_ref[:, at] = k_ref[far].T
     delta = jnp.sum(dt[...].astype(F32) * o, axis=0, keepdims=True) / l
     own_ref[0, TOK:] = stat_rows(top, (m + jnp.log2(l)) * (-1.0 / C2))
     own_ref[1, TOK:] = stat_rows(jnp.zeros((8, ROWS), F32), -delta)
-    for back in backs:
+    for back in backs + outs:
         back.wait()
 
 
@@ -160,7 +171,7 @@
     return pl.pallas_call(
         stats_kernel,
         in_specs=[far] * 8,
-        out_specs=[vmem] * 4 + [far],
+        out_specs=[vmem] + [far] * 4,
         out_shape=[
             jax.ShapeDtypeStruct((2, TOK + 16, ROWS), BF16),
             jax.ShapeDtypeStruct((4 * PIECE, 2 * DH), BF16),
@@ -176,9 +187,13 @@
             pltpu.VMEM((2, 8, 512, DH), BF16),
             pltpu.VMEM((2 * DH, ROWS), BF16),
             pltpu.VMEM((DH, ROWS), BF16),
+            pltpu.VMEM((4 * PIECE, 2 * DH), BF16),
+            pltpu.VMEM((4 * PIECE, 2 * DH), BF16),
+            pltpu.VMEM((DH, 4 * PIECE), BF16),
             pltpu.SemaphoreType.DMA((2, VISUAL // TILE)),
             pltpu.SemaphoreType.DMA((4,)),
             pltpu.SemaphoreType.DMA((4,)),
+            pltpu.SemaphoreType.DMA((3,)),
         ],
         compiler_params=pltpu.CompilerParams(vmem_limit_bytes=VMEM_A << 20),
         cost_estimate=cost(10),
@@ -186,7 +201,8 @@
     )(*args)
 
 
-def grads_kernel(pairs, first_call, last_call, *refs):
+def grads_kernel(done, pairs, last_call, *refs):
+    first_call = done == 0
     refs = list(refs)
     take = lambda n: [refs.pop(0) for _ in range(n)]
     ka, va, kt = take(3)
@@ -201,7 +217,7 @@
     ksum, vsum = refs
     if not first_call:
         for q_ref, q_old in zip(q_refs, q_in):
-            q_ref[0] = q_old[0]
+            q_ref[:done] = q_old[...]
     for block, ref in enumerate(bundles):
         heads = [slice(h * DH, (h + 1) * DH) for h in range(4)]
         empty = jnp.zeros((DH - 16, ROWS), BF16)
@@ -236,17 +252,17 @@
                     out[s, :, :DH] = (kp[rows] * SCALE).astype(BF16)
                     out[s, :, DH:] = vp[rows].astype(BF16)
             total = total + dot(kt[:, at], ds, NN)
-        q_refs[block % 2][block // 2 + (not first_call)] = total.astype(BF16)
-
-
-def visual_token_grads(name, before, bundles, first_call=False, last_call=False):
+        q_refs[block % 2][done + block // 2] = total.astype(BF16)
+
+
+def visual_token_grads(name, before, bundles, done=0, last_call=False):
     vmem = pl.BlockSpec(memory_space=pltpu.VMEM)
     shape = jax.ShapeDtypeStruct
-    outs = [shape((len(bundles) // 2 + (not first_call), DH, ROWS), BF16)] * 2
+    outs = [shape((done + len(bundles) // 2, DH, ROWS), BF16)] * 2
     outs += [shape((2, PIECE, 2 * DH), BF16)] * 2 if last_call else [shape((4 * PIECE, DH), F32)] * 2
     scratch = [pltpu.VMEM((4 * PIECE, DH), F32)] * 2
     return pl.pallas_call(
-        functools.partial(grads_kernel, len(bundles) // 2, first_call, last_call),
+        functools.partial(grads_kernel, done, len(bundles) // 2, last_call),
         in_specs=[vmem] * (len(before) + len(bundles)),
         out_specs=[vmem] * len(outs),
         out_shape=outs,
@@ -275,47 +291,61 @@
     )(mine, got)
 
 
-def visual_kernel(late, place, mine_ref, other_ref, g_ref, *rest):
-    sofar_ref, out_ref = rest if late else (None, rest[0])
+def early_kernel(place, mine_ref, other_ref, g_ref, sofar_ref, w_ref):
     af, ha = place[2], place[3]
     first = jnp.where(af == 0, 1, 6)
     second = jnp.where(af == 0, 2, 1)
     third = jnp.where(af == 0, 6, 2)
-    totals = []
     for side, ref in enumerate((mine_ref, other_ref)):
-        total = sofar_ref[side] if late else jnp.zeros((256, 512), F32)
+        total = jnp.zeros((256, 512), F32)
         for k in range(4):
-            source = ha ^ third if late else ha
+            source = ha
             for bit, mask in ((1, first), (2, second)):
                 if k & bit:
                     source = source ^ mask
             w = jnp.concatenate([ref[source, 0], ref[source, 1]], axis=1)
             total = total + dot(g_ref[k], w, NT)
-        if late:
-            totals.append(total)
-        else:
-            out_ref[side] = total
-    for core in range(2) if late else ():
-
-        @pl.when(af == core)
+            for i in range(2):
+                w_ref[side, k, :, i * DH:(i + 1) * DH] = ref[source ^ third, i]
+        sofar_ref[side] = total
+
+
+def late_kernel(place, w_ref, g_ref, sofar_ref, out_ref):
+    totals = []
+    for side in range(2):
+        total = sofar_ref[side]
+        for k in range(4):
+            total = total + dot(g_ref[k], w_ref[side, k], NT)
+        totals.append(total)
+    for core in range(2):
+
+        @pl.when(place[2] == core)
         def _():
             for side in range(2):
                 at = (side ^ core) * 512
                 out_ref[:, at:at + 512] = totals[side].astype(BF16)
 
 
-def visual_out(place, mine, other, g, *sofar):
+def visual_call(kernel, name, outs, *args):
     vmem = pl.BlockSpec(memory_space=pltpu.VMEM)
-    early = jax.ShapeDtypeStruct((2, 256, 512), F32)
     return pl.pallas_call(
-        functools.partial(visual_kernel, bool(sofar)),
-        in_specs=[pl.BlockSpec(memory_space=pltpu.SMEM)] + [vmem] * (3 + len(sofar)),
-        out_specs=vmem,
-        out_shape=jax.ShapeDtypeStruct((256, 1024), BF16) if sofar else early,
+        kernel,
+        in_specs=[pl.BlockSpec(memory_space=pltpu.SMEM)] + [vmem] * (len(args) - 1),
+        out_specs=[vmem] * len(outs),
+        out_shape=outs,
         compiler_params=pltpu.CompilerParams(vmem_limit_bytes=24 << 20),
         cost_estimate=cost(2),
-        name="visual_late" if sofar else "visual_early",
-    )(place, mine, other, g, *sofar)
+        name=name,
+    )(*args)
+
+
+def visual_early(*args):
+    outs = [jax.ShapeDtypeStruct((2, 256, 512), F32), jax.ShapeDtypeStruct((2, 4, 512, 2 * DH), BF16)]
+    return visual_call(early_kernel, "visual_early", outs, *args)
+
+
+def visual_late(*args):
+    return visual_call(late_kernel, "visual_late", [jax.ShapeDtypeStruct((256, 1024), BF16)], *args)[0]
 
 
 def swap_cores(a):
@@ -342,22 +372,23 @@
     weights = lax.all_to_all(weights, "ha", 0, 0, tiled=True)
     near, back = pair(own, "pb", (4, 12)), pair(own, "pb", (12, 4))
     own2 = swap_cores(own)
-    early = visual_token_grads("early", [ka, va, kt], [own, own2], first_call=True)
+    early = visual_token_grads("first", [ka, va, kt], [own, own2])
     near, back, early = tie((near, back, early))
     across = pair(near, "pb", (12, 4))
-    near2, back2 = swap_cores(near), swap_cores(back)
+    middle = visual_token_grads(
+        "second", [ka, va, kt, *early[2:], *early[:2]], [near, swap_cores(near), back, swap_cores(back)], done=1
+    )
+    across, middle = tie((across, middle))
     qown, qother, keep, send = visual_token_grads(
-        "late",
-        [ka, va, kt, *early[2:], *early[:2]],
-        [near, near2, back, back2, across, swap_cores(across)],
-        last_call=True,
+        "third", [ka, va, kt, *middle[2:], *middle[:2]], [across, swap_cores(across)], done=3, last_call=True
     )
 
     got = pair(send, "pb", (1, 3))
+    got, qother = tie((got, qother))
     qpart = plus(qown, swap_cores(qother))
-    qgot = pair(qpart[2:], "pb", (12, 4))
-    got, qpart = tie((got, qpart))
     got2 = pair(plus(keep[1], got[1]), "pb", (3, 1))
+    got2, weights, qgot_in = tie((got2, weights, qpart[2:]))
+    qgot = pair(qgot_in, "pb", (12, 4))
     g = plus(keep[0], got[0], got2)[None]
     weights2 = swap_cores(weights)
     g = jnp.concatenate([g, pair(g, "ha", (1, 6))], axis=0)
@@ -366,10 +397,10 @@
     g = jnp.concatenate([g, pair(g, "ha", (2, 1))], axis=0)
     g, qgot2 = tie((g, qgot2))
     far = pair(g, "ha", (6, 2))
-    early = visual_out(place, weights, weights2, g)
+    early, far_weights = visual_early(place, weights, weights2, g)
     query_grad = query_out(plus(qpart[0], qgot[0]), qgot2)
     far, query_grad, early = tie((far, query_grad, early))
-    visual_grad = visual_out(place, weights, weights2, far, early)
+    visual_grad = visual_late(place, far_weights, far, early)
     return query_grad, visual_grad
 
 

time: 92.4 us -> 90 us (0.974); the launches traced: 91 us -> 89.8 us
  starting transfers between devices: 29.9 us -> 28.9 us
    ppermute x10, starting transfers between devices: 23 us -> 21.5 us  [pair(): lax.ppermute(a, (axis, 'af'), [(2 * i + c, 2 * (i ^ masks[c]) + c) for i...]
    convert_element_type x3, other arithmetic: 1.28 us -> 0.23 us  [plus(): functools.reduce(jnp.add, [t.astype(F32) for t in terms]).astype(BF16)]
    pallas_call x5 -> x6, Pallas kernels: 26.4 us -> 26.6 us  [the longest x1 11.4 us: softmax_stats(): pl.pallas_call(stats_kernel, in_specs=[far] * 8, out_specs=[vmem] + [far]...]
where the time goes in v5:
time: 90 us; the launch traced here: 89.8 us
  waiting for transfers between devices  29.7 us (33%)
  starting transfers between devices  28.9 us (32%)
  Pallas kernels  27.3 us (30%)
  local copies, waits for them, and re-layouts  1.68 us (2%)
  other arithmetic  1.34 us (1%)
    ppermute x10, waiting for transfers between devices, pair(): lax.ppermute(a, (axis, 'af'), [(2 * i + c, 2 * (i ^ masks[c]) + c) for i...  28.1 us
    ppermute x10, starting transfers between devices, pair(): lax.ppermute(a, (axis, 'af'), [(2 * i + c, 2 * (i ^ masks[c]) + c) for i...  21.5 us
    pallas_call x1, Pallas kernels, softmax_stats(): pl.pallas_call(stats_kernel, in_specs=[far] * 8, out_specs=[vmem] + [far]...  11.4 us
    pallas_call x3, Pallas kernels, visual_token_grads(): pl.pallas_call(functools.partial(grads_kernel, done, len(bundles) // 2, l...  10.4 us
    all_to_all x1, starting transfers between devices, on_device(): weights = lax.all_to_all(weights, 'ha', 0, 0, tiled=True)  5.91 us
    pallas_call x2, Pallas kernels, visual_call(): pl.pallas_call(kernel, in_specs=[pl.BlockSpec(memory_space=pltpu.SMEM)] +...  4.74 us
  transfers between devices with their start and end apart: 17, of which 9 were waited for; matrix products, arithmetic and copies ran while one was open for 2% of the time, Pallas kernels for 15%

profile of v5, /device:TPU:32, one launch (start us, length us, event | category | flops | bytes accessed | tf_op | source)
XLA Modules:
  0.0 89.8 jit_solution(66569339930887576)
XLA Ops:
  0.6 11.4 %softmax_stats.1 = (bf16[2,144,512]{2,1,0:T(8,128)(2,1)}, bf16[1024,256]{1,0:T(8,128)(2,1)}, bf16[1024,256]{1,0:T(8,128)(2,1)}, bf16[128,1024]{1,0:T(8,128)(2,1)}, bf16[8,2,512,128]{3,2,1,0:T(8,128)(2,1)}) custom-call(s32[4,8]{1,0:T(4,128)} %mask_hbm.1, s32[64,128]{1,0:T(8,128)} %bitcast.23, bf16[128,512]{1,0:T(8,128)(2,1)} %q_hbm.1, ...), custom_call_target="tpu_custom_call" | custom-call | flops 11000000512 | bytes 1048576 | tf_op jit(solution)/shard_map/softmax_stats/pallas_call | solution.py:171
  12.0 5.9 %all-to-all-start = ((bf16[8,2,512,128]{3,2,1,0:T(8,128)(2,1)}), bf16[8,2,512,128]{3,2,1,0:T(8,128)(2,1)S(1)}, u32[]{:S(2)}, u32[]{:S(2)}) async-start(bf16[8,2,512,128]{3,2,1,0:T(8,128)(2,1)} %get-tuple-element.71), calls=%async_computation | async-start | bytes 4194304 | tf_op jit(solution)/shard_map/all_to_all | solution.py:372
  18.0 1.7 %collective-permute-start = (bf16[2,144,512]{2,1,0:T(8,128)(2,1)S(1)}, bf16[2,144,512]{2,1,0:T(8,128)(2,1)S(1)}, u32[]{:S(2)}, u32[]{:S(2)}) collective-permute-start(bf16[2,144,512]{2,1,0:T(8,128)(2,1)S(1)} %copy-done), channel_id=1, source_target_pairs={{0,64},{1,193},{16,80},{17,209},{32,96},{33,225},{48,112},{49,241}... | collective-permute-start | bytes 884744 | tf_op jit(solution)/shard_map/ppermute | solution.py:357
  19.6 2.2 %collective-permute-start.1 = (bf16[2,144,512]{2,1,0:T(8,128)(2,1)S(1)}, bf16[2,144,512]{2,1,0:T(8,128)(2,1)S(1)}, u32[]{:S(2)}, u32[]{:S(2)}) collective-permute-start(bf16[2,144,512]{2,1,0:T(8,128)(2,1)S(1)} %copy-done), channel_id=1, source_target_pairs={{0,192},{1,65},{16,208},{17,81},{32,224},{33,97},{48,240},{49,113}... | collective-permute-start | bytes 884744 | tf_op jit(solution)/shard_map/ppermute | solution.py:357
  21.8 0.9 %copy-done.3 = bf16[128,1024]{1,0:T(8,128)(2,1)S(1)} copy-done((bf16[128,1024]{1,0:T(8,128)(2,1)S(1)}, bf16[128,1024]{1,0:T(8,128)(2,1)}, u32[]{:S(2)}) %copy-start.3) | copy-done | bytes 262168
  22.8 2.7 %visual_token_grads_first.1 = (bf16[1,128,512]{2,1,0:T(8,128)(2,1)S(1)}, bf16[1,128,512]{2,1,0:T(8,128)(2,1)S(1)}, f32[1024,128]{1,0:T(8,128)S(1)}, f32[1024,128]{1,0:T(8,128)S(1)}) custom-call(bf16[1024,256]{1,0:T(8,128)(2,1)S(1)} %copy-done.1, bf16[1024,256]{1,0:T(8,128)(2,1)S(1)} %copy-done.2, bf16[128,1024]{1,0:T(8,128)(2,1)S(1)} %copy-done.3, ...), custom_call_target="tpu_custom_call" | custom-call | flops 3520000000 | bytes 1048576 | tf_op jit(solution)/shard_map/visual_token_grads_first/pallas_call | solution.py:264
  26.1 2.5 %collective-permute-done.1.refs_9_ = bf16[2,144,512]{2,1,0:T(8,128)(2,1)S(1)} collective-permute-done((bf16[2,144,512]{2,1,0:T(8,128)(2,1)S(1)}, bf16[2,144,512]{2,1,0:T(8,128)(2,1)S(1)}, u32[]{:S(2)}, u32[]{:S(2)}) %collective-permute-start.1) | collective-permute-done | bytes 294944 | tf_op jit(solution)/shard_map/ppermute | solution.py:357
  29.2 3.0 %collective-permute-start.3 = (bf16[2,144,512]{2,1,0:T(8,128)(2,1)S(1)}, bf16[2,144,512]{2,1,0:T(8,128)(2,1)S(1)}, u32[]{:S(2)}, u32[]{:S(2)}) collective-permute-start(bf16[2,144,512]{2,1,0:T(8,128)(2,1)S(1)} %collective-permute-done.refs_7_), channel_id=1, source_target_pairs={{0,192},{1,65},{16,208},{17,81},{32,224},{33,97},{48,240},{49,113}... | collective-permute-start | bytes 884744 | tf_op jit(solution)/shard_map/ppermute | solution.py:357
  32.1 5.1 %visual_token_grads_second.1 = (bf16[3,128,512]{2,1,0:T(8,128)(2,1)S(1)}, bf16[3,128,512]{2,1,0:T(8,128)(2,1)S(1)}, f32[1024,128]{1,0:T(8,128)S(1)}, f32[1024,128]{1,0:T(8,128)S(1)}) custom-call(bf16[1024,256]{1,0:T(8,128)(2,1)S(1)} %copy-done.1, bf16[1024,256]{1,0:T(8,128)(2,1)S(1)} %copy-done.2, bf16[128,1024]{1,0:T(8,128)(2,1)S(1)} %copy-done.3, ...), custom_call_target="tpu_custom_call" | custom-call | flops 7040000000 | bytes 1048576 | tf_op jit(solution)/shard_map/visual_token_grads_second/pallas_call | solution.py:264
  37.4 1.6 %collective-permute-done.6.refs_8_ = bf16[2,144,512]{2,1,0:T(8,128)(2,1)S(1)} collective-permute-done((bf16[2,144,512]{2,1,0:T(8,128)(2,1)S(1)}, bf16[2,144,512]{2,1,0:T(8,128)(2,1)S(1)}, u32[]{:S(2)}, u32[]{:S(2)}) %collective-permute-start.6) | collective-permute-done | bytes 294944 | tf_op jit(solution)/shard_map/ppermute | solution.py:352
  38.9 2.7 %visual_token_grads_third.1 = (bf16[4,128,512]{2,1,0:T(8,128)(2,1)S(1)}, bf16[4,128,512]{2,1,0:T(8,128)(2,1)S(1)}, bf16[2,256,256]{2,1,0:T(8,128)(2,1)S(1)}, bf16[2,256,256]{2,1,0:T(8,128)(2,1)S(1)}) custom-call(bf16[1024,256]{1,0:T(8,128)(2,1)S(1)} %copy-done.1, bf16[1024,256]{1,0:T(8,128)(2,1)S(1)} %copy-done.2, bf16[128,1024]{1,0:T(8,128)(2,1)S(1)} %copy-done.3, ...), custom_call_target="tpu_custom_call" | custom-call | flops 3520000000 | bytes 1048576 | tf_op jit(solution)/shard_map/visual_token_grads_third/pallas_call | solution.py:264
  41.6 3.4 %collective-permute-start.7 = (bf16[2,256,256]{2,1,0:T(8,128)(2,1)S(1)}, bf16[2,256,256]{2,1,0:T(8,128)(2,1)S(1)}, u32[]{:S(2)}, u32[]{:S(2)}) collective-permute-start(bf16[2,256,256]{2,1,0:T(8,128)(2,1)S(1)} %get-tuple-element.68), channel_id=1, source_target_pairs={{0,16},{1,49},{16,0},{17,33},{32,48},{33,17},{48,32},{49,1},{64,80... | collective-permute-start | bytes 786440 | tf_op jit(solution)/shard_map/ppermute | solution.py:357
  45.0 7.2 %collective-permute-done.7 = bf16[2,256,256]{2,1,0:T(8,128)(2,1)S(1)} collective-permute-done((bf16[2,256,256]{2,1,0:T(8,128)(2,1)S(1)}, bf16[2,256,256]{2,1,0:T(8,128)(2,1)S(1)}, u32[]{:S(2)}, u32[]{:S(2)}) %collective-permute-start.7) | collective-permute-done | bytes 262176 | tf_op jit(solution)/shard_map/ppermute | solution.py:357
  53.1 3.7 %collective-permute-start.8 = (bf16[256,256]{1,0:T(8,128)(2,1)S(1)}, bf16[256,256]{1,0:T(8,128)(2,1)S(1)}, u32[]{:S(2)}, u32[]{:S(2)}) collective-permute-start(bf16[256,256]{1,0:T(8,128)(2,1)S(1)} %fusion.1), channel_id=1, source_target_pairs={{0,48},{1,17},{16,32},{17,1},{32,16},{33,49},{48,0},{49,33},{64,11... | collective-permute-start | bytes 393224 | tf_op jit(solution)/shard_map/ppermute | solution.py:357
  57.7 3.7 %collective-permute-done.8 = bf16[256,256]{1,0:T(8,128)(2,1)S(1)} collective-permute-done((bf16[256,256]{1,0:T(8,128)(2,1)S(1)}, bf16[256,256]{1,0:T(8,128)(2,1)S(1)}, u32[]{:S(2)}, u32[]{:S(2)}) %collective-permute-start.8) | collective-permute-done | bytes 131104 | tf_op jit(solution)/shard_map/ppermute | solution.py:357
  61.4 2.7 %collective-permute-start.11 = (bf16[2,128,512]{2,1,0:T(8,128)(2,1)}, bf16[2,128,512]{2,1,0:T(8,128)(2,1)S(1)}, u32[]{:S(2)}, u32[]{:S(2)}) collective-permute-start(bf16[2,128,512]{2,1,0:T(8,128)(2,1)} %slice.36), channel_id=1, source_target_pairs={{0,192},{1,65},{16,208},{17,81},{32,224},{33,97},{48,240},{49,113}... | collective-permute-start | bytes 786440 | tf_op jit(solution)/shard_map/ppermute | solution.py:357
  64.1 1.0 %fusion.4 = bf16[1,256,256]{2,1,0:T(8,128)(2,1)S(1)} fusion(bf16[256,256]{1,0:T(8,128)(2,1)S(1)} %collective-permute-done.8, bf16[2,256,256]{2,1,0:T(8,128)(2,1)} %copy-done.4, bf16[2,256,256]{2,1,0:T(8,128)(2,1)S(1)} %get-tuple-element.67), kind=kLoop, calls=%fused_computation.11 | loop fusion | flops 393216 | bytes 524288 | tf_op jit(solution)/shard_map/broadcast_in_dim | solution.py:392
  65.3 4.8 %collective-permute-done.10 = bf16[1,256,256]{2,1,0:T(8,128)(2,1)S(1)} collective-permute-done((bf16[1,256,256]{2,1,0:T(8,128)(2,1)S(1)}, bf16[1,256,256]{2,1,0:T(8,128)(2,1)S(1)}, u32[]{:S(2)}, u32[]{:S(2)}) %collective-permute-start.10) | collective-permute-done | bytes 131104 | tf_op jit(solution)/shard_map/ppermute | solution.py:357
  70.1 2.0 %collective-permute-start.12 = (bf16[2,256,256]{2,1,0:T(8,128)(2,1)S(1)}, bf16[2,256,256]{2,1,0:T(8,128)(2,1)S(1)}, u32[]{:S(2)}, u32[]{:S(2)}) collective-permute-start(bf16[2,256,256]{2,1,0:T(8,128)(2,1)S(1)} %pad_maximum_fusion.1), channel_id=1, source_target_pairs={{0,4},{1,3},{2,6},{3,1},{4,0},{5,7},{6,2},{7,5},{8,12},{9,11},{10,... | collective-permute-start | bytes 786440 | tf_op jit(solution)/shard_map/ppermute | solution.py:357
  72.3 4.7 %collective-permute-done.12 = bf16[2,256,256]{2,1,0:T(8,128)(2,1)S(1)} collective-permute-done((bf16[2,256,256]{2,1,0:T(8,128)(2,1)S(1)}, bf16[2,256,256]{2,1,0:T(8,128)(2,1)S(1)}, u32[]{:S(2)}, u32[]{:S(2)}) %collective-permute-start.12) | collective-permute-done | bytes 262176 | tf_op jit(solution)/shard_map/ppermute | solution.py:357
  77.3 2.6 %collective-permute-start.14 = (bf16[4,256,256]{2,1,0:T(8,128)(2,1)S(1)}, bf16[4,256,256]{2,1,0:T(8,128)(2,1)S(1)}, u32[]{:S(2)}, u32[]{:S(2)}) collective-permute-start(bf16[4,256,256]{2,1,0:T(8,128)(2,1)S(1)} %pad_maximum_fusion.g_ref), channel_id=1, source_target_pairs={{0,12},{1,5},{2,14},{3,7},{4,8},{5,1},{6,10},{7,3},{8,4},{9,13},{1... | collective-permute-start | bytes 1572872 | tf_op jit(solution)/shard_map/ppermute | solution.py:357
  80.7 2.6 %visual_early.1 = (f32[2,256,512]{2,1,0:T(8,128)S(1)}, bf16[2,4,512,256]{3,2,1,0:T(8,128)(2,1)S(1)}) custom-call(s32[4]{0:T(128)S(1)} %pad_add_fusion.place, bf16[8,2,512,128]{3,2,1,0:T(8,128)(2,1)S(1)} %all-to-all-done.mine_ref, bf16[8,2,512,128]{3,2,1,0:T(8,128)(2,1)} %collective-permute-done.15.other_ref, bf16[4,256,256]{2,1,0:T(8,128)(2,1)S(1)} %pad_maximum_fusion.g_ref), custom_call_target="tpu_custom_call" | custom-call | flops 2200000000 | bytes 1048576 | tf_op jit(solution)/shard_map/visual_early/pallas_call | solution.py:331
  83.4 4.3 %collective-permute-done.14.g_ref = bf16[4,256,256]{2,1,0:T(8,128)(2,1)S(1)} collective-permute-done((bf16[4,256,256]{2,1,0:T(8,128)(2,1)S(1)}, bf16[4,256,256]{2,1,0:T(8,128)(2,1)S(1)}, u32[]{:S(2)}, u32[]{:S(2)}) %collective-permute-start.14) | collective-permute-done | bytes 524320 | tf_op jit(solution)/shard_map/ppermute | solution.py:357
  87.7 2.1 %visual_late.1 = bf16[256,1024]{1,0:T(8,128)(2,1)} custom-call(s32[4]{0:T(128)S(1)} %pad_add_fusion.place, bf16[2,4,512,256]{3,2,1,0:T(8,128)(2,1)S(1)} %get-tuple-element.83.w_ref, bf16[4,256,256]{2,1,0:T(8,128)(2,1)S(1)} %collective-permute-done.14.g_ref, f32[2,256,512]{2,1,0:T(8,128)S(1)} %get-tuple-element.85.sofar_ref), custom_call_target="tpu_custom_call" | custom-call | flops 2200000000 | bytes 1048576 | tf_op jit(solution)/shard_map/visual_late/pallas_call | solution.py:331
  (35 shorter events, 4.7 us)
Async XLA Ops:
  12.0 5.9 %copy-start = (bf16[2,144,512]{2,1,0:T(8,128)(2,1)S(1)}, bf16[2,144,512]{2,1,0:T(8,128)(2,1)}, u32[]{:S(2)}) copy-start(bf16[2,144,512]{2,1,0:T(8,128)(2,1)} %get-tuple-element.47.refs_3_) | copy-start | bytes 884740
  12.0 9.8 %copy-start.1 = (bf16[1024,256]{1,0:T(8,128)(2,1)S(1)}, bf16[1024,256]{1,0:T(8,128)(2,1)}, u32[]{:S(2)}) copy-start(bf16[1024,256]{1,0:T(8,128)(2,1)} %get-tuple-element.44.refs_0_) | copy-start | bytes 1572868
  12.0 9.8 %copy-start.2 = (bf16[1024,256]{1,0:T(8,128)(2,1)S(1)}, bf16[1024,256]{1,0:T(8,128)(2,1)}, u32[]{:S(2)}) copy-start(bf16[1024,256]{1,0:T(8,128)(2,1)} %get-tuple-element.45.refs_1_) | copy-start | bytes 1572868
  12.0 49.3 %all-to-all-start = ((bf16[8,2,512,128]{3,2,1,0:T(8,128)(2,1)}), bf16[8,2,512,128]{3,2,1,0:T(8,128)(2,1)S(1)}, u32[]{:S(2)}, u32[]{:S(2)}) async-start(bf16[8,2,512,128]{3,2,1,0:T(8,128)(2,1)} %get-tuple-element.71), calls=%async_computation | async-start | bytes 4194304 | tf_op jit(solution)/shard_map/all_to_all | solution.py:372
  17.9 3.9 %collective-permute-start.2 = (bf16[2,144,512]{2,1,0:T(8,128)(2,1)S(1)}, bf16[2,144,512]{2,1,0:T(8,128)(2,1)S(1)}, u32[]{:S(2)}, u32[]{:S(2)}) collective-permute-start(bf16[2,144,512]{2,1,0:T(8,128)(2,1)S(1)} %copy-done), channel_id=1, source_target_pairs={{0,1},{1,0},{2,3},{3,2},{4,5},{5,4},{6,7},{7,6},{8,9},{9,8},{10,11... | collective-permute-start | bytes 884744 | tf_op jit(solution)/shard_map/ppermute | solution.py:352
  18.0 8.2 %collective-permute-start = (bf16[2,144,512]{2,1,0:T(8,128)(2,1)S(1)}, bf16[2,144,512]{2,1,0:T(8,128)(2,1)S(1)}, u32[]{:S(2)}, u32[]{:S(2)}) collective-permute-start(bf16[2,144,512]{2,1,0:T(8,128)(2,1)S(1)} %copy-done), channel_id=1, source_target_pairs={{0,64},{1,193},{16,80},{17,209},{32,96},{33,225},{48,112},{49,241}... | collective-permute-start | bytes 884744 | tf_op jit(solution)/shard_map/ppermute | solution.py:357
  19.6 9.0 %collective-permute-start.1 = (bf16[2,144,512]{2,1,0:T(8,128)(2,1)S(1)}, bf16[2,144,512]{2,1,0:T(8,128)(2,1)S(1)}, u32[]{:S(2)}, u32[]{:S(2)}) collective-permute-start(bf16[2,144,512]{2,1,0:T(8,128)(2,1)S(1)} %copy-done), channel_id=1, source_target_pairs={{0,192},{1,65},{16,208},{17,81},{32,224},{33,97},{48,240},{49,113}... | collective-permute-start | bytes 884744 | tf_op jit(solution)/shard_map/ppermute | solution.py:357
  21.8 1.0 %copy-start.3 = (bf16[128,1024]{1,0:T(8,128)(2,1)S(1)}, bf16[128,1024]{1,0:T(8,128)(2,1)}, u32[]{:S(2)}) copy-start(bf16[128,1024]{1,0:T(8,128)(2,1)} %get-tuple-element.46.refs_2_) | copy-start | bytes 786436
  28.6 3.5 %collective-permute-start.4 = (bf16[2,144,512]{2,1,0:T(8,128)(2,1)S(1)}, bf16[2,144,512]{2,1,0:T(8,128)(2,1)S(1)}, u32[]{:S(2)}, u32[]{:S(2)}) collective-permute-start(bf16[2,144,512]{2,1,0:T(8,128)(2,1)S(1)} %collective-permute-done.refs_7_), channel_id=1, source_target_pairs={{0,1},{1,0},{2,3},{3,2},{4,5},{5,4},{6,7},{7,6},{8,9},{9,8},{10,11... | collective-permute-start | bytes 884744 | tf_op jit(solution)/shard_map/ppermute | solution.py:352
  28.6 3.5 %collective-permute-start.5 = (bf16[2,144,512]{2,1,0:T(8,128)(2,1)S(1)}, bf16[2,144,512]{2,1,0:T(8,128)(2,1)S(1)}, u32[]{:S(2)}, u32[]{:S(2)}) collective-permute-start(bf16[2,144,512]{2,1,0:T(8,128)(2,1)S(1)} %collective-permute-done.1.refs_9_), channel_id=1, source_target_pairs={{0,1},{1,0},{2,3},{3,2},{4,5},{5,4},{6,7},{7,6},{8,9},{9,8},{10,11... | collective-permute-start | bytes 884744 | tf_op jit(solution)/shard_map/ppermute | solution.py:352
  29.2 8.1 %collective-permute-start.3 = (bf16[2,144,512]{2,1,0:T(8,128)(2,1)S(1)}, bf16[2,144,512]{2,1,0:T(8,128)(2,1)S(1)}, u32[]{:S(2)}, u32[]{:S(2)}) collective-permute-start(bf16[2,144,512]{2,1,0:T(8,128)(2,1)S(1)} %collective-permute-done.refs_7_), channel_id=1, source_target_pairs={{0,192},{1,65},{16,208},{17,81},{32,224},{33,97},{48,240},{49,113}... | collective-permute-start | bytes 884744 | tf_op jit(solution)/shard_map/ppermute | solution.py:357
  37.3 1.7 %collective-permute-start.6 = (bf16[2,144,512]{2,1,0:T(8,128)(2,1)S(1)}, bf16[2,144,512]{2,1,0:T(8,128)(2,1)S(1)}, u32[]{:S(2)}, u32[]{:S(2)}) collective-permute-start(bf16[2,144,512]{2,1,0:T(8,128)(2,1)S(1)} %collective-permute-done.3.refs_7_), channel_id=1, source_target_pairs={{0,1},{1,0},{2,3},{3,2},{4,5},{5,4},{6,7},{7,6},{8,9},{9,8},{10,11... | collective-permute-start | bytes 884744 | tf_op jit(solution)/shard_map/ppermute | solution.py:352
  41.6 10.6 %collective-permute-start.7 = (bf16[2,256,256]{2,1,0:T(8,128)(2,1)S(1)}, bf16[2,256,256]{2,1,0:T(8,128)(2,1)S(1)}, u32[]{:S(2)}, u32[]{:S(2)}) collective-permute-start(bf16[2,256,256]{2,1,0:T(8,128)(2,1)S(1)} %get-tuple-element.68), channel_id=1, source_target_pairs={{0,16},{1,49},{16,0},{17,33},{32,48},{33,17},{48,32},{49,1},{64,80... | collective-permute-start | bytes 786440 | tf_op jit(solution)/shard_map/ppermute | solution.py:357
  52.2 4.7 %copy-start.4 = (bf16[2,256,256]{2,1,0:T(8,128)(2,1)}, bf16[2,256,256]{2,1,0:T(8,128)(2,1)S(1)}, u32[]{:S(2)}) copy-start(bf16[2,256,256]{2,1,0:T(8,128)(2,1)S(1)} %collective-permute-done.7) | copy-start | bytes 786436
  52.2 4.7 %collective-permute-start.9 = (bf16[4,128,512]{2,1,0:T(8,128)(2,1)S(1)}, bf16[4,128,512]{2,1,0:T(8,128)(2,1)S(1)}, u32[]{:S(2)}, u32[]{:S(2)}) collective-permute-start(bf16[4,128,512]{2,1,0:T(8,128)(2,1)S(1)} %get-tuple-element.73), channel_id=1, source_target_pairs={{0,1},{1,0},{2,3},{3,2},{4,5},{5,4},{6,7},{7,6},{8,9},{9,8},{10,11... | collective-permute-start | bytes 1572872 | tf_op jit(solution)/shard_map/ppermute | solution.py:352
  53.1 8.3 %collective-permute-start.8 = (bf16[256,256]{1,0:T(8,128)(2,1)S(1)}, bf16[256,256]{1,0:T(8,128)(2,1)S(1)}, u32[]{:S(2)}, u32[]{:S(2)}) collective-permute-start(bf16[256,256]{1,0:T(8,128)(2,1)S(1)} %fusion.1), channel_id=1, source_target_pairs={{0,48},{1,17},{16,32},{17,1},{32,16},{33,49},{48,0},{49,33},{64,11... | collective-permute-start | bytes 393224 | tf_op jit(solution)/shard_map/ppermute | solution.py:357
  61.4 19.4 %collective-permute-start.15 = (bf16[8,2,512,128]{3,2,1,0:T(8,128)(2,1)S(1)}, bf16[8,2,512,128]{3,2,1,0:T(8,128)(2,1)}, u32[]{:S(2)}, u32[]{:S(2)}) collective-permute-start(bf16[8,2,512,128]{3,2,1,0:T(8,128)(2,1)S(1)} %all-to-all-done.mine_ref), channel_id=1, source_target_pairs={{0,1},{1,0},{2,3},{3,2},{4,5},{5,4},{6,7},{7,6},{8,9},{9,8},{10,11... | collective-permute-start | bytes 6291464 | tf_op jit(solution)/shard_map/ppermute | solution.py:352
  61.4 8.7 %collective-permute-start.11 = (bf16[2,128,512]{2,1,0:T(8,128)(2,1)}, bf16[2,128,512]{2,1,0:T(8,128)(2,1)S(1)}, u32[]{:S(2)}, u32[]{:S(2)}) collective-permute-start(bf16[2,128,512]{2,1,0:T(8,128)(2,1)} %slice.36), channel_id=1, source_target_pairs={{0,192},{1,65},{16,208},{17,81},{32,224},{33,97},{48,240},{49,113}... | collective-permute-start | bytes 786440 | tf_op jit(solution)/shard_map/ppermute | solution.py:357
  65.0 5.1 %collective-permute-start.10 = (bf16[1,256,256]{2,1,0:T(8,128)(2,1)S(1)}, bf16[1,256,256]{2,1,0:T(8,128)(2,1)S(1)}, u32[]{:S(2)}, u32[]{:S(2)}) collective-permute-start(bf16[1,256,256]{2,1,0:T(8,128)(2,1)S(1)} %fusion.4), channel_id=1, source_target_pairs={{0,2},{1,13},{2,0},{3,15},{4,6},{5,9},{6,4},{7,11},{8,10},{9,5},{1... | collective-permute-start | bytes 393224 | tf_op jit(solution)/shard_map/ppermute | solution.py:357
  70.1 6.8 %collective-permute-start.12 = (bf16[2,256,256]{2,1,0:T(8,128)(2,1)S(1)}, bf16[2,256,256]{2,1,0:T(8,128)(2,1)S(1)}, u32[]{:S(2)}, u32[]{:S(2)}) collective-permute-start(bf16[2,256,256]{2,1,0:T(8,128)(2,1)S(1)} %pad_maximum_fusion.1), channel_id=1, source_target_pairs={{0,4},{1,3},{2,6},{3,1},{4,0},{5,7},{6,2},{7,5},{8,12},{9,11},{10,... | collective-permute-start | bytes 786440 | tf_op jit(solution)/shard_map/ppermute | solution.py:357
  72.2 5.1 %collective-permute-start.13 = (bf16[128,512]{1,0:T(8,128)(2,1)S(1)}, bf16[128,512]{1,0:T(8,128)(2,1)S(1)}, u32[]{:S(2)}, u32[]{:S(2)}) collective-permute-start(bf16[128,512]{1,0:T(8,128)(2,1)S(1)} %get-tuple-element.87), channel_id=1, source_target_pairs={{0,64},{1,193},{16,80},{17,209},{32,96},{33,225},{48,112},{49,241}... | collective-permute-start | bytes 393224 | tf_op jit(solution)/shard_map/ppermute | solution.py:357
  77.3 10.4 %collective-permute-start.14 = (bf16[4,256,256]{2,1,0:T(8,128)(2,1)S(1)}, bf16[4,256,256]{2,1,0:T(8,128)(2,1)S(1)}, u32[]{:S(2)}, u32[]{:S(2)}) collective-permute-start(bf16[4,256,256]{2,1,0:T(8,128)(2,1)S(1)} %pad_maximum_fusion.g_ref), channel_id=1, source_target_pairs={{0,12},{1,5},{2,14},{3,7},{4,8},{5,1},{6,10},{7,3},{8,4},{9,13},{1... | collective-permute-start | bytes 1572872 | tf_op jit(solution)/shard_map/ppermute | solution.py:357

commit v6 on v5

--- a/solution.py
+++ b/solution.py
@@ -14,8 +14,8 @@
 ROWS = 512
 VISUAL = 8192
 PIECE = 256
-SUB = 512
-TILE = 1024
+SUB = 1024
+TILES = ((0, 1024), (1024, 1024), (2048, 6144))
 SCALE = DH**-0.5
 C2 = SCALE * 1.4426950408889634
 BIG = 2.0**100
@@ -56,8 +56,8 @@
 
 
 def stats_kernel(
-    mask_hbm, fid_hbm, q_hbm, d_hbm, k_hbm, v_hbm, kw_hbm, vw_hbm, own_ref, ka_hbm, va_hbm, kt_hbm, w_hbm,
-    mask_ref, fid_ref, k_ref, v_ref, w_ref, qt, dt, ka_ref, va_ref, kt_ref, sems, wsem, small, osem,
+    mask_hbm, fid_hbm, q_hbm, d_hbm, k_hbm, v_hbm, kw_hbm, vw_hbm, own_ref, ka_ref, va_ref, kt_ref, w_hbm,
+    mask_ref, fid_ref, k_ref, v_ref, w_ref, qt, dt, sems, wsem, small,
 ):
     af = lax.axis_index("af")
     smalls = [
@@ -71,11 +71,9 @@
             )
         )
     ]
-    for copy in smalls:
-        copy.start()
     loads = []
-    for t in range(VISUAL // TILE):
-        at = pl.ds(t * TILE, TILE)
+    for t, (start, size) in enumerate(TILES):
+        at = pl.ds(start, size)
         loads.append(
             [
                 pltpu.make_async_copy(k_hbm.at[at], k_ref.at[at], sems.at[0, t]),
@@ -84,6 +82,9 @@
         )
         for load in loads[t]:
             load.start()
+        if t == 0:
+            for copy in smalls:
+                copy.start()
     moves = [pltpu.make_async_copy(w.at[:, af], w_ref.at[i], wsem.at[i]) for i, w in enumerate((kw_hbm, vw_hbm))]
     backs = [pltpu.make_async_copy(w_ref.at[i], w_hbm.at[:, i], wsem.at[2 + i]) for i in range(2)]
     for move in moves:
@@ -117,30 +118,12 @@
     o = jnp.zeros((DH, ROWS), F32)
 
     def scores(s):
-        if s % (TILE // SUB) == 0:
-            for load in loads[s // (TILE // SUB)]:
-                load.wait()
+        for (start, _), waits in zip(TILES, loads):
+            if start == s * SUB:
+                for load in waits:
+                    load.wait()
         ka = jnp.concatenate([k_ref[s * SUB:(s + 1) * SUB], marks(s * SUB, SUB, first, last)], axis=1)
         return dot(ka, qt[...], NN) * C2
-
-    outs = [
-        pltpu.make_async_copy(src, dst, osem.at[i])
-        for i, (src, dst) in enumerate(((ka_ref, ka_hbm), (va_ref, va_hbm), (kt_ref, kt_hbm)))
-    ]
-
-    def own_tokens():
-        y, z = lax.axis_index("pb") // 4, lax.axis_index("pb") % 4
-        order = (0, 3 - 2 * af, 1 + 2 * af, 2)
-        for s in range(4):
-            at = slice(s * PIECE, (s + 1) * PIECE)
-            base = y * 2048 + (z ^ order[s]) * 512 + af * 256
-            far = pl.ds(pl.multiple_of(base, 256), PIECE)
-            mark = marks(base, PIECE, first, last)
-            ka_ref[at] = jnp.concatenate([k_ref[far], mark], axis=1)
-            va_ref[at] = jnp.concatenate([v_ref[far], mark], axis=1)
-            kt_ref[:, at] = k_ref[far].T
-        for out in outs:
-            out.start()
 
     later = scores(0)
     for s in range(VISUAL // SUB):
@@ -152,17 +135,25 @@
             for move, back in zip(moves, backs):
                 move.wait()
                 back.start()
-        if s == VISUAL // SUB - 3:
-            own_tokens()
         shrink = jnp.exp2(m - m_new)
         p = jnp.exp2(x - m_new)
         l = l * shrink + jnp.sum(p, axis=0, keepdims=True)
         o = o * shrink + dot(v_ref[s * SUB:(s + 1) * SUB], p.astype(BF16), TN)
         m = m_new
+    y, z = lax.axis_index("pb") // 4, lax.axis_index("pb") % 4
+    order = (0, 3 - 2 * af, 1 + 2 * af, 2)
+    for s in range(4):
+        at = slice(s * PIECE, (s + 1) * PIECE)
+        base = y * 2048 + (z ^ order[s]) * 512 + af * 256
+        far = pl.ds(pl.multiple_of(base, 256), PIECE)
+        mark = marks(base, PIECE, first, last)
+        ka_ref[at] = jnp.concatenate([k_ref[far], mark], axis=1)
+        va_ref[at] = jnp.concatenate([v_ref[far], mark], axis=1)
+        kt_ref[:, at] = k_ref[far].T
     delta = jnp.sum(dt[...].astype(F32) * o, axis=0, keepdims=True) / l
     own_ref[0, TOK:] = stat_rows(top, (m + jnp.log2(l)) * (-1.0 / C2))
     own_ref[1, TOK:] = stat_rows(jnp.zeros((8, ROWS), F32), -delta)
-    for back in backs + outs:
+    for back in backs:
         back.wait()
 
 
@@ -171,7 +162,7 @@
     return pl.pallas_call(
         stats_kernel,
         in_specs=[far] * 8,
-        out_specs=[vmem] + [far] * 4,
+        out_specs=[vmem] * 4 + [far],
         out_shape=[
             jax.ShapeDtypeStruct((2, TOK + 16, ROWS), BF16),
             jax.ShapeDtypeStruct((4 * PIECE, 2 * DH), BF16),
@@ -187,13 +178,9 @@
             pltpu.VMEM((2, 8, 512, DH), BF16),
             pltpu.VMEM((2 * DH, ROWS), BF16),
             pltpu.VMEM((DH, ROWS), BF16),
-            pltpu.VMEM((4 * PIECE, 2 * DH), BF16),
-            pltpu.VMEM((4 * PIECE, 2 * DH), BF16),
-            pltpu.VMEM((DH, 4 * PIECE), BF16),
-            pltpu.SemaphoreType.DMA((2, VISUAL // TILE)),
+            pltpu.SemaphoreType.DMA((2, len(TILES))),
             pltpu.SemaphoreType.DMA((4,)),
             pltpu.SemaphoreType.DMA((4,)),
-            pltpu.SemaphoreType.DMA((3,)),
         ],
         compiler_params=pltpu.CompilerParams(vmem_limit_bytes=VMEM_A << 20),
         cost_estimate=cost(10),

time: 90 us -> 88.5 us (0.983)
  Pallas kernels: 27.3 us -> 25.8 us
    pallas_call x1, Pallas kernels: 11.4 us -> 9.85 us  [softmax_stats(): pl.pallas_call(stats_kernel, in_specs=[far] * 8, out_specs=[vmem] * 4 + [...]
  transfers between devices with their start and end apart: 17 -> 17, of which waited for: 9 -> 9; matrix products, arithmetic and copies ran while one was open for 2% -> 2% of each run, Pallas kernels for 15% -> 16%
where the time goes in v6:
time: 88.5 us; the launch traced here: 88.3 us
  waiting for transfers between devices  29.7 us (34%)
  starting transfers between devices  28.9 us (33%)
  Pallas kernels  25.8 us (29%)
  local copies, waits for them, and re-layouts  1.68 us (2%)
  other arithmetic  1.34 us (2%)
    ppermute x10, waiting for transfers between devices, pair(): lax.ppermute(a, (axis, 'af'), [(2 * i + c, 2 * (i ^ masks[c]) + c) for i...  28.2 us
    ppermute x10, starting transfers between devices, pair(): lax.ppermute(a, (axis, 'af'), [(2 * i + c, 2 * (i ^ masks[c]) + c) for i...  21.5 us
    pallas_call x3, Pallas kernels, visual_token_grads(): pl.pallas_call(functools.partial(grads_kernel, done, len(bundles) // 2, l...  10.5 us
    pallas_call x1, Pallas kernels, softmax_stats(): pl.pallas_call(stats_kernel, in_specs=[far] * 8, out_specs=[vmem] * 4 + [...  9.85 us
    all_to_all x1, starting transfers between devices, on_device(): weights = lax.all_to_all(weights, 'ha', 0, 0, tiled=True)  5.91 us
    pallas_call x2, Pallas kernels, visual_call(): pl.pallas_call(kernel, in_specs=[pl.BlockSpec(memory_space=pltpu.SMEM)] +...  4.75 us
  transfers between devices with their start and end apart: 17, of which 9 were waited for; matrix products, arithmetic and copies ran while one was open for 2% of the time, Pallas kernels for 16%

profile of v6, /device:TPU:32, one launch (start us, length us, event | category | flops | bytes accessed | tf_op | source)
XLA Modules:
  0.0 88.3 jit_solution(10365936592686589518)
XLA Ops:
  0.6 9.8 %softmax_stats.1 = (bf16[2,144,512]{2,1,0:T(8,128)(2,1)}, bf16[1024,256]{1,0:T(8,128)(2,1)}, bf16[1024,256]{1,0:T(8,128)(2,1)}, bf16[128,1024]{1,0:T(8,128)(2,1)}, bf16[8,2,512,128]{3,2,1,0:T(8,128)(2,1)}) custom-call(s32[4,8]{1,0:T(4,128)} %mask_hbm.1, s32[64,128]{1,0:T(8,128)} %bitcast.23, bf16[128,512]{1,0:T(8,128)(2,1)} %q_hbm.1, ...), custom_call_target="tpu_custom_call" | custom-call | flops 11000000512 | bytes 1048576 | tf_op jit(solution)/shard_map/softmax_stats/pallas_call | solution.py:162
  10.5 5.9 %all-to-all-start = ((bf16[8,2,512,128]{3,2,1,0:T(8,128)(2,1)}), bf16[8,2,512,128]{3,2,1,0:T(8,128)(2,1)S(1)}, u32[]{:S(2)}, u32[]{:S(2)}) async-start(bf16[8,2,512,128]{3,2,1,0:T(8,128)(2,1)} %get-tuple-element.71), calls=%async_computation | async-start | bytes 4194304 | tf_op jit(solution)/shard_map/all_to_all | solution.py:359
  16.4 1.7 %collective-permute-start = (bf16[2,144,512]{2,1,0:T(8,128)(2,1)S(1)}, bf16[2,144,512]{2,1,0:T(8,128)(2,1)S(1)}, u32[]{:S(2)}, u32[]{:S(2)}) collective-permute-start(bf16[2,144,512]{2,1,0:T(8,128)(2,1)S(1)} %copy-done), channel_id=1, source_target_pairs={{0,64},{1,193},{16,80},{17,209},{32,96},{33,225},{48,112},{49,241}... | collective-permute-start | bytes 884744 | tf_op jit(solution)/shard_map/ppermute | solution.py:344
  18.1 2.2 %collective-permute-start.1 = (bf16[2,144,512]{2,1,0:T(8,128)(2,1)S(1)}, bf16[2,144,512]{2,1,0:T(8,128)(2,1)S(1)}, u32[]{:S(2)}, u32[]{:S(2)}) collective-permute-start(bf16[2,144,512]{2,1,0:T(8,128)(2,1)S(1)} %copy-done), channel_id=1, source_target_pairs={{0,192},{1,65},{16,208},{17,81},{32,224},{33,97},{48,240},{49,113}... | collective-permute-start | bytes 884744 | tf_op jit(solution)/shard_map/ppermute | solution.py:344
  20.3 0.9 %copy-done.3 = bf16[128,1024]{1,0:T(8,128)(2,1)S(1)} copy-done((bf16[128,1024]{1,0:T(8,128)(2,1)S(1)}, bf16[128,1024]{1,0:T(8,128)(2,1)}, u32[]{:S(2)}) %copy-start.3) | copy-done | bytes 262168
  21.2 2.7 %visual_token_grads_first.1 = (bf16[1,128,512]{2,1,0:T(8,128)(2,1)S(1)}, bf16[1,128,512]{2,1,0:T(8,128)(2,1)S(1)}, f32[1024,128]{1,0:T(8,128)S(1)}, f32[1024,128]{1,0:T(8,128)S(1)}) custom-call(bf16[1024,256]{1,0:T(8,128)(2,1)S(1)} %copy-done.1, bf16[1024,256]{1,0:T(8,128)(2,1)S(1)} %copy-done.2, bf16[128,1024]{1,0:T(8,128)(2,1)S(1)} %copy-done.3, ...), custom_call_target="tpu_custom_call" | custom-call | flops 3520000000 | bytes 1048576 | tf_op jit(solution)/shard_map/visual_token_grads_first/pallas_call | solution.py:251
  24.6 2.5 %collective-permute-done.1.refs_9_ = bf16[2,144,512]{2,1,0:T(8,128)(2,1)S(1)} collective-permute-done((bf16[2,144,512]{2,1,0:T(8,128)(2,1)S(1)}, bf16[2,144,512]{2,1,0:T(8,128)(2,1)S(1)}, u32[]{:S(2)}, u32[]{:S(2)}) %collective-permute-start.1) | collective-permute-done | bytes 294944 | tf_op jit(solution)/shard_map/ppermute | solution.py:344
  27.6 3.0 %collective-permute-start.3 = (bf16[2,144,512]{2,1,0:T(8,128)(2,1)S(1)}, bf16[2,144,512]{2,1,0:T(8,128)(2,1)S(1)}, u32[]{:S(2)}, u32[]{:S(2)}) collective-permute-start(bf16[2,144,512]{2,1,0:T(8,128)(2,1)S(1)} %collective-permute-done.refs_7_), channel_id=1, source_target_pairs={{0,192},{1,65},{16,208},{17,81},{32,224},{33,97},{48,240},{49,113}... | collective-permute-start | bytes 884744 | tf_op jit(solution)/shard_map/ppermute | solution.py:344
  30.6 5.1 %visual_token_grads_second.1 = (bf16[3,128,512]{2,1,0:T(8,128)(2,1)S(1)}, bf16[3,128,512]{2,1,0:T(8,128)(2,1)S(1)}, f32[1024,128]{1,0:T(8,128)S(1)}, f32[1024,128]{1,0:T(8,128)S(1)}) custom-call(bf16[1024,256]{1,0:T(8,128)(2,1)S(1)} %copy-done.1, bf16[1024,256]{1,0:T(8,128)(2,1)S(1)} %copy-done.2, bf16[128,1024]{1,0:T(8,128)(2,1)S(1)} %copy-done.3, ...), custom_call_target="tpu_custom_call" | custom-call | flops 7040000000 | bytes 1048576 | tf_op jit(solution)/shard_map/visual_token_grads_second/pallas_call | solution.py:251
  35.8 1.6 %collective-permute-done.6.refs_8_ = bf16[2,144,512]{2,1,0:T(8,128)(2,1)S(1)} collective-permute-done((bf16[2,144,512]{2,1,0:T(8,128)(2,1)S(1)}, bf16[2,144,512]{2,1,0:T(8,128)(2,1)S(1)}, u32[]{:S(2)}, u32[]{:S(2)}) %collective-permute-start.6) | collective-permute-done | bytes 294944 | tf_op jit(solution)/shard_map/ppermute | solution.py:339
  37.4 2.7 %visual_token_grads_third.1 = (bf16[4,128,512]{2,1,0:T(8,128)(2,1)S(1)}, bf16[4,128,512]{2,1,0:T(8,128)(2,1)S(1)}, bf16[2,256,256]{2,1,0:T(8,128)(2,1)S(1)}, bf16[2,256,256]{2,1,0:T(8,128)(2,1)S(1)}) custom-call(bf16[1024,256]{1,0:T(8,128)(2,1)S(1)} %copy-done.1, bf16[1024,256]{1,0:T(8,128)(2,1)S(1)} %copy-done.2, bf16[128,1024]{1,0:T(8,128)(2,1)S(1)} %copy-done.3, ...), custom_call_target="tpu_custom_call" | custom-call | flops 3520000000 | bytes 1048576 | tf_op jit(solution)/shard_map/visual_token_grads_third/pallas_call | solution.py:251
  40.1 3.4 %collective-permute-start.7 = (bf16[2,256,256]{2,1,0:T(8,128)(2,1)S(1)}, bf16[2,256,256]{2,1,0:T(8,128)(2,1)S(1)}, u32[]{:S(2)}, u32[]{:S(2)}) collective-permute-start(bf16[2,256,256]{2,1,0:T(8,128)(2,1)S(1)} %get-tuple-element.68), channel_id=1, source_target_pairs={{0,16},{1,49},{16,0},{17,33},{32,48},{33,17},{48,32},{49,1},{64,80... | collective-permute-start | bytes 786440 | tf_op jit(solution)/shard_map/ppermute | solution.py:344
  43.4 7.2 %collective-permute-done.7 = bf16[2,256,256]{2,1,0:T(8,128)(2,1)S(1)} collective-permute-done((bf16[2,256,256]{2,1,0:T(8,128)(2,1)S(1)}, bf16[2,256,256]{2,1,0:T(8,128)(2,1)S(1)}, u32[]{:S(2)}, u32[]{:S(2)}) %collective-permute-start.7) | collective-permute-done | bytes 262176 | tf_op jit(solution)/shard_map/ppermute | solution.py:344
  51.6 3.7 %collective-permute-start.8 = (bf16[256,256]{1,0:T(8,128)(2,1)S(1)}, bf16[256,256]{1,0:T(8,128)(2,1)S(1)}, u32[]{:S(2)}, u32[]{:S(2)}) collective-permute-start(bf16[256,256]{1,0:T(8,128)(2,1)S(1)} %fusion.1), channel_id=1, source_target_pairs={{0,48},{1,17},{16,32},{17,1},{32,16},{33,49},{48,0},{49,33},{64,11... | collective-permute-start | bytes 393224 | tf_op jit(solution)/shard_map/ppermute | solution.py:344
  56.2 3.7 %collective-permute-done.8 = bf16[256,256]{1,0:T(8,128)(2,1)S(1)} collective-permute-done((bf16[256,256]{1,0:T(8,128)(2,1)S(1)}, bf16[256,256]{1,0:T(8,128)(2,1)S(1)}, u32[]{:S(2)}, u32[]{:S(2)}) %collective-permute-start.8) | collective-permute-done | bytes 131104 | tf_op jit(solution)/shard_map/ppermute | solution.py:344
  59.9 2.7 %collective-permute-start.11 = (bf16[2,128,512]{2,1,0:T(8,128)(2,1)}, bf16[2,128,512]{2,1,0:T(8,128)(2,1)S(1)}, u32[]{:S(2)}, u32[]{:S(2)}) collective-permute-start(bf16[2,128,512]{2,1,0:T(8,128)(2,1)} %slice.36), channel_id=1, source_target_pairs={{0,192},{1,65},{16,208},{17,81},{32,224},{33,97},{48,240},{49,113}... | collective-permute-start | bytes 786440 | tf_op jit(solution)/shard_map/ppermute | solution.py:344
  62.6 1.0 %fusion.4 = bf16[1,256,256]{2,1,0:T(8,128)(2,1)S(1)} fusion(bf16[256,256]{1,0:T(8,128)(2,1)S(1)} %collective-permute-done.8, bf16[2,256,256]{2,1,0:T(8,128)(2,1)} %copy-done.4, bf16[2,256,256]{2,1,0:T(8,128)(2,1)S(1)} %get-tuple-element.67), kind=kLoop, calls=%fused_computation.11 | loop fusion | flops 393216 | bytes 524288 | tf_op jit(solution)/shard_map/broadcast_in_dim | solution.py:379
  63.7 4.8 %collective-permute-done.10 = bf16[1,256,256]{2,1,0:T(8,128)(2,1)S(1)} collective-permute-done((bf16[1,256,256]{2,1,0:T(8,128)(2,1)S(1)}, bf16[1,256,256]{2,1,0:T(8,128)(2,1)S(1)}, u32[]{:S(2)}, u32[]{:S(2)}) %collective-permute-start.10) | collective-permute-done | bytes 131104 | tf_op jit(solution)/shard_map/ppermute | solution.py:344
  68.6 2.0 %collective-permute-start.12 = (bf16[2,256,256]{2,1,0:T(8,128)(2,1)S(1)}, bf16[2,256,256]{2,1,0:T(8,128)(2,1)S(1)}, u32[]{:S(2)}, u32[]{:S(2)}) collective-permute-start(bf16[2,256,256]{2,1,0:T(8,128)(2,1)S(1)} %pad_maximum_fusion.1), channel_id=1, source_target_pairs={{0,4},{1,3},{2,6},{3,1},{4,0},{5,7},{6,2},{7,5},{8,12},{9,11},{10,... | collective-permute-start | bytes 786440 | tf_op jit(solution)/shard_map/ppermute | solution.py:344
  70.8 4.7 %collective-permute-done.12 = bf16[2,256,256]{2,1,0:T(8,128)(2,1)S(1)} collective-permute-done((bf16[2,256,256]{2,1,0:T(8,128)(2,1)S(1)}, bf16[2,256,256]{2,1,0:T(8,128)(2,1)S(1)}, u32[]{:S(2)}, u32[]{:S(2)}) %collective-permute-start.12) | collective-permute-done | bytes 262176 | tf_op jit(solution)/shard_map/ppermute | solution.py:344
  75.8 2.6 %collective-permute-start.14 = (bf16[4,256,256]{2,1,0:T(8,128)(2,1)S(1)}, bf16[4,256,256]{2,1,0:T(8,128)(2,1)S(1)}, u32[]{:S(2)}, u32[]{:S(2)}) collective-permute-start(bf16[4,256,256]{2,1,0:T(8,128)(2,1)S(1)} %pad_maximum_fusion.g_ref), channel_id=1, source_target_pairs={{0,12},{1,5},{2,14},{3,7},{4,8},{5,1},{6,10},{7,3},{8,4},{9,13},{1... | collective-permute-start | bytes 1572872 | tf_op jit(solution)/shard_map/ppermute | solution.py:344
  79.2 2.6 %visual_early.1 = (f32[2,256,512]{2,1,0:T(8,128)S(1)}, bf16[2,4,512,256]{3,2,1,0:T(8,128)(2,1)S(1)}) custom-call(s32[4]{0:T(128)S(1)} %pad_add_fusion.place, bf16[8,2,512,128]{3,2,1,0:T(8,128)(2,1)S(1)} %all-to-all-done.mine_ref, bf16[8,2,512,128]{3,2,1,0:T(8,128)(2,1)} %collective-permute-done.15.other_ref, bf16[4,256,256]{2,1,0:T(8,128)(2,1)S(1)} %pad_maximum_fusion.g_ref), custom_call_target="tpu_custom_call" | custom-call | flops 2200000000 | bytes 1048576 | tf_op jit(solution)/shard_map/visual_early/pallas_call | solution.py:318
  81.8 4.3 %collective-permute-done.14.g_ref = bf16[4,256,256]{2,1,0:T(8,128)(2,1)S(1)} collective-permute-done((bf16[4,256,256]{2,1,0:T(8,128)(2,1)S(1)}, bf16[4,256,256]{2,1,0:T(8,128)(2,1)S(1)}, u32[]{:S(2)}, u32[]{:S(2)}) %collective-permute-start.14) | collective-permute-done | bytes 524320 | tf_op jit(solution)/shard_map/ppermute | solution.py:344
  86.2 2.1 %visual_late.1 = bf16[256,1024]{1,0:T(8,128)(2,1)} custom-call(s32[4]{0:T(128)S(1)} %pad_add_fusion.place, bf16[2,4,512,256]{3,2,1,0:T(8,128)(2,1)S(1)} %get-tuple-element.83.w_ref, bf16[4,256,256]{2,1,0:T(8,128)(2,1)S(1)} %collective-permute-done.14.g_ref, f32[2,256,512]{2,1,0:T(8,128)S(1)} %get-tuple-element.85.sofar_ref), custom_call_target="tpu_custom_call" | custom-call | flops 2200000000 | bytes 1048576 | tf_op jit(solution)/shard_map/visual_late/pallas_call | solution.py:318
  (35 shorter events, 4.7 us)
Async XLA Ops:
  10.5 5.9 %copy-start = (bf16[2,144,512]{2,1,0:T(8,128)(2,1)S(1)}, bf16[2,144,512]{2,1,0:T(8,128)(2,1)}, u32[]{:S(2)}) copy-start(bf16[2,144,512]{2,1,0:T(8,128)(2,1)} %get-tuple-element.47.refs_3_) | copy-start | bytes 884740
  10.5 9.8 %copy-start.1 = (bf16[1024,256]{1,0:T(8,128)(2,1)S(1)}, bf16[1024,256]{1,0:T(8,128)(2,1)}, u32[]{:S(2)}) copy-start(bf16[1024,256]{1,0:T(8,128)(2,1)} %get-tuple-element.44.refs_0_) | copy-start | bytes 1572868
  10.5 9.8 %copy-start.2 = (bf16[1024,256]{1,0:T(8,128)(2,1)S(1)}, bf16[1024,256]{1,0:T(8,128)(2,1)}, u32[]{:S(2)}) copy-start(bf16[1024,256]{1,0:T(8,128)(2,1)} %get-tuple-element.45.refs_1_) | copy-start | bytes 1572868
  10.5 49.3 %all-to-all-start = ((bf16[8,2,512,128]{3,2,1,0:T(8,128)(2,1)}), bf16[8,2,512,128]{3,2,1,0:T(8,128)(2,1)S(1)}, u32[]{:S(2)}, u32[]{:S(2)}) async-start(bf16[8,2,512,128]{3,2,1,0:T(8,128)(2,1)} %get-tuple-element.71), calls=%async_computation | async-start | bytes 4194304 | tf_op jit(solution)/shard_map/all_to_all | solution.py:359
  16.4 3.8 %collective-permute-start.2 = (bf16[2,144,512]{2,1,0:T(8,128)(2,1)S(1)}, bf16[2,144,512]{2,1,0:T(8,128)(2,1)S(1)}, u32[]{:S(2)}, u32[]{:S(2)}) collective-permute-start(bf16[2,144,512]{2,1,0:T(8,128)(2,1)S(1)} %copy-done), channel_id=1, source_target_pairs={{0,1},{1,0},{2,3},{3,2},{4,5},{5,4},{6,7},{7,6},{8,9},{9,8},{10,11... | collective-permute-start | bytes 884744 | tf_op jit(solution)/shard_map/ppermute | solution.py:339
  16.4 8.2 %collective-permute-start = (bf16[2,144,512]{2,1,0:T(8,128)(2,1)S(1)}, bf16[2,144,512]{2,1,0:T(8,128)(2,1)S(1)}, u32[]{:S(2)}, u32[]{:S(2)}) collective-permute-start(bf16[2,144,512]{2,1,0:T(8,128)(2,1)S(1)} %copy-done), channel_id=1, source_target_pairs={{0,64},{1,193},{16,80},{17,209},{32,96},{33,225},{48,112},{49,241}... | collective-permute-start | bytes 884744 | tf_op jit(solution)/shard_map/ppermute | solution.py:344
  18.1 9.0 %collective-permute-start.1 = (bf16[2,144,512]{2,1,0:T(8,128)(2,1)S(1)}, bf16[2,144,512]{2,1,0:T(8,128)(2,1)S(1)}, u32[]{:S(2)}, u32[]{:S(2)}) collective-permute-start(bf16[2,144,512]{2,1,0:T(8,128)(2,1)S(1)} %copy-done), channel_id=1, source_target_pairs={{0,192},{1,65},{16,208},{17,81},{32,224},{33,97},{48,240},{49,113}... | collective-permute-start | bytes 884744 | tf_op jit(solution)/shard_map/ppermute | solution.py:344
  20.3 1.0 %copy-start.3 = (bf16[128,1024]{1,0:T(8,128)(2,1)S(1)}, bf16[128,1024]{1,0:T(8,128)(2,1)}, u32[]{:S(2)}) copy-start(bf16[128,1024]{1,0:T(8,128)(2,1)} %get-tuple-element.46.refs_2_) | copy-start | bytes 786436
  27.1 3.5 %collective-permute-start.4 = (bf16[2,144,512]{2,1,0:T(8,128)(2,1)S(1)}, bf16[2,144,512]{2,1,0:T(8,128)(2,1)S(1)}, u32[]{:S(2)}, u32[]{:S(2)}) collective-permute-start(bf16[2,144,512]{2,1,0:T(8,128)(2,1)S(1)} %collective-permute-done.refs_7_), channel_id=1, source_target_pairs={{0,1},{1,0},{2,3},{3,2},{4,5},{5,4},{6,7},{7,6},{8,9},{9,8},{10,11... | collective-permute-start | bytes 884744 | tf_op jit(solution)/shard_map/ppermute | solution.py:339
  27.1 3.5 %collective-permute-start.5 = (bf16[2,144,512]{2,1,0:T(8,128)(2,1)S(1)}, bf16[2,144,512]{2,1,0:T(8,128)(2,1)S(1)}, u32[]{:S(2)}, u32[]{:S(2)}) collective-permute-start(bf16[2,144,512]{2,1,0:T(8,128)(2,1)S(1)} %collective-permute-done.1.refs_9_), channel_id=1, source_target_pairs={{0,1},{1,0},{2,3},{3,2},{4,5},{5,4},{6,7},{7,6},{8,9},{9,8},{10,11... | collective-permute-start | bytes 884744 | tf_op jit(solution)/shard_map/ppermute | solution.py:339
  27.6 8.1 %collective-permute-start.3 = (bf16[2,144,512]{2,1,0:T(8,128)(2,1)S(1)}, bf16[2,144,512]{2,1,0:T(8,128)(2,1)S(1)}, u32[]{:S(2)}, u32[]{:S(2)}) collective-permute-start(bf16[2,144,512]{2,1,0:T(8,128)(2,1)S(1)} %collective-permute-done.refs_7_), channel_id=1, source_target_pairs={{0,192},{1,65},{16,208},{17,81},{32,224},{33,97},{48,240},{49,113}... | collective-permute-start | bytes 884744 | tf_op jit(solution)/shard_map/ppermute | solution.py:344
  35.7 1.7 %collective-permute-start.6 = (bf16[2,144,512]{2,1,0:T(8,128)(2,1)S(1)}, bf16[2,144,512]{2,1,0:T(8,128)(2,1)S(1)}, u32[]{:S(2)}, u32[]{:S(2)}) collective-permute-start(bf16[2,144,512]{2,1,0:T(8,128)(2,1)S(1)} %collective-permute-done.3.refs_7_), channel_id=1, source_target_pairs={{0,1},{1,0},{2,3},{3,2},{4,5},{5,4},{6,7},{7,6},{8,9},{9,8},{10,11... | collective-permute-start | bytes 884744 | tf_op jit(solution)/shard_map/ppermute | solution.py:339
  40.1 10.6 %collective-permute-start.7 = (bf16[2,256,256]{2,1,0:T(8,128)(2,1)S(1)}, bf16[2,256,256]{2,1,0:T(8,128)(2,1)S(1)}, u32[]{:S(2)}, u32[]{:S(2)}) collective-permute-start(bf16[2,256,256]{2,1,0:T(8,128)(2,1)S(1)} %get-tuple-element.68), channel_id=1, source_target_pairs={{0,16},{1,49},{16,0},{17,33},{32,48},{33,17},{48,32},{49,1},{64,80... | collective-permute-start | bytes 786440 | tf_op jit(solution)/shard_map/ppermute | solution.py:344
  50.6 4.7 %copy-start.4 = (bf16[2,256,256]{2,1,0:T(8,128)(2,1)}, bf16[2,256,256]{2,1,0:T(8,128)(2,1)S(1)}, u32[]{:S(2)}) copy-start(bf16[2,256,256]{2,1,0:T(8,128)(2,1)S(1)} %collective-permute-done.7) | copy-start | bytes 786436
  50.6 4.7 %collective-permute-start.9 = (bf16[4,128,512]{2,1,0:T(8,128)(2,1)S(1)}, bf16[4,128,512]{2,1,0:T(8,128)(2,1)S(1)}, u32[]{:S(2)}, u32[]{:S(2)}) collective-permute-start(bf16[4,128,512]{2,1,0:T(8,128)(2,1)S(1)} %get-tuple-element.73), channel_id=1, source_target_pairs={{0,1},{1,0},{2,3},{3,2},{4,5},{5,4},{6,7},{7,6},{8,9},{9,8},{10,11... | collective-permute-start | bytes 1572872 | tf_op jit(solution)/shard_map/ppermute | solution.py:339
  51.6 8.3 %collective-permute-start.8 = (bf16[256,256]{1,0:T(8,128)(2,1)S(1)}, bf16[256,256]{1,0:T(8,128)(2,1)S(1)}, u32[]{:S(2)}, u32[]{:S(2)}) collective-permute-start(bf16[256,256]{1,0:T(8,128)(2,1)S(1)} %fusion.1), channel_id=1, source_target_pairs={{0,48},{1,17},{16,32},{17,1},{32,16},{33,49},{48,0},{49,33},{64,11... | collective-permute-start | bytes 393224 | tf_op jit(solution)/shard_map/ppermute | solution.py:344
  59.9 19.4 %collective-permute-start.15 = (bf16[8,2,512,128]{3,2,1,0:T(8,128)(2,1)S(1)}, bf16[8,2,512,128]{3,2,1,0:T(8,128)(2,1)}, u32[]{:S(2)}, u32[]{:S(2)}) collective-permute-start(bf16[8,2,512,128]{3,2,1,0:T(8,128)(2,1)S(1)} %all-to-all-done.mine_ref), channel_id=1, source_target_pairs={{0,1},{1,0},{2,3},{3,2},{4,5},{5,4},{6,7},{7,6},{8,9},{9,8},{10,11... | collective-permute-start | bytes 6291464 | tf_op jit(solution)/shard_map/ppermute | solution.py:339
  59.9 8.7 %collective-permute-start.11 = (bf16[2,128,512]{2,1,0:T(8,128)(2,1)}, bf16[2,128,512]{2,1,0:T(8,128)(2,1)S(1)}, u32[]{:S(2)}, u32[]{:S(2)}) collective-permute-start(bf16[2,128,512]{2,1,0:T(8,128)(2,1)} %slice.36), channel_id=1, source_target_pairs={{0,192},{1,65},{16,208},{17,81},{32,224},{33,97},{48,240},{49,113}... | collective-permute-start | bytes 786440 | tf_op jit(solution)/shard_map/ppermute | solution.py:344
  63.5 5.1 %collective-permute-start.10 = (bf16[1,256,256]{2,1,0:T(8,128)(2,1)S(1)}, bf16[1,256,256]{2,1,0:T(8,128)(2,1)S(1)}, u32[]{:S(2)}, u32[]{:S(2)}) collective-permute-start(bf16[1,256,256]{2,1,0:T(8,128)(2,1)S(1)} %fusion.4), channel_id=1, source_target_pairs={{0,2},{1,13},{2,0},{3,15},{4,6},{5,9},{6,4},{7,11},{8,10},{9,5},{1... | collective-permute-start | bytes 393224 | tf_op jit(solution)/shard_map/ppermute | solution.py:344
  68.6 6.9 %collective-permute-start.12 = (bf16[2,256,256]{2,1,0:T(8,128)(2,1)S(1)}, bf16[2,256,256]{2,1,0:T(8,128)(2,1)S(1)}, u32[]{:S(2)}, u32[]{:S(2)}) collective-permute-start(bf16[2,256,256]{2,1,0:T(8,128)(2,1)S(1)} %pad_maximum_fusion.1), channel_id=1, source_target_pairs={{0,4},{1,3},{2,6},{3,1},{4,0},{5,7},{6,2},{7,5},{8,12},{9,11},{10,... | collective-permute-start | bytes 786440 | tf_op jit(solution)/shard_map/ppermute | solution.py:344
  70.7 5.1 %collective-permute-start.13 = (bf16[128,512]{1,0:T(8,128)(2,1)S(1)}, bf16[128,512]{1,0:T(8,128)(2,1)S(1)}, u32[]{:S(2)}, u32[]{:S(2)}) collective-permute-start(bf16[128,512]{1,0:T(8,128)(2,1)S(1)} %get-tuple-element.87), channel_id=1, source_target_pairs={{0,64},{1,193},{16,80},{17,209},{32,96},{33,225},{48,112},{49,241}... | collective-permute-start | bytes 393224 | tf_op jit(solution)/shard_map/ppermute | solution.py:344
  75.8 10.4 %collective-permute-start.14 = (bf16[4,256,256]{2,1,0:T(8,128)(2,1)S(1)}, bf16[4,256,256]{2,1,0:T(8,128)(2,1)S(1)}, u32[]{:S(2)}, u32[]{:S(2)}) collective-permute-start(bf16[4,256,256]{2,1,0:T(8,128)(2,1)S(1)} %pad_maximum_fusion.g_ref), channel_id=1, source_target_pairs={{0,12},{1,5},{2,14},{3,7},{4,8},{5,1},{6,10},{7,3},{8,4},{9,13},{1... | collective-permute-start | bytes 1572872 | tf_op jit(solution)/shard_map/ppermute | solution.py:344

commit v7 on v6

--- a/solution.py
+++ b/solution.py
@@ -374,12 +374,12 @@
     got, qother = tie((got, qother))
     qpart = plus(qown, swap_cores(qother))
     got2 = pair(plus(keep[1], got[1]), "pb", (3, 1))
-    got2, weights, qgot_in = tie((got2, weights, qpart[2:]))
+    got2, qgot_in = tie((got2, qpart[2:]))
     qgot = pair(qgot_in, "pb", (12, 4))
     g = plus(keep[0], got[0], got2)[None]
+    g = jnp.concatenate([g, pair(g, "ha", (1, 6))], axis=0)
+    g, qgot, weights = tie((g, qgot, weights))
     weights2 = swap_cores(weights)
-    g = jnp.concatenate([g, pair(g, "ha", (1, 6))], axis=0)
-    g, qgot = tie((g, qgot))
     qgot2 = pair(plus(qpart[1], qgot[1]), "pb", (4, 12))
     g = jnp.concatenate([g, pair(g, "ha", (2, 1))], axis=0)
     g, qgot2 = tie((g, qgot2))

time: 88.5 us -> 88.1 us (level)
  waiting for transfers between devices: 29.7 us -> 28.5 us
  starting transfers between devices: 28.9 us -> 30 us
    ppermute x10, waiting for transfers between devices: 28.2 us -> 27 us  [pair(): lax.ppermute(a, (axis, 'af'), [(2 * i + c, 2 * (i ^ masks[c]) + c) for i...]
    ppermute x6, starting transfers between devices: 1.49 us -> 2.61 us  [swap_cores(): return lax.ppermute(a, 'af', [(0, 1), (1, 0)])]
    concatenate x1, other arithmetic: 0.05 us -> 1 us  [on_device(): g = jnp.concatenate([g, pair(g, 'ha', (2, 1))], axis=0)]
    broadcast_in_dim x1, other arithmetic: 0.95 us -> 0.05 us  [on_device(): g = plus(keep[0], got[0], got2)[None]]
  transfers between devices with their start and end apart: 17 -> 17, of which waited for: 9 -> 8; matrix products, arithmetic and copies ran while one was open for 2% -> 2% of each run, Pallas kernels for 16% -> 16%
where the time goes in v7:
time: 88.1 us; the launch traced here: 87.7 us
  starting transfers between devices  30 us (34%)
  waiting for transfers between devices  28.5 us (32%)
  Pallas kernels  25.8 us (29%)
  other arithmetic  1.39 us (2%)
  local copies, waits for them, and re-layouts  1.07 us (1%)
    ppermute x10, waiting for transfers between devices, pair(): lax.ppermute(a, (axis, 'af'), [(2 * i + c, 2 * (i ^ masks[c]) + c) for i...  27 us
    ppermute x10, starting transfers between devices, pair(): lax.ppermute(a, (axis, 'af'), [(2 * i + c, 2 * (i ^ masks[c]) + c) for i...  21.5 us
    pallas_call x3, Pallas kernels, visual_token_grads(): pl.pallas_call(functools.partial(grads_kernel, done, len(bundles) // 2, l...  10.5 us
    pallas_call x1, Pallas kernels, softmax_stats(): pl.pallas_call(stats_kernel, in_specs=[far] * 8, out_specs=[vmem] * 4 + [...  9.85 us
    all_to_all x1, starting transfers between devices, on_device(): weights = lax.all_to_all(weights, 'ha', 0, 0, tiled=True)  5.91 us
    pallas_call x2, Pallas kernels, visual_call(): pl.pallas_call(kernel, in_specs=[pl.BlockSpec(memory_space=pltpu.SMEM)] +...  4.74 us
    ppermute x6, starting transfers between devices, swap_cores(): return lax.ppermute(a, 'af', [(0, 1), (1, 0)])  2.61 us
  transfers between devices with their start and end apart: 17, of which 8 were waited for; matrix products, arithmetic and copies ran while one was open for 2% of the time, Pallas kernels for 16%

profile of v7, /device:TPU:32, one launch (start us, length us, event | category | flops | bytes accessed | tf_op | source)
XLA Modules:
  0.0 87.7 jit_solution(5015571449760100681)
XLA Ops:
  0.6 9.8 %softmax_stats.1 = (bf16[2,144,512]{2,1,0:T(8,128)(2,1)}, bf16[1024,256]{1,0:T(8,128)(2,1)}, bf16[1024,256]{1,0:T(8,128)(2,1)}, bf16[128,1024]{1,0:T(8,128)(2,1)}, bf16[8,2,512,128]{3,2,1,0:T(8,128)(2,1)}) custom-call(s32[4,8]{1,0:T(4,128)} %mask_hbm.1, s32[64,128]{1,0:T(8,128)} %bitcast.23, bf16[128,512]{1,0:T(8,128)(2,1)} %q_hbm.1, ...), custom_call_target="tpu_custom_call" | custom-call | flops 11000000512 | bytes 1048576 | tf_op jit(solution)/shard_map/softmax_stats/pallas_call | solution.py:162
  10.6 5.9 %all-to-all-start = ((bf16[8,2,512,128]{3,2,1,0:T(8,128)(2,1)}), bf16[8,2,512,128]{3,2,1,0:T(8,128)(2,1)S(1)}, u32[]{:S(2)}, u32[]{:S(2)}) async-start(bf16[8,2,512,128]{3,2,1,0:T(8,128)(2,1)} %get-tuple-element.75), calls=%async_computation | async-start | bytes 4194304 | tf_op jit(solution)/shard_map/all_to_all | solution.py:359
  16.5 1.6 %collective-permute-start = (bf16[2,144,512]{2,1,0:T(8,128)(2,1)S(1)}, bf16[2,144,512]{2,1,0:T(8,128)(2,1)S(1)}, u32[]{:S(2)}, u32[]{:S(2)}) collective-permute-start(bf16[2,144,512]{2,1,0:T(8,128)(2,1)S(1)} %copy-done), channel_id=1, source_target_pairs={{0,64},{1,193},{16,80},{17,209},{32,96},{33,225},{48,112},{49,241}... | collective-permute-start | bytes 884744 | tf_op jit(solution)/shard_map/ppermute | solution.py:344
  18.1 2.2 %collective-permute-start.1 = (bf16[2,144,512]{2,1,0:T(8,128)(2,1)S(1)}, bf16[2,144,512]{2,1,0:T(8,128)(2,1)S(1)}, u32[]{:S(2)}, u32[]{:S(2)}) collective-permute-start(bf16[2,144,512]{2,1,0:T(8,128)(2,1)S(1)} %copy-done), channel_id=1, source_target_pairs={{0,192},{1,65},{16,208},{17,81},{32,224},{33,97},{48,240},{49,113}... | collective-permute-start | bytes 884744 | tf_op jit(solution)/shard_map/ppermute | solution.py:344
  21.3 2.7 %visual_token_grads_first.1 = (bf16[1,128,512]{2,1,0:T(8,128)(2,1)S(1)}, bf16[1,128,512]{2,1,0:T(8,128)(2,1)S(1)}, f32[1024,128]{1,0:T(8,128)S(1)}, f32[1024,128]{1,0:T(8,128)S(1)}) custom-call(bf16[1024,256]{1,0:T(8,128)(2,1)S(1)} %copy-done.1, bf16[1024,256]{1,0:T(8,128)(2,1)S(1)} %copy-done.2, bf16[128,1024]{1,0:T(8,128)(2,1)S(1)} %copy-done.3, ...), custom_call_target="tpu_custom_call" | custom-call | flops 3520000000 | bytes 1048576 | tf_op jit(solution)/shard_map/visual_token_grads_first/pallas_call | solution.py:251
  24.0 1.2 %collective-permute-done.refs_7_ = bf16[2,144,512]{2,1,0:T(8,128)(2,1)S(1)} collective-permute-done((bf16[2,144,512]{2,1,0:T(8,128)(2,1)S(1)}, bf16[2,144,512]{2,1,0:T(8,128)(2,1)S(1)}, u32[]{:S(2)}, u32[]{:S(2)}) %collective-permute-start) | collective-permute-done | bytes 294944 | tf_op jit(solution)/shard_map/ppermute | solution.py:344
  25.2 1.4 %collective-permute-done.1.refs_9_ = bf16[2,144,512]{2,1,0:T(8,128)(2,1)S(1)} collective-permute-done((bf16[2,144,512]{2,1,0:T(8,128)(2,1)S(1)}, bf16[2,144,512]{2,1,0:T(8,128)(2,1)S(1)}, u32[]{:S(2)}, u32[]{:S(2)}) %collective-permute-start.1) | collective-permute-done | bytes 294944 | tf_op jit(solution)/shard_map/ppermute | solution.py:344
  27.1 3.0 %collective-permute-start.3 = (bf16[2,144,512]{2,1,0:T(8,128)(2,1)S(1)}, bf16[2,144,512]{2,1,0:T(8,128)(2,1)S(1)}, u32[]{:S(2)}, u32[]{:S(2)}) collective-permute-start(bf16[2,144,512]{2,1,0:T(8,128)(2,1)S(1)} %collective-permute-done.refs_7_), channel_id=1, source_target_pairs={{0,192},{1,65},{16,208},{17,81},{32,224},{33,97},{48,240},{49,113}... | collective-permute-start | bytes 884744 | tf_op jit(solution)/shard_map/ppermute | solution.py:344
  30.1 5.1 %visual_token_grads_second.1 = (bf16[3,128,512]{2,1,0:T(8,128)(2,1)S(1)}, bf16[3,128,512]{2,1,0:T(8,128)(2,1)S(1)}, f32[1024,128]{1,0:T(8,128)S(1)}, f32[1024,128]{1,0:T(8,128)S(1)}) custom-call(bf16[1024,256]{1,0:T(8,128)(2,1)S(1)} %copy-done.1, bf16[1024,256]{1,0:T(8,128)(2,1)S(1)} %copy-done.2, bf16[128,1024]{1,0:T(8,128)(2,1)S(1)} %copy-done.3, ...), custom_call_target="tpu_custom_call" | custom-call | flops 7040000000 | bytes 1048576 | tf_op jit(solution)/shard_map/visual_token_grads_second/pallas_call | solution.py:251
  35.3 1.6 %collective-permute-done.6.refs_8_ = bf16[2,144,512]{2,1,0:T(8,128)(2,1)S(1)} collective-permute-done((bf16[2,144,512]{2,1,0:T(8,128)(2,1)S(1)}, bf16[2,144,512]{2,1,0:T(8,128)(2,1)S(1)}, u32[]{:S(2)}, u32[]{:S(2)}) %collective-permute-start.6) | collective-permute-done | bytes 294944 | tf_op jit(solution)/shard_map/ppermute | solution.py:339
  36.9 2.7 %visual_token_grads_third.1 = (bf16[4,128,512]{2,1,0:T(8,128)(2,1)S(1)}, bf16[4,128,512]{2,1,0:T(8,128)(2,1)S(1)}, bf16[2,256,256]{2,1,0:T(8,128)(2,1)S(1)}, bf16[2,256,256]{2,1,0:T(8,128)(2,1)S(1)}) custom-call(bf16[1024,256]{1,0:T(8,128)(2,1)S(1)} %copy-done.1, bf16[1024,256]{1,0:T(8,128)(2,1)S(1)} %copy-done.2, bf16[128,1024]{1,0:T(8,128)(2,1)S(1)} %copy-done.3, ...), custom_call_target="tpu_custom_call" | custom-call | flops 3520000000 | bytes 1048576 | tf_op jit(solution)/shard_map/visual_token_grads_third/pallas_call | solution.py:251
  39.6 3.4 %collective-permute-start.7 = (bf16[2,256,256]{2,1,0:T(8,128)(2,1)S(1)}, bf16[2,256,256]{2,1,0:T(8,128)(2,1)S(1)}, u32[]{:S(2)}, u32[]{:S(2)}) collective-permute-start(bf16[2,256,256]{2,1,0:T(8,128)(2,1)S(1)} %get-tuple-element.68), channel_id=1, source_target_pairs={{0,16},{1,49},{16,0},{17,33},{32,48},{33,17},{48,32},{49,1},{64,80... | collective-permute-start | bytes 786440 | tf_op jit(solution)/shard_map/ppermute | solution.py:344
  42.9 6.6 %collective-permute-done.7 = bf16[2,256,256]{2,1,0:T(8,128)(2,1)S(1)} collective-permute-done((bf16[2,256,256]{2,1,0:T(8,128)(2,1)S(1)}, bf16[2,256,256]{2,1,0:T(8,128)(2,1)S(1)}, u32[]{:S(2)}, u32[]{:S(2)}) %collective-permute-start.7) | collective-permute-done | bytes 262176 | tf_op jit(solution)/shard_map/ppermute | solution.py:344
  49.5 1.8 %collective-permute-start.9 = (bf16[4,128,512]{2,1,0:T(8,128)(2,1)S(1)}, bf16[4,128,512]{2,1,0:T(8,128)(2,1)S(1)}, u32[]{:S(2)}, u32[]{:S(2)}) collective-permute-start(bf16[4,128,512]{2,1,0:T(8,128)(2,1)S(1)} %get-tuple-element.72), channel_id=1, source_target_pairs={{0,1},{1,0},{2,3},{3,2},{4,5},{5,4},{6,7},{7,6},{8,9},{9,8},{10,11... | collective-permute-start | bytes 1572872 | tf_op jit(solution)/shard_map/ppermute | solution.py:339
  51.3 3.7 %collective-permute-start.8 = (bf16[256,256]{1,0:T(8,128)(2,1)S(1)}, bf16[256,256]{1,0:T(8,128)(2,1)S(1)}, u32[]{:S(2)}, u32[]{:S(2)}) collective-permute-start(bf16[256,256]{1,0:T(8,128)(2,1)S(1)} %fusion.1), channel_id=1, source_target_pairs={{0,48},{1,17},{16,32},{17,1},{32,16},{33,49},{48,0},{49,33},{64,11... | collective-permute-start | bytes 393224 | tf_op jit(solution)/shard_map/ppermute | solution.py:344
  55.2 4.4 %collective-permute-done.8 = bf16[256,256]{1,0:T(8,128)(2,1)S(1)} collective-permute-done((bf16[256,256]{1,0:T(8,128)(2,1)S(1)}, bf16[256,256]{1,0:T(8,128)(2,1)S(1)}, u32[]{:S(2)}, u32[]{:S(2)}) %collective-permute-start.8) | collective-permute-done | bytes 131104 | tf_op jit(solution)/shard_map/ppermute | solution.py:344
  59.6 2.7 %collective-permute-start.11 = (bf16[2,128,512]{2,1,0:T(8,128)(2,1)S(1)}, bf16[2,128,512]{2,1,0:T(8,128)(2,1)S(1)}, u32[]{:S(2)}, u32[]{:S(2)}) collective-permute-start(bf16[2,128,512]{2,1,0:T(8,128)(2,1)S(1)} %slice.36), channel_id=1, source_target_pairs={{0,192},{1,65},{16,208},{17,81},{32,224},{33,97},{48,240},{49,113}... | collective-permute-start | bytes 786440 | tf_op jit(solution)/shard_map/ppermute | solution.py:344
  62.6 4.8 %collective-permute-done.10 = bf16[1,256,256]{2,1,0:T(8,128)(2,1)S(1)} collective-permute-done((bf16[1,256,256]{2,1,0:T(8,128)(2,1)S(1)}, bf16[1,256,256]{2,1,0:T(8,128)(2,1)S(1)}, u32[]{:S(2)}, u32[]{:S(2)}) %collective-permute-start.10) | collective-permute-done | bytes 131104 | tf_op jit(solution)/shard_map/ppermute | solution.py:344
  67.6 1.7 %collective-permute-start.12 = (bf16[2,256,256]{2,1,0:T(8,128)(2,1)S(1)}, bf16[2,256,256]{2,1,0:T(8,128)(2,1)S(1)}, u32[]{:S(2)}, u32[]{:S(2)}) collective-permute-start(bf16[2,256,256]{2,1,0:T(8,128)(2,1)S(1)} %pad_maximum_fusion.1), channel_id=1, source_target_pairs={{0,4},{1,3},{2,6},{3,1},{4,0},{5,7},{6,2},{7,5},{8,12},{9,11},{10,... | collective-permute-start | bytes 786440 | tf_op jit(solution)/shard_map/ppermute | solution.py:344
  69.5 4.5 %collective-permute-done.12 = bf16[2,256,256]{2,1,0:T(8,128)(2,1)S(1)} collective-permute-done((bf16[2,256,256]{2,1,0:T(8,128)(2,1)S(1)}, bf16[2,256,256]{2,1,0:T(8,128)(2,1)S(1)}, u32[]{:S(2)}, u32[]{:S(2)}) %collective-permute-start.12) | collective-permute-done | bytes 262176 | tf_op jit(solution)/shard_map/ppermute | solution.py:344
  75.1 3.0 %collective-permute-start.14 = (bf16[4,256,256]{2,1,0:T(8,128)(2,1)S(1)}, bf16[4,256,256]{2,1,0:T(8,128)(2,1)S(1)}, u32[]{:S(2)}, u32[]{:S(2)}) collective-permute-start(bf16[4,256,256]{2,1,0:T(8,128)(2,1)S(1)} %pad_maximum_fusion.g_ref), channel_id=1, source_target_pairs={{0,12},{1,5},{2,14},{3,7},{4,8},{5,1},{6,10},{7,3},{8,4},{9,13},{1... | collective-permute-start | bytes 1572872 | tf_op jit(solution)/shard_map/ppermute | solution.py:344
  78.9 2.6 %visual_early.1 = (f32[2,256,512]{2,1,0:T(8,128)S(1)}, bf16[2,4,512,256]{3,2,1,0:T(8,128)(2,1)S(1)}) custom-call(s32[4]{0:T(128)S(1)} %pad_add_fusion.place, bf16[8,2,512,128]{3,2,1,0:T(8,128)(2,1)S(1)} %all-to-all-done.mine_ref, bf16[8,2,512,128]{3,2,1,0:T(8,128)(2,1)} %collective-permute-done.15.other_ref, bf16[4,256,256]{2,1,0:T(8,128)(2,1)S(1)} %pad_maximum_fusion.g_ref), custom_call_target="tpu_custom_call" | custom-call | flops 2200000000 | bytes 1048576 | tf_op jit(solution)/shard_map/visual_early/pallas_call | solution.py:318
  81.5 4.1 %collective-permute-done.14.g_ref = bf16[4,256,256]{2,1,0:T(8,128)(2,1)S(1)} collective-permute-done((bf16[4,256,256]{2,1,0:T(8,128)(2,1)S(1)}, bf16[4,256,256]{2,1,0:T(8,128)(2,1)S(1)}, u32[]{:S(2)}, u32[]{:S(2)}) %collective-permute-start.14) | collective-permute-done | bytes 524320 | tf_op jit(solution)/shard_map/ppermute | solution.py:344
  85.5 2.1 %visual_late.1 = bf16[256,1024]{1,0:T(8,128)(2,1)} custom-call(s32[4]{0:T(128)S(1)} %pad_add_fusion.place, bf16[2,4,512,256]{3,2,1,0:T(8,128)(2,1)S(1)} %get-tuple-element.83.w_ref, bf16[4,256,256]{2,1,0:T(8,128)(2,1)S(1)} %collective-permute-done.14.g_ref, f32[2,256,512]{2,1,0:T(8,128)S(1)} %get-tuple-element.85.sofar_ref), custom_call_target="tpu_custom_call" | custom-call | flops 2200000000 | bytes 1048576 | tf_op jit(solution)/shard_map/visual_late/pallas_call | solution.py:318
  (35 shorter events, 4.4 us)
Async XLA Ops:
  10.5 9.8 %collective-permute-start.2 = (bf16[2,144,512]{2,1,0:T(8,128)(2,1)}, bf16[2,144,512]{2,1,0:T(8,128)(2,1)S(1)}, u32[]{:S(2)}, u32[]{:S(2)}) collective-permute-start(bf16[2,144,512]{2,1,0:T(8,128)(2,1)} %get-tuple-element.47.refs_3_), channel_id=1, source_target_pairs={{0,1},{1,0},{2,3},{3,2},{4,5},{5,4},{6,7},{7,6},{8,9},{9,8},{10,11... | collective-permute-start | bytes 884744 | tf_op jit(solution)/shard_map/ppermute | solution.py:339
  10.6 5.9 %copy-start = (bf16[2,144,512]{2,1,0:T(8,128)(2,1)S(1)}, bf16[2,144,512]{2,1,0:T(8,128)(2,1)}, u32[]{:S(2)}) copy-start(bf16[2,144,512]{2,1,0:T(8,128)(2,1)} %get-tuple-element.47.refs_3_) | copy-start | bytes 884740
  10.6 9.7 %copy-start.1 = (bf16[1024,256]{1,0:T(8,128)(2,1)S(1)}, bf16[1024,256]{1,0:T(8,128)(2,1)}, u32[]{:S(2)}) copy-start(bf16[1024,256]{1,0:T(8,128)(2,1)} %get-tuple-element.44.refs_0_) | copy-start | bytes 1572868
  10.6 9.7 %copy-start.3 = (bf16[128,1024]{1,0:T(8,128)(2,1)S(1)}, bf16[128,1024]{1,0:T(8,128)(2,1)}, u32[]{:S(2)}) copy-start(bf16[128,1024]{1,0:T(8,128)(2,1)} %get-tuple-element.46.refs_2_) | copy-start | bytes 786436
  10.6 56.9 %all-to-all-start = ((bf16[8,2,512,128]{3,2,1,0:T(8,128)(2,1)}), bf16[8,2,512,128]{3,2,1,0:T(8,128)(2,1)S(1)}, u32[]{:S(2)}, u32[]{:S(2)}) async-start(bf16[8,2,512,128]{3,2,1,0:T(8,128)(2,1)} %get-tuple-element.75), calls=%async_computation | async-start | bytes 4194304 | tf_op jit(solution)/shard_map/all_to_all | solution.py:359
  16.5 8.7 %collective-permute-start = (bf16[2,144,512]{2,1,0:T(8,128)(2,1)S(1)}, bf16[2,144,512]{2,1,0:T(8,128)(2,1)S(1)}, u32[]{:S(2)}, u32[]{:S(2)}) collective-permute-start(bf16[2,144,512]{2,1,0:T(8,128)(2,1)S(1)} %copy-done), channel_id=1, source_target_pairs={{0,64},{1,193},{16,80},{17,209},{32,96},{33,225},{48,112},{49,241}... | collective-permute-start | bytes 884744 | tf_op jit(solution)/shard_map/ppermute | solution.py:344
  18.1 8.5 %collective-permute-start.1 = (bf16[2,144,512]{2,1,0:T(8,128)(2,1)S(1)}, bf16[2,144,512]{2,1,0:T(8,128)(2,1)S(1)}, u32[]{:S(2)}, u32[]{:S(2)}) collective-permute-start(bf16[2,144,512]{2,1,0:T(8,128)(2,1)S(1)} %copy-done), channel_id=1, source_target_pairs={{0,192},{1,65},{16,208},{17,81},{32,224},{33,97},{48,240},{49,113}... | collective-permute-start | bytes 884744 | tf_op jit(solution)/shard_map/ppermute | solution.py:344
  20.3 1.0 %copy-start.2 = (bf16[1024,256]{1,0:T(8,128)(2,1)S(1)}, bf16[1024,256]{1,0:T(8,128)(2,1)}, u32[]{:S(2)}) copy-start(bf16[1024,256]{1,0:T(8,128)(2,1)} %get-tuple-element.45.refs_1_) | copy-start | bytes 1572868
  26.6 3.5 %collective-permute-start.4 = (bf16[2,144,512]{2,1,0:T(8,128)(2,1)S(1)}, bf16[2,144,512]{2,1,0:T(8,128)(2,1)S(1)}, u32[]{:S(2)}, u32[]{:S(2)}) collective-permute-start(bf16[2,144,512]{2,1,0:T(8,128)(2,1)S(1)} %collective-permute-done.refs_7_), channel_id=1, source_target_pairs={{0,1},{1,0},{2,3},{3,2},{4,5},{5,4},{6,7},{7,6},{8,9},{9,8},{10,11... | collective-permute-start | bytes 884744 | tf_op jit(solution)/shard_map/ppermute | solution.py:339
  26.6 3.5 %collective-permute-start.5 = (bf16[2,144,512]{2,1,0:T(8,128)(2,1)S(1)}, bf16[2,144,512]{2,1,0:T(8,128)(2,1)S(1)}, u32[]{:S(2)}, u32[]{:S(2)}) collective-permute-start(bf16[2,144,512]{2,1,0:T(8,128)(2,1)S(1)} %collective-permute-done.1.refs_9_), channel_id=1, source_target_pairs={{0,1},{1,0},{2,3},{3,2},{4,5},{5,4},{6,7},{7,6},{8,9},{9,8},{10,11... | collective-permute-start | bytes 884744 | tf_op jit(solution)/shard_map/ppermute | solution.py:339
  27.1 8.1 %collective-permute-start.3 = (bf16[2,144,512]{2,1,0:T(8,128)(2,1)S(1)}, bf16[2,144,512]{2,1,0:T(8,128)(2,1)S(1)}, u32[]{:S(2)}, u32[]{:S(2)}) collective-permute-start(bf16[2,144,512]{2,1,0:T(8,128)(2,1)S(1)} %collective-permute-done.refs_7_), channel_id=1, source_target_pairs={{0,192},{1,65},{16,208},{17,81},{32,224},{33,97},{48,240},{49,113}... | collective-permute-start | bytes 884744 | tf_op jit(solution)/shard_map/ppermute | solution.py:344
  35.2 1.7 %collective-permute-start.6 = (bf16[2,144,512]{2,1,0:T(8,128)(2,1)S(1)}, bf16[2,144,512]{2,1,0:T(8,128)(2,1)S(1)}, u32[]{:S(2)}, u32[]{:S(2)}) collective-permute-start(bf16[2,144,512]{2,1,0:T(8,128)(2,1)S(1)} %collective-permute-done.3.refs_7_), channel_id=1, source_target_pairs={{0,1},{1,0},{2,3},{3,2},{4,5},{5,4},{6,7},{7,6},{8,9},{9,8},{10,11... | collective-permute-start | bytes 884744 | tf_op jit(solution)/shard_map/ppermute | solution.py:339
  39.6 9.9 %collective-permute-start.7 = (bf16[2,256,256]{2,1,0:T(8,128)(2,1)S(1)}, bf16[2,256,256]{2,1,0:T(8,128)(2,1)S(1)}, u32[]{:S(2)}, u32[]{:S(2)}) collective-permute-start(bf16[2,256,256]{2,1,0:T(8,128)(2,1)S(1)} %get-tuple-element.68), channel_id=1, source_target_pairs={{0,16},{1,49},{16,0},{17,33},{32,48},{33,17},{48,32},{49,1},{64,80... | collective-permute-start | bytes 786440 | tf_op jit(solution)/shard_map/ppermute | solution.py:344
  49.5 5.6 %collective-permute-start.9 = (bf16[4,128,512]{2,1,0:T(8,128)(2,1)S(1)}, bf16[4,128,512]{2,1,0:T(8,128)(2,1)S(1)}, u32[]{:S(2)}, u32[]{:S(2)}) collective-permute-start(bf16[4,128,512]{2,1,0:T(8,128)(2,1)S(1)} %get-tuple-element.72), channel_id=1, source_target_pairs={{0,1},{1,0},{2,3},{3,2},{4,5},{5,4},{6,7},{7,6},{8,9},{9,8},{10,11... | collective-permute-start | bytes 1572872 | tf_op jit(solution)/shard_map/ppermute | solution.py:339
  51.3 8.3 %collective-permute-start.8 = (bf16[256,256]{1,0:T(8,128)(2,1)S(1)}, bf16[256,256]{1,0:T(8,128)(2,1)S(1)}, u32[]{:S(2)}, u32[]{:S(2)}) collective-permute-start(bf16[256,256]{1,0:T(8,128)(2,1)S(1)} %fusion.1), channel_id=1, source_target_pairs={{0,48},{1,17},{16,32},{17,1},{32,16},{33,49},{48,0},{49,33},{64,11... | collective-permute-start | bytes 393224 | tf_op jit(solution)/shard_map/ppermute | solution.py:344
  59.6 7.9 %collective-permute-start.11 = (bf16[2,128,512]{2,1,0:T(8,128)(2,1)S(1)}, bf16[2,128,512]{2,1,0:T(8,128)(2,1)S(1)}, u32[]{:S(2)}, u32[]{:S(2)}) collective-permute-start(bf16[2,128,512]{2,1,0:T(8,128)(2,1)S(1)} %slice.36), channel_id=1, source_target_pairs={{0,192},{1,65},{16,208},{17,81},{32,224},{33,97},{48,240},{49,113}... | collective-permute-start | bytes 786440 | tf_op jit(solution)/shard_map/ppermute | solution.py:344
  62.4 5.1 %collective-permute-start.10 = (bf16[1,256,256]{2,1,0:T(8,128)(2,1)S(1)}, bf16[1,256,256]{2,1,0:T(8,128)(2,1)S(1)}, u32[]{:S(2)}, u32[]{:S(2)}) collective-permute-start(bf16[1,256,256]{2,1,0:T(8,128)(2,1)S(1)} %fusion.4), channel_id=1, source_target_pairs={{0,2},{1,13},{2,0},{3,15},{4,6},{5,9},{6,4},{7,11},{8,10},{9,5},{1... | collective-permute-start | bytes 393224 | tf_op jit(solution)/shard_map/ppermute | solution.py:344
  67.5 2.0 %copy-start.4 = (bf16[2,256,256]{2,1,0:T(8,128)(2,1)}, bf16[2,256,256]{2,1,0:T(8,128)(2,1)S(1)}, u32[]{:S(2)}) copy-start(bf16[2,256,256]{2,1,0:T(8,128)(2,1)S(1)} %pad_maximum_fusion.1) | copy-start | bytes 786436
  67.5 11.4 %collective-permute-start.15 = (bf16[8,2,512,128]{3,2,1,0:T(8,128)(2,1)S(1)}, bf16[8,2,512,128]{3,2,1,0:T(8,128)(2,1)}, u32[]{:S(2)}, u32[]{:S(2)}) collective-permute-start(bf16[8,2,512,128]{3,2,1,0:T(8,128)(2,1)S(1)} %all-to-all-done.mine_ref), channel_id=1, source_target_pairs={{0,1},{1,0},{2,3},{3,2},{4,5},{5,4},{6,7},{7,6},{8,9},{9,8},{10,11... | collective-permute-start | bytes 6291464 | tf_op jit(solution)/shard_map/ppermute | solution.py:339
  67.6 6.5 %collective-permute-start.12 = (bf16[2,256,256]{2,1,0:T(8,128)(2,1)S(1)}, bf16[2,256,256]{2,1,0:T(8,128)(2,1)S(1)}, u32[]{:S(2)}, u32[]{:S(2)}) collective-permute-start(bf16[2,256,256]{2,1,0:T(8,128)(2,1)S(1)} %pad_maximum_fusion.1), channel_id=1, source_target_pairs={{0,4},{1,3},{2,6},{3,1},{4,0},{5,7},{6,2},{7,5},{8,12},{9,11},{10,... | collective-permute-start | bytes 786440 | tf_op jit(solution)/shard_map/ppermute | solution.py:344
  69.4 5.7 %collective-permute-start.13 = (bf16[128,512]{1,0:T(8,128)(2,1)S(1)}, bf16[128,512]{1,0:T(8,128)(2,1)S(1)}, u32[]{:S(2)}, u32[]{:S(2)}) collective-permute-start(bf16[128,512]{1,0:T(8,128)(2,1)S(1)} %get-tuple-element.87), channel_id=1, source_target_pairs={{0,64},{1,193},{16,80},{17,209},{32,96},{33,225},{48,112},{49,241}... | collective-permute-start | bytes 393224 | tf_op jit(solution)/shard_map/ppermute | solution.py:344
  75.1 10.5 %collective-permute-start.14 = (bf16[4,256,256]{2,1,0:T(8,128)(2,1)S(1)}, bf16[4,256,256]{2,1,0:T(8,128)(2,1)S(1)}, u32[]{:S(2)}, u32[]{:S(2)}) collective-permute-start(bf16[4,256,256]{2,1,0:T(8,128)(2,1)S(1)} %pad_maximum_fusion.g_ref), channel_id=1, source_target_pairs={{0,12},{1,5},{2,14},{3,7},{4,8},{5,1},{6,10},{7,3},{8,4},{9,13},{1... | collective-permute-start | bytes 1572872 | tf_op jit(solution)/shard_map/ppermute | solution.py:344
